TPU v7x, 256 devices: a whole 4x4x8 slice. The times are simulated.
256 devices in a mesh: row: 16 (over x, z_hi), col: 16 (over z_lo, y, core).
Axes of the slice: x: 4, y: 4, z: 8 (z_hi: 4, z_lo: 2; z = z_hi * 2 + z_lo), core: 2. Of those that a mesh axis runs over, the one named last changes fastest.
Arguments:
- src_embed: bfloat16 [64, 32768], P(None, ('row', 'col')), may hold values from -6.5 to 6.5, as said below
- tgt_embed: bfloat16 [64, 32768], P(None, ('row', 'col')), may hold values from -6.5 to 6.5, as said below
- src_weight: bfloat16 [32768], P(('row', 'col')), may hold values from 0.5 to 2
- tgt_weight: bfloat16 [32768], P(('row', 'col')), may hold values from 0.5 to 2
Outputs:
- src_potential: float32 [32768], P(('row', 'col'))
- tgt_potential: float32 [32768], P(('row', 'col'))
- marginal_error: float32 [], replicated
Inputs may be any that keep to these rules, and one draw needn't show every extreme that they name: `src_embed`: entries are real-valued embedding coordinates. `tgt_embed`: entries are real-valued embedding coordinates.
All inputs are finite; a program needn't handle non-finite values.
Results may differ from a plain program's by a relative error of at most 0.0003.
Values may be sent and summed in bfloat16 or wider, within the bound.
No kernel may reach another device: no remote copies, remote signals or barrier semaphores. Data moves between devices by JAX's collectives and lax.ppermute only.
A program may use at most 64 MiB of HBM per device.

v0:
```python
import math

import jax
import jax.numpy as jnp
from jax import lax
from jax.sharding import PartitionSpec as P

ITERS = 3


EPS = 0.02


def local_partial(a_embed, a_norm, a_weight, b_embed, b_norm, b_weight, b_pot):
    rows = a_embed.shape[1]
    block = min(512, rows)
    count = rows // block
    depth = a_embed.shape[0]

    def one(index):
        start = index * block
        embed = lax.dynamic_slice_in_dim(a_embed, start, block, 1)
        norm = lax.dynamic_slice_in_dim(a_norm, start, block, 0)
        weight = lax.dynamic_slice_in_dim(a_weight, start, block, 0)
        inner = lax.dot_general(
            embed, b_embed, (((0,), (0,)), ((), ())), preferred_element_type=jnp.float32
        )
        cost = (
            weight[:, None]
            * b_weight[None, :]
            * (norm[:, None] + b_norm[None, :] - 2.0 * inner)
            / depth
        )
        score = (b_pot[None, :] - cost) / EPS
        top = jnp.max(score, axis=1)
        return (top, jnp.sum(jnp.exp(score - top[:, None]), axis=1))

    tops, masses = lax.map(one, jnp.arange(count, dtype=jnp.int32))
    return (tops.reshape(rows), masses.reshape(rows))


def reduce_sources(partial_top, partial_mass):
    top = lax.pmax(partial_top, "col")
    mass = lax.psum(partial_mass * jnp.exp(partial_top - top), "col")
    return top + jnp.log(mass)


def reduce_targets(partial_top, partial_mass):
    top = lax.pmax(partial_top, "row")
    mass = lax.psum(partial_mass * jnp.exp(partial_top - top), "row")
    return top + jnp.log(mass)


def on_device(src_embed, tgt_embed, src_weight, tgt_weight):
    per_dev = src_embed.shape[1]
    total = per_dev * lax.axis_size("row") * lax.axis_size("col")
    shift = EPS * math.log(total)
    src_block, src_w = (
        lax.all_gather(src_embed, "col", axis=1, tiled=True),
        lax.all_gather(src_weight, "col", axis=0, tiled=True),
    )
    tgt_block, tgt_w = (
        lax.all_gather(tgt_embed, "row", axis=1, tiled=True),
        lax.all_gather(tgt_weight, "row", axis=0, tiled=True),
    )
    src_norm = jnp.sum(src_block.astype(jnp.float32) ** 2, axis=0)
    tgt_norm = jnp.sum(tgt_block.astype(jnp.float32) ** 2, axis=0)
    src_w32 = src_w.astype(jnp.float32)
    tgt_w32 = tgt_w.astype(jnp.float32)

    def source_update(tgt_pot):
        top, mass = local_partial(
            src_block, src_norm, src_w32, tgt_block, tgt_norm, tgt_w32, tgt_pot
        )
        return -EPS * reduce_sources(top, mass) - shift

    tgt_pot = jnp.zeros((tgt_block.shape[1],), jnp.float32)
    src_pot = jnp.zeros((src_block.shape[1],), jnp.float32)
    for step in range(ITERS):
        src_pot = source_update(tgt_pot)
        target_top, target_mass = local_partial(
            tgt_block, tgt_norm, tgt_w32, src_block, src_norm, src_w32, src_pot
        )
        tgt_pot = -EPS * reduce_targets(target_top, target_mass) - shift
    check = source_update(tgt_pot)
    diff = (src_pot - check) / EPS
    own_src = lax.dynamic_slice_in_dim(src_pot, lax.axis_index("col") * per_dev, per_dev, 0)
    own_tgt = lax.dynamic_slice_in_dim(tgt_pot, lax.axis_index("row") * per_dev, per_dev, 0)
    own_diff = lax.dynamic_slice_in_dim(diff, lax.axis_index("col") * per_dev, per_dev, 0)
    squares = lax.psum(jnp.sum(own_diff * own_diff), ("row", "col"))
    error = jnp.sqrt(squares / total)
    return (own_src, own_tgt, error)


def solution(mesh):
    return jax.shard_map(
        on_device,
        mesh=mesh,
        in_specs=(
            P(None, ("row", "col")),
            P(None, ("row", "col")),
            P(("row", "col")),
            P(("row", "col")),
        ),
        out_specs=(P(("row", "col")), P(("row", "col")), P()),
        check_vma=False,
    )
```

profile of v0, /device:TPU:1, one launch (start us, length us, event | category | flops | bytes accessed | tf_op | source)
XLA Modules:
  0.0 777.6 jit_solution(6892334257829738039)
XLA Ops:
  0.6 42.1 %all_gather.15 = bf16[64,2048]{1,0:T(8,128)(2,1)S(1)} all-gather(bf16[64,128]{1,0:T(8,128)(2,1)} %param.19), channel_id=1, replica_groups=mesh['row'=16,'col'=16] {'row'}, dimensions={1}, use_global_device_ids=true | all-gather | bytes 278528 | tf_op jit(solution)/shard_map/all_gather | solution.py:63
  42.8 27.9 %all_gather.14 = bf16[64,2048]{1,0:T(8,128)(2,1)S(1)} all-gather(bf16[64,128]{1,0:T(8,128)(2,1)} %param.18), channel_id=1, replica_groups=mesh['row'=16,'col'=16] {'col'}, dimensions={1}, use_global_device_ids=true | all-gather | bytes 278528 | tf_op jit(solution)/shard_map/all_gather | solution.py:59
  70.7 16.3 %all-gather = bf16[16,1,128]{2,1,0:T(2,128)(2,1)S(1)} all-gather(bf16[1,1,128]{2,1,0:T(2,128)(2,1)} %bitcast.167), channel_id=1, replica_groups=mesh['row'=16,'col'=16] {'col'}, dimensions={0}, use_global_device_ids=true | all-gather | bytes 4352 | tf_op jit(solution)/shard_map/all_gather | solution.py:60
  87.0 31.0 %all-gather.1 = bf16[16,1,128]{2,1,0:T(2,128)(2,1)S(1)} all-gather(bf16[1,1,128]{2,1,0:T(2,128)(2,1)} %bitcast.168), channel_id=1, replica_groups=mesh['row'=16,'col'=16] {'row'}, dimensions={0}, use_global_device_ids=true | all-gather | bytes 4352 | tf_op jit(solution)/shard_map/all_gather | solution.py:64
  133.4 34.1 %pmax.49 = f32[2048]{0:T(1024)S(1)} all-reduce(f32[2048]{0:T(1024)S(1)} %bitcast.132), channel_id=1, replica_groups=mesh['row'=16,'col'=16] {'col'}, use_global_device_ids=true, to_apply=%region_6.7 | all-reduce | flops 2048 | bytes 16384 | tf_op jit(solution)/shard_map/pmax | solution.py:43
  167.6 27.6 %psum.56 = f32[2048]{0:T(1024)S(1)} all-reduce(f32[2048]{0:T(1024)S(1)} %exponential_multiply_fusion.6), channel_id=1, replica_groups=mesh['row'=16,'col'=16] {'col'}, use_global_device_ids=true, to_apply=%region_7.8 | all-reduce | flops 2048 | bytes 16384 | tf_op jit(solution)/shard_map/psum | solution.py:44
  195.3 15.4 %while.85 = (s32[]{:T(128)}, f32[4,512]{1,0:T(4,128)S(1)}, f32[4,512]{1,0:T(4,128)S(1)}, f32[2048]{0:T(1024)S(1)}, s32[4]{0:T(128)S(1)}, /*index=5*/f32[2048]{0:...) while((s32[]{:T(128)}, f32[4,512]{1,0:T(4,128)S(1)}, ...), condition=%wide.region_11.12_spmd, body=%wide.region_8.11_spmd.sunk | while | flops 145751040 | bytes 8767707 | solution.py:38
  210.7 35.1 %pmax.50 = f32[2048]{0:T(1024)S(1)} all-reduce(f32[2048]{0:T(1024)S(1)} %bitcast.134), channel_id=1, replica_groups=mesh['row'=16,'col'=16] {'row'}, use_global_device_ids=true, to_apply=%region_12.13 | all-reduce | flops 2048 | bytes 16384 | tf_op jit(solution)/shard_map/pmax | solution.py:49
  245.9 32.7 %psum.57 = f32[2048]{0:T(1024)S(1)} all-reduce(f32[2048]{0:T(1024)S(1)} %exponential_multiply_fusion.5), channel_id=1, replica_groups=mesh['row'=16,'col'=16] {'row'}, use_global_device_ids=true, to_apply=%region_13.14 | all-reduce | flops 2048 | bytes 16384 | tf_op jit(solution)/shard_map/psum | solution.py:50
  278.6 15.4 %while.86 = (s32[]{:T(128)}, f32[4,512]{1,0:T(4,128)S(1)}, f32[4,512]{1,0:T(4,128)S(1)}, f32[2048]{0:T(1024)S(1)}, s32[4]{0:T(128)S(1)}, /*index=5*/f32[2048]{0:...) while((s32[]{:T(128)}, f32[4,512]{1,0:T(4,128)S(1)}, ...), condition=%wide.region_17.18_spmd, body=%wide.region_14.17_spmd.sunk | while | flops 145751040 | bytes 8767707 | solution.py:38
  294.0 41.8 %pmax.51 = f32[2048]{0:T(1024)S(1)} all-reduce(f32[2048]{0:T(1024)S(1)} %bitcast.136), channel_id=1, replica_groups=mesh['row'=16,'col'=16] {'col'}, use_global_device_ids=true, to_apply=%region_18.19 | all-reduce | flops 2048 | bytes 16384 | tf_op jit(solution)/shard_map/pmax | solution.py:43
  335.9 27.6 %psum.58 = f32[2048]{0:T(1024)S(1)} all-reduce(f32[2048]{0:T(1024)S(1)} %exponential_multiply_fusion.4), channel_id=1, replica_groups=mesh['row'=16,'col'=16] {'col'}, use_global_device_ids=true, to_apply=%region_19.20 | all-reduce | flops 2048 | bytes 16384 | tf_op jit(solution)/shard_map/psum | solution.py:44
  363.6 15.4 %while.87 = (s32[]{:T(128)}, f32[4,512]{1,0:T(4,128)S(1)}, f32[4,512]{1,0:T(4,128)S(1)}, f32[2048]{0:T(1024)S(1)}, s32[4]{0:T(128)S(1)}, /*index=5*/f32[2048]{0:...) while((s32[]{:T(128)}, f32[4,512]{1,0:T(4,128)S(1)}, ...), condition=%wide.region_23.24_spmd, body=%wide.region_20.23_spmd.sunk | while | flops 145751040 | bytes 8767707 | solution.py:38
  379.0 35.1 %pmax.52 = f32[2048]{0:T(1024)S(1)} all-reduce(f32[2048]{0:T(1024)S(1)} %bitcast.138), channel_id=1, replica_groups=mesh['row'=16,'col'=16] {'row'}, use_global_device_ids=true, to_apply=%region_24.25 | all-reduce | flops 2048 | bytes 16384 | tf_op jit(solution)/shard_map/pmax | solution.py:49
  414.2 32.9 %psum.59 = f32[2048]{0:T(1024)S(1)} all-reduce(f32[2048]{0:T(1024)S(1)} %exponential_multiply_fusion.3), channel_id=1, replica_groups=mesh['row'=16,'col'=16] {'row'}, use_global_device_ids=true, to_apply=%region_25.26 | all-reduce | flops 2048 | bytes 16384 | tf_op jit(solution)/shard_map/psum | solution.py:50
  447.1 15.4 %while.88 = (s32[]{:T(128)}, f32[4,512]{1,0:T(4,128)S(1)}, f32[4,512]{1,0:T(4,128)S(1)}, f32[2048]{0:T(1024)S(1)}, s32[4]{0:T(128)S(1)}, /*index=5*/f32[2048]{0:...) while((s32[]{:T(128)}, f32[4,512]{1,0:T(4,128)S(1)}, ...), condition=%wide.region_29.30_spmd, body=%wide.region_26.29_spmd.sunk | while | flops 145751040 | bytes 8767707 | solution.py:38
  462.5 41.9 %pmax.53 = f32[2048]{0:T(1024)S(1)} all-reduce(f32[2048]{0:T(1024)S(1)} %bitcast.140), channel_id=1, replica_groups=mesh['row'=16,'col'=16] {'col'}, use_global_device_ids=true, to_apply=%region_30.31 | all-reduce | flops 2048 | bytes 16384 | tf_op jit(solution)/shard_map/pmax | solution.py:43
  504.4 27.6 %psum.60 = f32[2048]{0:T(1024)S(1)} all-reduce(f32[2048]{0:T(1024)S(1)} %exponential_multiply_fusion.2), channel_id=1, replica_groups=mesh['row'=16,'col'=16] {'col'}, use_global_device_ids=true, to_apply=%region_31.32 | all-reduce | flops 2048 | bytes 16384 | tf_op jit(solution)/shard_map/psum | solution.py:44
  547.5 35.1 %pmax.54 = f32[2048]{0:T(1024)S(1)} all-reduce(f32[2048]{0:T(1024)S(1)} %bitcast.142), channel_id=1, replica_groups=mesh['row'=16,'col'=16] {'row'}, use_global_device_ids=true, to_apply=%region_36.37 | all-reduce | flops 2048 | bytes 16384 | tf_op jit(solution)/shard_map/pmax | solution.py:49
  582.7 32.7 %psum.61 = f32[2048]{0:T(1024)S(1)} all-reduce(f32[2048]{0:T(1024)S(1)} %exponential_multiply_fusion.1), channel_id=1, replica_groups=mesh['row'=16,'col'=16] {'row'}, use_global_device_ids=true, to_apply=%region_37.38 | all-reduce | flops 2048 | bytes 16384 | tf_op jit(solution)/shard_map/psum | solution.py:50
  615.5 15.4 %while.90 = (s32[]{:T(128)}, f32[4,512]{1,0:T(4,128)S(1)}, f32[4,512]{1,0:T(4,128)S(1)}, f32[2048]{0:T(1024)S(1)}, s32[4]{0:T(128)S(1)}, /*index=5*/f32[2048]{0:...) while((s32[]{:T(128)}, f32[4,512]{1,0:T(4,128)S(1)}, ...), condition=%wide.region_41.42_spmd, body=%wide.region_38.41_spmd.sunk | while | flops 145751040 | bytes 8767707 | solution.py:38
  630.9 41.8 %pmax.55 = f32[2048]{0:T(1024)S(1)} all-reduce(f32[2048]{0:T(1024)S(1)} %bitcast.144), channel_id=1, replica_groups=mesh['row'=16,'col'=16] {'col'}, use_global_device_ids=true, to_apply=%region_42.43 | all-reduce | flops 2048 | bytes 16384 | tf_op jit(solution)/shard_map/pmax | solution.py:43
  672.8 27.6 %psum.62 = f32[2048]{0:T(1024)S(1)} all-reduce(f32[2048]{0:T(1024)S(1)} %exponential_multiply_fusion), channel_id=1, replica_groups=mesh['row'=16,'col'=16] {'col'}, use_global_device_ids=true, to_apply=%region_43.44 | all-reduce | flops 2048 | bytes 16384 | tf_op jit(solution)/shard_map/psum | solution.py:44
  701.6 73.5 %psum.63 = f32[]{:T(128)} all-reduce(f32[]{:T(128)} %get-tuple-element.570), channel_id=1, replica_groups=mesh['row'=16,'col'=16] {'row','col'}, use_global_device_ids=true, to_apply=%region_45.46 | all-reduce | flops 1 | bytes 8 | tf_op jit(solution)/shard_map/psum | solution.py:90
  (252 shorter events, 121.5 us)
where the time goes:
time: 778 us
  blocking collectives  665 us (85%)
  matrix products  45.3 us (6%)
  local copies, waits for them, and re-layouts  24.1 us (3%)
  other arithmetic  21.4 us (3%)
  loops' own time  19 us (2%)
    pmax x4, blocking collectives, reduce_sources(): top = lax.pmax(partial_top, 'col')  160 us
    psum x4, blocking collectives, reduce_sources(): mass = lax.psum(partial_mass * jnp.exp(partial_top - top), 'col')  111 us
    pmax x3, blocking collectives, reduce_targets(): top = lax.pmax(partial_top, 'row')  105 us
    psum x3, blocking collectives, reduce_targets(): mass = lax.psum(partial_mass * jnp.exp(partial_top - top), 'row')  98.4 us
    psum x1, blocking collectives, on_device(): squares = lax.psum(jnp.sum(own_diff * own_diff), ('row', 'col'))  73.5 us
    dot_general x28, matrix products, one(): lax.dot_general(embed, b_embed, (((0,), (0,)), ((), ())), preferred_eleme...  45.3 us
    all_gather x1, blocking collectives, on_device(): lax.all_gather(tgt_embed, 'row', axis=1, tiled=True)  42.1 us
    all_gather x1, blocking collectives, on_device(): lax.all_gather(tgt_weight, 'row', axis=0, tiled=True)  31 us

commit v1 on v0

v1 whole, which is shorter than its diff:
```python
import functools
import math

import jax
import jax.numpy as jnp
from jax import lax
from jax.experimental import pallas as pl
from jax.experimental.pallas import tpu as pltpu
from jax.sharding import Mesh, PartitionSpec as P

EPS = 0.02
ITERS = 3
LANES = 128
TAIL = 16
PACK = 16
UNIT = 1.0 / (EPS * math.log(2.0))
AXES = ("x", "zh", "zl", "y", "c")
SRC_GROUP = ("x", "y")
TGT_GROUP = ("zh", "zl", "c")

f32 = jnp.float32
bf16 = jnp.bfloat16


def log2(value):
    return jnp.log(value) * (1.0 / math.log(2.0))


def pieces(value):
    high = value.astype(bf16).astype(f32)
    rest = value - high
    middle = rest.astype(bf16).astype(f32)
    low = (rest - middle).astype(bf16).astype(f32)
    return high, middle, low


def stack(rows, width):
    index = lax.broadcasted_iota(jnp.int32, (TAIL, width), 0)
    out = jnp.zeros((TAIL, width), f32)
    for place, row in rows:
        out = jnp.where(index == place, row, out)
    return out


def prepare(cells_ref, wide_ref, tail_ref, raw_ref, scale_ref):
    depth = raw_ref.shape[0]
    for b in range(cells_ref.shape[0]):
        at = pl.ds(b * LANES, LANES)
        embed = cells_ref[b, :depth, :]
        raw_ref[:, at] = embed
        value = embed.astype(f32)
        weight = cells_ref[b, depth : depth + PACK, :].astype(f32)[0:1]
        norm = jnp.sum(value * value, axis=0, keepdims=True)
        scale_ref[b : b + 1, :] = weight * (UNIT / depth)
        scaled = (2.0 * weight) * value
        high = scaled.astype(bf16).astype(f32)
        low = scaled - high
        one = jnp.ones_like(weight)
        n = pieces(norm)
        wn = pieces(weight * norm)
        tail_ref[:, at] = stack([(0, one), (1, one), (2, one), (3, n[0]), (4, n[1]), (5, n[2])], LANES)
        tail = stack(
            [(0, -wn[0]), (1, -wn[1]), (2, -wn[2])]
            + [(3, -weight), (4, -weight), (5, -weight), (6, one), (7, one), (8, one)],
            LANES,
        )
        wide_ref[at, :] = jnp.concatenate([high, low, tail], axis=0).T.astype(bf16)


def block_pass(wide_ref, raw_ref, tail_ref, scale_ref, summed, kept, rows_ref, part_ref, with_top):
    size = raw_ref.shape[1]
    width = 2 * LANES
    if summed is not None:
        column = summed.T
        for b in range(wide_ref.shape[0] // LANES):
            rows_ref[pl.ds(b * LANES, LANES), :] = jnp.broadcast_to(column[:, b : b + 1], (LANES, LANES))
    if kept is not None:
        ratio = pieces(kept / scale_ref[...])
    for s in range(size // width):
        at = pl.ds(s * width, width)

        def row(array):
            return jnp.concatenate([array[2 * s : 2 * s + 1, :], array[2 * s + 1 : 2 * s + 2, :]], axis=1)

        tail = tail_ref[:, at]
        if kept is not None:
            tail = tail + stack([(6, row(ratio[0])), (7, row(ratio[1])), (8, row(ratio[2]))], width)
        raw = raw_ref[:, at]
        operand = jnp.concatenate([raw, raw, tail.astype(bf16)], axis=0)
        score = jnp.dot(wide_ref[...], operand, preferred_element_type=f32)
        score = score * row(scale_ref)
        if summed is not None:
            score = score + jnp.concatenate([rows_ref[...], rows_ref[...]], axis=1)
        if with_top:
            top = jnp.max(score, axis=0, keepdims=True)
            score = score - top
            part_ref[1, 2 * s : 2 * s + 1, :] = top[:, :LANES]
            part_ref[1, 2 * s + 1 : 2 * s + 2, :] = top[:, LANES:]
        mass = jnp.sum(jnp.exp2(score), axis=0, keepdims=True)
        part_ref[0, 2 * s : 2 * s + 1, :] = mass[:, :LANES]
        part_ref[0, 2 * s + 1 : 2 * s + 2, :] = mass[:, LANES:]


def combine_tops(got_ref, shift):
    top = jnp.max(got_ref[:, 1], axis=0)
    mass = jnp.sum(got_ref[:, 0] * jnp.exp2(got_ref[:, 1] - top[None]), axis=0)
    return -(top + log2(mass)) - shift


def combine(got_ref, old, shift):
    return old - log2(jnp.sum(got_ref[:, 0], axis=0)) - shift


def send(part_ref, out_ref):
    out_ref[...] = jnp.broadcast_to(part_ref[...][None], out_ref.shape)


def first_kernel(src, tgt, s_wide, s_tail, s_raw, s_scale, t_wide, t_tail, t_raw, t_scale, out, part):
    prepare(src, s_wide, s_tail, s_raw, s_scale)
    prepare(tgt, t_wide, t_tail, t_raw, t_scale)
    block_pass(t_wide, s_raw, s_tail, s_scale, None, None, None, part, True)
    send(part, out)


def second_kernel(shift, got, wide, raw, tail, scale, new, out, rows, part):
    new[...] = combine_tops(got, shift)
    block_pass(wide, raw, tail, scale, new[...], None, rows, part, True)
    send(part, out)


def third_kernel(shift, got, kept, wide, raw, tail, scale, new, out, rows, part):
    new[...] = combine_tops(got, shift)
    block_pass(wide, raw, tail, scale, new[...], kept[...], rows, part, False)
    send(part, out)


def later_kernel(shift, got, old, kept, wide, raw, tail, scale, new, out, rows, part):
    new[...] = combine(got, old[...], shift)
    block_pass(wide, raw, tail, scale, new[...], kept[...], rows, part, False)
    send(part, out)


def last_kernel(shift, got, out):
    diff = (log2(jnp.sum(got[:, 0], axis=0)) + shift) * math.log(2.0)
    out[...] = jnp.full(out.shape, jnp.sum(diff * diff), f32)


def call(kernel, args, outs, scratch, name):
    return pl.pallas_call(
        kernel,
        out_shape=[jax.ShapeDtypeStruct(shape, dtype) for shape, dtype in outs],
        in_specs=[pl.BlockSpec(memory_space=pltpu.VMEM)] * len(args),
        out_specs=[pl.BlockSpec(memory_space=pltpu.VMEM)] * len(outs),
        scratch_shapes=scratch,
        compiler_params=pltpu.CompilerParams(vmem_limit_bytes=48 * 1024 * 1024),
        name=name,
    )(*args)


def gather(array, group):
    count = lax.axis_size(group)
    return lax.all_to_all(jnp.broadcast_to(array[None], (count,) + array.shape), group, 0, 0)


def on_device(src_embed, tgt_embed, src_weight, tgt_weight):
    depth, per_dev = src_embed.shape
    src_count, tgt_count = lax.axis_size(SRC_GROUP), lax.axis_size(TGT_GROUP)
    total = per_dev * src_count * tgt_count
    shift = math.log2(total)
    src_size, tgt_size = per_dev * src_count, per_dev * tgt_count
    src_rows, tgt_rows = (src_count, per_dev), (tgt_count, per_dev)

    def packed(embed, weight):
        return jnp.concatenate([embed, jnp.broadcast_to(weight[None], (PACK, per_dev))], axis=0)

    src = gather(packed(src_embed, src_weight), SRC_GROUP)
    tgt = gather(packed(tgt_embed, tgt_weight), TGT_GROUP)

    wide = 2 * depth + TAIL
    operands = []
    for size, rows in ((src_size, src_rows), (tgt_size, tgt_rows)):
        operands += [((size, wide), bf16), ((TAIL, size), f32), ((depth, size), bf16), (rows, f32)]

    def row_out(tops):
        return ((src_count, tops) + src_rows, f32), pltpu.VMEM((tops,) + src_rows, f32)

    def col_out(tops):
        return ((tgt_count, tops) + tgt_rows, f32), pltpu.VMEM((tops,) + tgt_rows, f32)

    out, part = row_out(2)
    s_wide, s_tail, s_raw, s_scale, t_wide, t_tail, t_raw, t_scale, sent = call(
        first_kernel, [src, tgt], operands + [out], [part], "row_pass_1"
    )
    got = gather_parts(sent, SRC_GROUP)
    src_spread = pltpu.VMEM((src_size, LANES), f32)
    tgt_spread = pltpu.VMEM((tgt_size, LANES), f32)
    keep_tgt = [t_raw, t_tail, t_scale]
    keep_src = [s_raw, s_tail, s_scale]

    out, part = col_out(2)
    f, sent = call(
        functools.partial(second_kernel, shift),
        [got, s_wide] + keep_tgt,
        [(src_rows, f32), out],
        [src_spread, part],
        "col_pass_1",
    )
    got = gather_parts(sent, TGT_GROUP)
    out, part = row_out(1)
    g, sent = call(
        functools.partial(third_kernel, shift),
        [got, f, t_wide] + keep_src,
        [(tgt_rows, f32), out],
        [tgt_spread, part],
        "row_pass_2",
    )
    for step in range(2, ITERS + 1):
        got = gather_parts(sent, SRC_GROUP)
        out, part = col_out(1)
        f, sent = call(
            functools.partial(later_kernel, shift),
            [got, f, g, s_wide] + keep_tgt,
            [(src_rows, f32), out],
            [src_spread, part],
            f"col_pass_{step}",
        )
        got = gather_parts(sent, TGT_GROUP)
        out, part = row_out(1)
        g, sent = call(
            functools.partial(later_kernel, shift),
            [got, g, f, t_wide] + keep_src,
            [(tgt_rows, f32), out],
            [tgt_spread, part],
            f"row_pass_{step + 1}",
        )
    got = gather_parts(sent, SRC_GROUP)
    (sent,) = call(
        functools.partial(last_kernel, shift), [got], [((tgt_count, 8, LANES), f32)], [], "mismatch"
    )
    squares = jnp.sum(gather_parts(sent, TGT_GROUP)[:, 0, 0])
    error = jnp.sqrt(squares / total)
    own_src = lax.dynamic_index_in_dim(f, lax.axis_index(SRC_GROUP), 0, False) * (1.0 / UNIT)
    own_tgt = lax.dynamic_index_in_dim(g, lax.axis_index(TGT_GROUP), 0, False) * (1.0 / UNIT)
    return own_src, own_tgt, error


def gather_parts(sent, group):
    return lax.all_to_all(sent, group, 0, 0)


def solution(mesh, shape=(4, 4, 2, 4, 2)):
    placed = Mesh(mesh.devices.reshape(shape), AXES)
    return jax.shard_map(
        on_device,
        mesh=placed,
        in_specs=(P(None, AXES), P(None, AXES), P(AXES), P(AXES)),
        out_specs=(P(AXES), P(AXES), P()),
        check_vma=False,
    )
```

time: 778 us -> 166 us (0.21)
  blocking collectives: 665 us -> 96.4 us
  matrix products: 45.3 us -> 0 us
  Pallas kernels: 0 us -> 25.1 us
  local copies, waits for them, and re-layouts: 24.1 us -> 1.48 us
  waiting for transfers between devices: 0 us -> 21.8 us
  other arithmetic: 21.4 us -> 2.37 us
  loops' own time: 19 us -> 0 us
  starting transfers between devices: 0 us -> 15.4 us
    psum x8 -> x0, blocking collectives: 282 us -> none  [the longest x4 111 us: reduce_sources(): mass = lax.psum(partial_mass * jnp.exp(partial_top - top), 'col')]
    pmax x7 -> x0, blocking collectives: 265 us -> none  [the longest x4 160 us: reduce_sources(): top = lax.pmax(partial_top, 'col')]
    all_gather x4 -> x0, blocking collectives: 117 us -> none  [the longest x1 42.1 us: on_device(): lax.all_gather(tgt_embed, 'row', axis=1, tiled=True)]
    all_to_all x0 -> x7, blocking collectives: none -> 96.4 us  [the longest x6 72.8 us: gather_parts(): return lax.all_to_all(sent, group, 0, 0)]
    dot_general x28 -> x0, matrix products: 45.3 us -> none  [one(): lax.dot_general(embed, b_embed, (((0,), (0,)), ((), ())), preferred_eleme...]
    pallas_call x0 -> x8, Pallas kernels: none -> 25.1 us  [call(): pl.pallas_call(kernel, out_shape=[jax.ShapeDtypeStruct(shape, dtype) for...]
    all_to_all x0 -> x3, waiting for transfers between devices: none -> 21.8 us  [the longest x2 14 us: gather_parts(): return lax.all_to_all(sent, group, 0, 0)]
    dynamic_slice x85 -> x0, local copies, waits for them, and re-layouts: 21.3 us -> none  [the longest x28 16.4 us: local_partial(): tops, masses = lax.map(one, jnp.arange(count, dtype=jnp.int32))]
  transfers between devices with their start and end apart: 0 -> 3, of which waited for: 0 -> 3; matrix products, arithmetic and copies ran while one was open for 0% -> 1% of each run, Pallas kernels for 0% -> 0%
where the time goes in v1:
time: 166 us; the launch traced here: 165 us
  blocking collectives  96.4 us (58%)
  Pallas kernels  25.1 us (15%)
  waiting for transfers between devices  21.8 us (13%)
  starting transfers between devices  15.4 us (9%)
  between operations  2.54 us (2%)
  other arithmetic  2.37 us (1%)
    all_to_all x6, blocking collectives, gather_parts(): return lax.all_to_all(sent, group, 0, 0)  72.8 us
    pallas_call x8, Pallas kernels, call(): pl.pallas_call(kernel, out_shape=[jax.ShapeDtypeStruct(shape, dtype) for...  25.1 us
    all_to_all x1, blocking collectives, gather(): lax.all_to_all(jnp.broadcast_to(array[None], (count,) + array.shape), gro...  23.6 us
    all_to_all x2, waiting for transfers between devices, gather_parts(): return lax.all_to_all(sent, group, 0, 0)  14 us
    all_to_all x1, waiting for transfers between devices, gather(): lax.all_to_all(jnp.broadcast_to(array[None], (count,) + array.shape), gro...  7.78 us
    all_to_all x1, starting transfers between devices, gather(): lax.all_to_all(jnp.broadcast_to(array[None], (count,) + array.shape), gro...  7.72 us
    all_to_all x2, starting transfers between devices, gather_parts(): return lax.all_to_all(sent, group, 0, 0)  7.64 us
  transfers between devices with their start and end apart: 3, of which 3 were waited for; matrix products, arithmetic and copies ran while one was open for 1% of the time, Pallas kernels for 0%

profile of v1, /device:TPU:1, one launch (start us, length us, event | category | flops | bytes accessed | tf_op | source)
XLA Modules:
  0.0 165.0 jit_solution(2367520073316418494)
XLA Ops:
  0.6 0.7 broadcast_in_dim.8
  1.3 0.7 pad_maximum_fusion
  2.0 0.8 broadcast_in_dim.9
  2.8 7.7 %all-to-all-start = ((bf16[16,80,128]{2,1,0:T(8,128)(2,1)}), bf16[16,80,128]{2,1,0:T(8,128)(2,1)S(1)}, u32[]{:S(2)}, u32[]{:S(2)}) async-start(bf16[16,80,128]{2,1,0:T(8,128)(2,1)} %broadcast_in_dim.9), calls=%async_computation | async-start | bytes 655360 | tf_op jit(solution)/shard_map/all_to_all | solution.py:162
  10.5 7.8 %all-to-all-done.src = bf16[16,80,128]{2,1,0:T(8,128)(2,1)S(1)} async-done(((bf16[16,80,128]{2,1,0:T(8,128)(2,1)}), bf16[16,80,128]{2,1,0:T(8,128)(2,1)S(1)}, u32[]{:S(2)}, u32[]{:S(2)}) %all-to-all-start) | async-done | bytes 327712 | tf_op jit(solution)/shard_map/all_to_all | solution.py:162
  18.4 23.6 %all_to_all.50.tgt = bf16[16,80,128]{2,1,0:T(8,128)(2,1)S(1)} all-to-all(bf16[16,80,128]{2,1,0:T(8,128)(2,1)S(1)} %broadcast_in_dim.11), channel_id=1, replica_groups=mesh['x'=4,'zh'=4,'zl'=2,'y'=4,'c'=2] {'zh','zl','c'}, dimensions={0} | all-to-all | bytes 655360 | tf_op jit(solution)/shard_map/all_to_all | solution.py:162
  42.0 5.3 %row_pass_1.1 = (bf16[2048,144]{1,0:T(8,128)(2,1)S(1)}, f32[16,2048]{1,0:T(8,128)S(1)}, bf16[64,2048]{1,0:T(8,128)(2,1)S(1)}, f32[16,128]{1,0:T(8,128)S(1)}, bf1...) custom-call(bf16[16,80,128]{2,1,0:T(8,128)(2,1)S(1)} %all-to-all-don, ...), custom_call_target="tpu_custom_call" | custom-call | tf_op jit(solution)/shard_map/row_pass_1/pallas_call | solution.py:149
  47.3 11.6 %all_to_all.51.got = f32[16,2,16,128]{3,2,1,0:T(8,128)S(1)} all-to-all(f32[16,2,16,128]{3,2,1,0:T(8,128)S(1)} %get-tuple-element.24), channel_id=1, replica_groups=mesh['x'=4,'zh'=4,'zl'=2,'y'=4,'c'=2] {'x','y'}, dimensions={0} | all-to-all | bytes 524288 | tf_op jit(solution)/shard_map/all_to_all | solution.py:248
  58.9 4.8 %col_pass_1.1 = (f32[16,128]{1,0:T(8,128)S(1)}, f32[16,2,16,128]{3,2,1,0:T(8,128)S(1)}) custom-call(f32[16,2,16,128]{3,2,1,0:T(8,128)S(1)} %all_to_all.51.got, bf16[2048,144]{1,0:T(8,128)(2,1)S(1)} %get-tuple-element.25.wide, bf16[64,2048]{1,0:T(8,128)(2,1)S(1)} %get-tuple-element.26.raw, f32[16,2048]{1,0:T(8,128)S(1)} %get-tuple-element.27.tail, ...), custom_call_target="tpu_custom_call" | custom-call | tf_op jit(solution)/shard_map/col_pass_1/pallas_call | solution.py:149
  63.7 15.4 %all_to_all.52.got = f32[16,2,16,128]{3,2,1,0:T(8,128)S(1)} all-to-all(f32[16,2,16,128]{3,2,1,0:T(8,128)S(1)} %get-tuple-element.29), channel_id=1, replica_groups=mesh['x'=4,'zh'=4,'zl'=2,'y'=4,'c'=2] {'zh','zl','c'}, dimensions={0} | all-to-all | bytes 524288 | tf_op jit(solution)/shard_map/all_to_all | solution.py:248
  79.2 2.8 %row_pass_2.1 = (f32[16,128]{1,0:T(8,128)S(1)}, f32[16,1,16,128]{3,2,1,0:T(8,128)S(1)}) custom-call(f32[16,2,16,128]{3,2,1,0:T(8,128)S(1)} %all_to_all.52.got, f32[16,128]{1,0:T(8,128)S(1)} %get-tuple-element.30.kept.old, bf16[2048,144]{1,0:T(8,128)(2,1)S(1)} %get-tuple-element.31.wide, bf16[64,2048]{1,0:T(8,128)(2,1)S(1)} %get-tuple-element.32.raw, ...), custom_call_target="tpu_custom_call" | custom-call | tf_op jit(solution)/shard_map/row_pass_2/pallas_call | solution.py:149
  82.0 10.2 %all_to_all.53.got = f32[16,1,16,128]{3,2,1,0:T(8,128)S(1)} all-to-all(f32[16,1,16,128]{3,2,1,0:T(8,128)S(1)} %get-tuple-element.35), channel_id=1, replica_groups=mesh['x'=4,'zh'=4,'zl'=2,'y'=4,'c'=2] {'x','y'}, dimensions={0} | all-to-all | bytes 262144 | tf_op jit(solution)/shard_map/all_to_all | solution.py:248
  92.2 2.6 %col_pass_2.1 = (f32[16,128]{1,0:T(8,128)S(1)}, f32[16,1,16,128]{3,2,1,0:T(8,128)S(1)}) custom-call(f32[16,1,16,128]{3,2,1,0:T(8,128)S(1)} %all_to_all.53.got, f32[16,128]{1,0:T(8,128)S(1)} %get-tuple-element.30.kept.old, f32[16,128]{1,0:T(8,128)S(1)} %get-tuple-element.36.kept.old, bf16[2048,144]{1,0:T(8,128)(2,1)S(1)} %get-tuple-element.25.wide, ...), custom_call_target="tpu_custom_call" | custom-call | tf_op jit(solution)/shard_map/col_pass_2/pallas_call | solution.py:149
  94.8 12.7 %all_to_all.54.got = f32[16,1,16,128]{3,2,1,0:T(8,128)S(1)} all-to-all(f32[16,1,16,128]{3,2,1,0:T(8,128)S(1)} %get-tuple-element.37), channel_id=1, replica_groups=mesh['x'=4,'zh'=4,'zl'=2,'y'=4,'c'=2] {'zh','zl','c'}, dimensions={0} | all-to-all | bytes 262144 | tf_op jit(solution)/shard_map/all_to_all | solution.py:248
  107.5 2.8 %row_pass_3.1 = (f32[16,128]{1,0:T(8,128)S(1)}, f32[16,1,16,128]{3,2,1,0:T(8,128)S(1)}) custom-call(f32[16,1,16,128]{3,2,1,0:T(8,128)S(1)} %all_to_all.54.got, f32[16,128]{1,0:T(8,128)S(1)} %get-tuple-element.36.kept.old, f32[16,128]{1,0:T(8,128)S(1)} %get-tuple-element.38.kept.old, bf16[2048,144]{1,0:T(8,128)(2,1)S(1)} %get-tuple-element.31.wide, ...), custom_call_target="tpu_custom_call" | custom-call | tf_op jit(solution)/shard_map/row_pass_3/pallas_call | solution.py:149
  110.3 10.3 %all_to_all.55.got = f32[16,1,16,128]{3,2,1,0:T(8,128)S(1)} all-to-all(f32[16,1,16,128]{3,2,1,0:T(8,128)S(1)} %get-tuple-element.39), channel_id=1, replica_groups=mesh['x'=4,'zh'=4,'zl'=2,'y'=4,'c'=2] {'x','y'}, dimensions={0} | all-to-all | bytes 262144 | tf_op jit(solution)/shard_map/all_to_all | solution.py:248
  120.5 2.6 %col_pass_3.1 = (f32[16,128]{1,0:T(8,128)S(1)}, f32[16,1,16,128]{3,2,1,0:T(8,128)S(1)}) custom-call(f32[16,1,16,128]{3,2,1,0:T(8,128)S(1)} %all_to_all.55.got, f32[16,128]{1,0:T(8,128)S(1)} %get-tuple-element.38.kept.old, f32[16,128]{1,0:T(8,128)S(1)} %get-tuple-element.40.kept.old, bf16[2048,144]{1,0:T(8,128)(2,1)S(1)} %get-tuple-element.25.wide, ...), custom_call_target="tpu_custom_call" | custom-call | tf_op jit(solution)/shard_map/col_pass_3/pallas_call | solution.py:149
  123.1 12.6 %all_to_all.56.got = f32[16,1,16,128]{3,2,1,0:T(8,128)S(1)} all-to-all(f32[16,1,16,128]{3,2,1,0:T(8,128)S(1)} %get-tuple-element.42), channel_id=1, replica_groups=mesh['x'=4,'zh'=4,'zl'=2,'y'=4,'c'=2] {'zh','zl','c'}, dimensions={0} | all-to-all | bytes 262144 | tf_op jit(solution)/shard_map/all_to_all | solution.py:248
  135.7 3.4 %row_pass_4.1 = (f32[16,128]{1,0:T(8,128)S(1)}, f32[16,1,16,128]{3,2,1,0:T(8,128)}) custom-call(f32[16,1,16,128]{3,2,1,0:T(8,128)S(1)} %all_to_all.56.got, f32[16,128]{1,0:T(8,128)S(1)} %get-tuple-element.40.kept.old, f32[16,128]{1,0:T(8,128)S(1)} %get-tuple-element.41.kept, bf16[2048,144]{1,0:T(8,128)(2,1)S(1)} %get-tuple-element.31.wide, ...), custom_call_target="tpu_custom_call" | custom-call | tf_op jit(solution)/shard_map/row_pass_4/pallas_call | solution.py:149
  139.1 3.5 %all-to-all-start.8 = ((f32[16,1,16,128]{3,2,1,0:T(8,128)}), f32[16,1,16,128]{3,2,1,0:T(8,128)S(1)}, u32[]{:S(2)}, u32[]{:S(2)}) async-start(f32[16,1,16,128]{3,2,1,0:T(8,128)} %get-tuple-element.44), calls=%async_computation.8 | async-start | bytes 262144 | tf_op jit(solution)/shard_map/all_to_all | solution.py:248
  142.7 7.2 %all-to-all-done.8.got = f32[16,1,16,128]{3,2,1,0:T(8,128)S(1)} async-done(((f32[16,1,16,128]{3,2,1,0:T(8,128)}), f32[16,1,16,128]{3,2,1,0:T(8,128)S(1)}, u32[]{:S(2)}, u32[]{:S(2)}) %all-to-all-start.8) | async-done | bytes 131104 | tf_op jit(solution)/shard_map/all_to_all | solution.py:248
  149.8 0.8 mismatch.1
  150.6 4.1 %all-to-all-start.9 = ((f32[16,8,128]{2,1,0:T(8,128)}), f32[16,8,128]{2,1,0:T(8,128)S(1)}, u32[]{:S(2)}, u32[]{:S(2)}) async-start(f32[16,8,128]{2,1,0:T(8,128)} %mismatch.1), calls=%async_computation.9 | async-start | bytes 131072 | tf_op jit(solution)/shard_map/all_to_all | solution.py:248
  155.8 6.8 %all-to-all-done.9 = f32[16,8,128]{2,1,0:T(8,128)S(1)} async-done(((f32[16,8,128]{2,1,0:T(8,128)}), f32[16,8,128]{2,1,0:T(8,128)S(1)}, u32[]{:S(2)}, u32[]{:S(2)}) %all-to-all-start.9) | async-done | bytes 65568 | tf_op jit(solution)/shard_map/all_to_all | solution.py:248
  (10 shorter events, 1.7 us)
Async XLA Ops:
  2.8 7.7 %copy-start.1 = (bf16[128]{0:T(256)(128)(2,1)S(1)}, bf16[128]{0:T(256)(128)(2,1)}, u32[]{:S(2)}) copy-start(bf16[128]{0:T(256)(128)(2,1)} %param.7) | copy-start | bytes 772
  2.8 7.7 %copy-start = (bf16[64,128]{1,0:T(8,128)(2,1)S(1)}, bf16[64,128]{1,0:T(8,128)(2,1)}, u32[]{:S(2)}) copy-start(bf16[64,128]{1,0:T(8,128)(2,1)} %param.5) | copy-start | bytes 49156
  2.8 15.5 %all-to-all-start = ((bf16[16,80,128]{2,1,0:T(8,128)(2,1)}), bf16[16,80,128]{2,1,0:T(8,128)(2,1)S(1)}, u32[]{:S(2)}, u32[]{:S(2)}) async-start(bf16[16,80,128]{2,1,0:T(8,128)(2,1)} %broadcast_in_dim.9), calls=%async_computation | async-start | bytes 655360 | tf_op jit(solution)/shard_map/all_to_all | solution.py:162
  139.1 10.7 %all-to-all-start.8 = ((f32[16,1,16,128]{3,2,1,0:T(8,128)}), f32[16,1,16,128]{3,2,1,0:T(8,128)S(1)}, u32[]{:S(2)}, u32[]{:S(2)}) async-start(f32[16,1,16,128]{3,2,1,0:T(8,128)} %get-tuple-element.44), calls=%async_computation.8 | async-start | bytes 262144 | tf_op jit(solution)/shard_map/all_to_all | solution.py:248
  150.6 12.0 %all-to-all-start.9 = ((f32[16,8,128]{2,1,0:T(8,128)}), f32[16,8,128]{2,1,0:T(8,128)S(1)}, u32[]{:S(2)}, u32[]{:S(2)}) async-start(f32[16,8,128]{2,1,0:T(8,128)} %mismatch.1), calls=%async_computation.9 | async-start | bytes 131072 | tf_op jit(solution)/shard_map/all_to_all | solution.py:248

commit v2 on v1

v2 whole, which is shorter than its diff:
```python
import functools
import math

import jax
import jax.numpy as jnp
from jax import lax
from jax.experimental import pallas as pl
from jax.experimental.pallas import tpu as pltpu
from jax.sharding import Mesh, PartitionSpec as P

EPS = 0.02
ITERS = 3
LANES = 128
TAIL = 16
PACK = 16
WIDTH = 2 * LANES
HEAD = 512
MARGIN = 80.0
LARGE = 2.0**120
UNIT = 1.0 / (EPS * math.log(2.0))
AXES = ("x", "zh", "zl", "y", "c")
SRC_GROUP = ("x", "y")
TGT_GROUP = ("zh", "zl", "c")

f32 = jnp.float32
bf16 = jnp.bfloat16


def log2(value):
    return jnp.log(value) * (1.0 / math.log(2.0))


def pieces(value):
    high = value.astype(bf16).astype(f32)
    rest = value - high
    middle = rest.astype(bf16).astype(f32)
    low = (rest - middle).astype(bf16).astype(f32)
    return high, middle, low


def stack(rows, width):
    index = lax.broadcasted_iota(jnp.int32, (TAIL, width), 0)
    out = jnp.zeros((TAIL, width), f32)
    for place, row in rows:
        out = jnp.where(index == place, row, out)
    return out


def prepare(blocks, wide_ref, tail_ref, raw_ref, scale_ref):
    depth = raw_ref.shape[0]
    for cells, place in blocks:
        at = pl.ds(pl.multiple_of(place * LANES, LANES), LANES)
        embed = cells[:depth, :]
        raw_ref[:, at] = embed
        value = embed.astype(f32)
        weight = cells[depth : depth + PACK, :].astype(f32)[0:1]
        norm = jnp.sum(value * value, axis=0, keepdims=True)
        scale_ref[pl.ds(place, 1), :] = weight * (UNIT / depth)
        scaled = (2.0 * weight) * value
        high = scaled.astype(bf16).astype(f32)
        low = scaled - high
        one = jnp.ones_like(weight)
        n = pieces(norm)
        wn = pieces(weight * norm)
        tail_ref[:, at] = stack([(0, one), (1, one), (2, one), (3, n[0]), (4, n[1]), (5, n[2])], LANES)
        tail = stack(
            [(0, -wn[0]), (1, -wn[1]), (2, -wn[2])]
            + [(3, -weight), (4, -weight), (5, -weight), (6, one), (7, one), (8, one)],
            LANES,
        )
        wide_ref[at, :] = jnp.concatenate([high, low, tail], axis=0).T.astype(bf16)


def spread(summed, rows_ref):
    column = summed.T
    for b in range(rows_ref.shape[0] // LANES):
        rows_ref[pl.ds(b * LANES, LANES), :] = jnp.broadcast_to(column[:, b : b + 1], (LANES, LANES))


def strip_score(s, wide_ref, raw_ref, tail_ref, scale_ref, ratio, rows_ref):
    at = pl.ds(s * WIDTH, WIDTH) if isinstance(s, int) else pl.ds(pl.multiple_of(s * WIDTH, WIDTH), WIDTH)

    def row(array):
        return jnp.concatenate([array[pl.ds(2 * s, 1), :], array[pl.ds(2 * s + 1, 1), :]], axis=1)

    tail = tail_ref[:, at]
    if ratio is not None:
        parts = [jnp.concatenate([p[2 * s : 2 * s + 1], p[2 * s + 1 : 2 * s + 2]], axis=1) for p in ratio]
        tail = tail + stack([(6, parts[0]), (7, parts[1]), (8, parts[2])], WIDTH)
    raw = raw_ref[:, at]
    operand = jnp.concatenate([raw, raw, tail.astype(bf16)], axis=0)
    score = jnp.dot(wide_ref[...], operand, preferred_element_type=f32) * row(scale_ref)
    if rows_ref is not None:
        score = score + jnp.concatenate([rows_ref[...], rows_ref[...]], axis=1)
    return score


def put(ref, s, value):
    ref[pl.ds(2 * s, 1), :] = value[:, :LANES]
    ref[pl.ds(2 * s + 1, 1), :] = value[:, LANES:]


def sum_pass(operands, rows_ref, kept, part_ref):
    ratio = pieces(kept / operands[3][...])
    for s in range(part_ref.shape[0] // 2):
        score = strip_score(s, *operands, ratio, rows_ref)
        put(part_ref, s, jnp.sum(jnp.exp2(score), axis=0, keepdims=True))


def log_pass(operands, rows_ref, part_ref, top_ref):
    count = part_ref.shape[0] // 2
    for s in range(count):
        score = strip_score(s, *operands, None, rows_ref)
        top = jnp.max(score[: min(HEAD, score.shape[0])], axis=0, keepdims=True) + MARGIN
        put(top_ref, s, top)
        put(part_ref, s, jnp.sum(jnp.exp2(score - top), axis=0, keepdims=True))

    @pl.when(jnp.logical_not(jnp.max(part_ref[...]) < LARGE))
    def _():
        def again(s, carry):
            score = strip_score(s, *operands, None, rows_ref)
            top = jnp.max(score, axis=0, keepdims=True)
            put(top_ref, s, top)
            put(part_ref, s, jnp.sum(jnp.exp2(score - top), axis=0, keepdims=True))
            return carry

        lax.fori_loop(0, count, again, 0)


def combine_logs(got_ref, shift):
    got = got_ref[...]
    top = jnp.max(got, axis=0)
    return -(top + log2(jnp.sum(jnp.exp2(got - top[None]), axis=0))) - shift


def combine(got_ref, old, shift):
    return old - log2(jnp.sum(got_ref[...], axis=0)) - shift


def send(part, out_ref):
    out_ref[...] = jnp.broadcast_to(part[None], out_ref.shape)


def pack_kernel(src_embed, tgt_embed, src_weight, tgt_weight, src_out, tgt_out, embeds, weights, sems):
    copies = [
        pltpu.make_async_copy(source, target, sems.at[k])
        for k, (source, target) in enumerate(
            [
                (src_embed, embeds.at[0]),
                (tgt_embed, embeds.at[1]),
                (src_weight, weights.at[0]),
                (tgt_weight, weights.at[1]),
            ]
        )
    ]
    for copy in copies:
        copy.start()
    for copy in copies:
        copy.wait()
    for k, out in enumerate((src_out, tgt_out)):
        row = jnp.broadcast_to(weights[k].astype(f32), (PACK, LANES)).astype(bf16)
        send(jnp.concatenate([embeds[k], row], axis=0), out)


def sources_kernel(own, far, wide, tail, raw, scale):
    x, y = lax.axis_index("x"), lax.axis_index("y")
    blocks = []
    for m in range(4):
        for k in range(4):
            ref = (own.at[k] if m == 0 else far.at[m - 1, k])
            blocks.append((ref, (x ^ k) * 4 + (y ^ m)))
    prepare(blocks, wide, tail, raw, scale)


def first_kernel(own, other, s_tail, s_raw, s_scale, t_wide, t_tail, t_raw, t_scale, out, part, top):
    core = lax.axis_index("c")
    blocks = [(own.at[z], 2 * z + core) for z in range(own.shape[0])]
    blocks += [(other.at[z], 2 * z + 1 - core) for z in range(own.shape[0])]
    prepare(blocks, t_wide, t_tail, t_raw, t_scale)
    log_pass((t_wide, s_raw, s_tail, s_scale), None, part, top)
    send(top[...] + log2(part[...]), out)


def second_kernel(shift, got, wide, raw, tail, scale, new, out, rows, part, top):
    new[...] = combine_logs(got, shift)
    spread(new[...], rows)
    log_pass((wide, raw, tail, scale), rows, part, top)
    send(top[...] + log2(part[...]), out)


def third_kernel(shift, got, kept, wide, raw, tail, scale, new, out, rows, part):
    new[...] = combine_logs(got, shift)
    spread(new[...], rows)
    sum_pass((wide, raw, tail, scale), rows, kept[...], part)
    send(part[...], out)


def later_kernel(shift, got, old, kept, wide, raw, tail, scale, new, out, rows, part):
    new[...] = combine(got, old[...], shift)
    spread(new[...], rows)
    sum_pass((wide, raw, tail, scale), rows, kept[...], part)
    send(part[...], out)


def last_kernel(shift, got, f, g, out, own_src, own_tgt):
    diff = (log2(jnp.sum(got[...], axis=0)) + shift) * math.log(2.0)
    out[...] = jnp.full(out.shape, jnp.sum(diff * diff), f32)
    own_src[...] = f[pl.ds(lax.axis_index(SRC_GROUP), 1), :] * (1.0 / UNIT)
    own_tgt[...] = g[pl.ds(lax.axis_index(TGT_GROUP), 1), :] * (1.0 / UNIT)


def call(kernel, args, outs, scratch, name):
    return pl.pallas_call(
        kernel,
        out_shape=[jax.ShapeDtypeStruct(shape, dtype) for shape, dtype in outs],
        in_specs=[pl.BlockSpec(memory_space=pltpu.VMEM)] * len(args),
        out_specs=[pl.BlockSpec(memory_space=pltpu.VMEM)] * len(outs),
        scratch_shapes=scratch,
        compiler_params=pltpu.CompilerParams(vmem_limit_bytes=48 * 1024 * 1024),
        name=name,
    )(*args)


def exchange(sent, group):
    return lax.all_to_all(sent, group, 0, 0)


def on_device(src_embed, tgt_embed, src_weight, tgt_weight):
    depth, per_dev = src_embed.shape
    src_count, tgt_count = lax.axis_size(SRC_GROUP), lax.axis_size(TGT_GROUP)
    total = per_dev * src_count * tgt_count
    shift = math.log2(total)
    src_size, tgt_size = per_dev * src_count, per_dev * tgt_count
    src_rows, tgt_rows = (src_count, per_dev), (tgt_count, per_dev)

    cells = (depth + PACK, per_dev)
    z_count = tgt_count // lax.axis_size("c")
    src_sent, tgt_sent = pl.pallas_call(
        pack_kernel,
        out_shape=[
            jax.ShapeDtypeStruct((1,) + cells, bf16),
            jax.ShapeDtypeStruct((z_count,) + cells, bf16),
        ],
        in_specs=[pl.BlockSpec(memory_space=pl.ANY)] * 4,
        out_specs=[pl.BlockSpec(memory_space=pltpu.VMEM)] * 2,
        scratch_shapes=[
            pltpu.VMEM((2, depth, per_dev), bf16),
            pltpu.VMEM((2, 1, per_dev), bf16),
            pltpu.SemaphoreType.DMA((4,)),
        ],
        name="pack",
    )(src_embed, tgt_embed, src_weight[None], tgt_weight[None])

    def neighbours(array, axis):
        size = lax.axis_size(axis)
        return [lax.ppermute(array, axis, [(i, i ^ k) for i in range(size)]) for k in range(1, size)]

    tgt = exchange(tgt_sent, ("zh", "zl"))
    src = jnp.concatenate([src_sent] + neighbours(src_sent, "x"), axis=0)
    src_far = jnp.stack(neighbours(src, "y"))
    (tgt_other,) = neighbours(tgt, "c")

    wide = 2 * depth + TAIL

    def operands(size, rows):
        return [((size, wide), bf16), ((TAIL, size), f32), ((depth, size), bf16), (rows, f32)]

    row_out = ((src_count,) + src_rows, f32)
    col_out = ((tgt_count,) + tgt_rows, f32)
    row_part = pltpu.VMEM(src_rows, f32)
    col_part = pltpu.VMEM(tgt_rows, f32)

    s_wide, s_tail, s_raw, s_scale = call(
        sources_kernel, [src, src_far], operands(src_size, src_rows), [], "sources"
    )
    t_wide, t_tail, t_raw, t_scale, sent = call(
        first_kernel,
        [tgt, tgt_other, s_tail, s_raw, s_scale],
        operands(tgt_size, tgt_rows) + [row_out],
        [row_part, row_part],
        "row_pass_1",
    )
    got = exchange(sent, SRC_GROUP)
    src_spread = pltpu.VMEM((src_size, LANES), f32)
    tgt_spread = pltpu.VMEM((tgt_size, LANES), f32)
    keep_tgt = [t_raw, t_tail, t_scale]
    keep_src = [s_raw, s_tail, s_scale]

    f, sent = call(
        functools.partial(second_kernel, shift),
        [got, s_wide] + keep_tgt,
        [(src_rows, f32), col_out],
        [src_spread, col_part, col_part],
        "col_pass_1",
    )
    got = exchange(sent, TGT_GROUP)
    g, sent = call(
        functools.partial(third_kernel, shift),
        [got, f, t_wide] + keep_src,
        [(tgt_rows, f32), row_out],
        [tgt_spread, row_part],
        "row_pass_2",
    )
    for step in range(2, ITERS + 1):
        got = exchange(sent, SRC_GROUP)
        f, sent = call(
            functools.partial(later_kernel, shift),
            [got, f, g, s_wide] + keep_tgt,
            [(src_rows, f32), col_out],
            [src_spread, col_part],
            f"col_pass_{step}",
        )
        got = exchange(sent, TGT_GROUP)
        g, sent = call(
            functools.partial(later_kernel, shift),
            [got, g, f, t_wide] + keep_src,
            [(tgt_rows, f32), row_out],
            [tgt_spread, row_part],
            f"row_pass_{step + 1}",
        )
    got = exchange(sent, SRC_GROUP)
    sent, own_src, own_tgt = call(
        functools.partial(last_kernel, shift),
        [got, f, g],
        [((tgt_count, 8, LANES), f32), ((1, per_dev), f32), ((1, per_dev), f32)],
        [],
        "mismatch",
    )
    squares = jnp.sum(exchange(sent, TGT_GROUP)[:, 0, 0])
    return own_src[0], own_tgt[0], jnp.sqrt(squares / total)


def solution(mesh, shape=(4, 4, 2, 4, 2)):
    placed = Mesh(mesh.devices.reshape(shape), AXES)
    return jax.shard_map(
        on_device,
        mesh=placed,
        in_specs=(P(None, AXES), P(None, AXES), P(AXES), P(AXES)),
        out_specs=(P(AXES), P(AXES), P()),
        check_vma=False,
    )
```

time: 166 us -> 149 us (0.90)
  waiting for transfers between devices: 21.8 us -> 5.23 us
  starting transfers between devices: 15.4 us -> 18.9 us
  other arithmetic: 2.37 us -> 0.65 us
    all_to_all x3 -> x1, waiting for transfers between devices: 21.8 us -> 4.73 us  [exchange(): return lax.all_to_all(sent, group, 0, 0)]
    ppermute x0 -> x7, starting transfers between devices: none -> 10.5 us  [neighbours(): lax.ppermute(array, axis, [(i, i ^ k) for i in range(size)])]
    all_to_all x3 -> x1, starting transfers between devices: 15.4 us -> 8.42 us  [exchange(): return lax.all_to_all(sent, group, 0, 0)]
    pallas_call x8 -> x9, Pallas kernels: 25.1 us -> 23.3 us  [call(): pl.pallas_call(kernel, out_shape=[jax.ShapeDtypeStruct(shape, dtype) for...]
    all_to_all x7 -> x8, blocking collectives: 96.4 us -> 96 us  [exchange(): return lax.all_to_all(sent, group, 0, 0)]
  transfers between devices with their start and end apart: 3 -> 8, of which waited for: 3 -> 2; matrix products, arithmetic and copies ran while one was open for 1% -> 0% of each run, Pallas kernels for 0% -> 0%
where the time goes in v2:
time: 149 us; the launch traced here: 148 us
  blocking collectives  96 us (64%)
  Pallas kernels  24.8 us (17%)
  starting transfers between devices  18.9 us (13%)
  waiting for transfers between devices  5.23 us (4%)
  between operations  2.57 us (2%)
    all_to_all x8, blocking collectives, exchange(): return lax.all_to_all(sent, group, 0, 0)  96 us
    pallas_call x9, Pallas kernels, call(): pl.pallas_call(kernel, out_shape=[jax.ShapeDtypeStruct(shape, dtype) for...  23.3 us
    ppermute x7, starting transfers between devices, neighbours(): lax.ppermute(array, axis, [(i, i ^ k) for i in range(size)])  10.5 us
    all_to_all x1, starting transfers between devices, exchange(): return lax.all_to_all(sent, group, 0, 0)  8.42 us
    all_to_all x1, waiting for transfers between devices, exchange(): return lax.all_to_all(sent, group, 0, 0)  4.73 us
  transfers between devices with their start and end apart: 8, of which 2 were waited for; matrix products, arithmetic and copies ran while one was open for 0% of the time, Pallas kernels for 0%

profile of v2, /device:TPU:1, one launch (start us, length us, event | category | flops | bytes accessed | tf_op | source)
XLA Modules:
  0.0 148.1 jit_solution(16309202651933252839)
XLA Ops:
  0.6 1.5 pack.1
  2.1 3.4 %collective-permute-start.3 = (bf16[1,80,128]{2,1,0:T(8,128)(2,1)}, bf16[1,80,128]{2,1,0:T(8,128)(2,1)S(1)}, u32[]{:S(2)}, u32[]{:S(2)}) collective-permute-start(bf16[1,80,128]{2,1,0:T(8,128)(2,1)} %get-tuple-element.30), channel_id=1, source_target_pairs={{0,192},{64,128},{128,64},{192,0},{1,193},{65,129},{129,65},{193,1... | collective-permute-start | bytes 61448 | tf_op jit(solution)/shard_map/ppermute | solution.py:256
  5.5 0.5 collective-permute-start.2
  6.2 8.4 %all-to-all-start = ((bf16[8,80,128]{2,1,0:T(8,128)(2,1)}), bf16[8,80,128]{2,1,0:T(8,128)(2,1)S(1)}, u32[]{:S(2)}, u32[]{:S(2)}) async-start(bf16[8,80,128]{2,1,0:T(8,128)(2,1)} %get-tuple-element.29), calls=%async_computation | async-start | bytes 327680 | tf_op jit(solution)/shard_map/all_to_all | solution.py:225
  14.7 2.8 %collective-permute-start.6 = (bf16[4,80,128]{2,1,0:T(8,128)(2,1)S(1)}, bf16[4,80,128]{2,1,0:T(8,128)(2,1)S(1)}, u32[]{:S(2)}, u32[]{:S(2)}) collective-permute-start(bf16[4,80,128]{2,1,0:T(8,128)(2,1)S(1)} %constant_dynamic-update-slice_fusion.own), channel_id=1, source_target_pairs={{0,6},{2,4},{4,2},{6,0},{1,7},{3,5},{5,3},{7,1},{8,14},{10,12},{12... | collective-permute-start | bytes 245768 | tf_op jit(solution)/shard_map/ppermute | solution.py:256
  18.2 4.7 %all-to-all-done.own = bf16[8,80,128]{2,1,0:T(8,128)(2,1)S(1)} async-done(((bf16[8,80,128]{2,1,0:T(8,128)(2,1)}), bf16[8,80,128]{2,1,0:T(8,128)(2,1)S(1)}, u32[]{:S(2)}, u32[]{:S(2)}) %all-to-all-start) | async-done | bytes 163872 | tf_op jit(solution)/shard_map/all_to_all | solution.py:225
  22.9 2.9 %collective-permute-start = (bf16[8,80,128]{2,1,0:T(8,128)(2,1)S(1)}, bf16[8,80,128]{2,1,0:T(8,128)(2,1)S(1)}, u32[]{:S(2)}, u32[]{:S(2)}) collective-permute-start(bf16[8,80,128]{2,1,0:T(8,128)(2,1)S(1)} %all-to-all-done.own), channel_id=1, source_target_pairs={{0,1},{1,0},{2,3},{3,2},{4,5},{5,4},{6,7},{7,6},{8,9},{9,8},{10,11... | collective-permute-start | bytes 491528 | tf_op jit(solution)/shard_map/ppermute | solution.py:256
  26.9 4.2 %row_pass_1.1 = (bf16[2048,144]{1,0:T(8,128)(2,1)S(1)}, f32[16,2048]{1,0:T(8,128)S(1)}, bf16[64,2048]{1,0:T(8,128)(2,1)S(1)}, f32[16,128]{1,0:T(8,128)S(1)}, f32[16,16,128]{2,1,0:T(8,128)S(1)}) custom-call(bf16[8,80,128]{2,1,0:T(8,128)(2,1)S(1)} %all-to-all-done.own, bf16[8,80,128]{2,1,0:T(8,128)(2,1)S(1)} %collective-permute-done.other, ...), custom_call_target="tpu_custom_call" | custom-call | tf_op jit(solution)/shard_map/row_pass_1/pallas_call | solution.py:213
  31.0 13.2 %all_to_all.45.got = f32[16,16,128]{2,1,0:T(8,128)S(1)} all-to-all(f32[16,16,128]{2,1,0:T(8,128)S(1)} %get-tuple-element.34), channel_id=1, replica_groups=mesh['x'=4,'zh'=4,'zl'=2,'y'=4,'c'=2] {'x','y'}, dimensions={0} | all-to-all | bytes 262144 | tf_op jit(solution)/shard_map/all_to_all | solution.py:225
  44.3 4.2 %col_pass_1.1 = (f32[16,128]{1,0:T(8,128)S(1)}, f32[16,16,128]{2,1,0:T(8,128)S(1)}) custom-call(f32[16,16,128]{2,1,0:T(8,128)S(1)} %all_to_all.45.got, bf16[2048,144]{1,0:T(8,128)(2,1)S(1)} %get-tuple-element.35.wide, bf16[64,2048]{1,0:T(8,128)(2,1)S(1)} %get-tuple-element.36.raw, f32[16,2048]{1,0:T(8,128)S(1)} %get-tuple-element.37.tail, ...), custom_call_target="tpu_custom_call" | custom-call | tf_op jit(solution)/shard_map/col_pass_1/pallas_call | solution.py:213
  48.5 15.6 %all_to_all.46.got = f32[16,16,128]{2,1,0:T(8,128)S(1)} all-to-all(f32[16,16,128]{2,1,0:T(8,128)S(1)} %get-tuple-element.39), channel_id=1, replica_groups=mesh['x'=4,'zh'=4,'zl'=2,'y'=4,'c'=2] {'zh','zl','c'}, dimensions={0} | all-to-all | bytes 262144 | tf_op jit(solution)/shard_map/all_to_all | solution.py:225
  64.1 2.8 %row_pass_2.1 = (f32[16,128]{1,0:T(8,128)S(1)}, f32[16,16,128]{2,1,0:T(8,128)S(1)}) custom-call(f32[16,16,128]{2,1,0:T(8,128)S(1)} %all_to_all.46.got, f32[16,128]{1,0:T(8,128)S(1)} %get-tuple-element.40.kept.old, bf16[2048,144]{1,0:T(8,128)(2,1)S(1)} %get-tuple-element.41.wide, bf16[64,2048]{1,0:T(8,128)(2,1)S(1)} %get-tuple-element.32.s_raw.raw, ...), custom_call_target="tpu_custom_call" | custom-call | tf_op jit(solution)/shard_map/row_pass_2/pallas_call | solution.py:213
  67.0 10.3 %all_to_all.47.got = f32[16,16,128]{2,1,0:T(8,128)S(1)} all-to-all(f32[16,16,128]{2,1,0:T(8,128)S(1)} %get-tuple-element.42), channel_id=1, replica_groups=mesh['x'=4,'zh'=4,'zl'=2,'y'=4,'c'=2] {'x','y'}, dimensions={0} | all-to-all | bytes 262144 | tf_op jit(solution)/shard_map/all_to_all | solution.py:225
  77.2 2.8 %col_pass_2.1 = (f32[16,128]{1,0:T(8,128)S(1)}, f32[16,16,128]{2,1,0:T(8,128)S(1)}) custom-call(f32[16,16,128]{2,1,0:T(8,128)S(1)} %all_to_all.47.got, f32[16,128]{1,0:T(8,128)S(1)} %get-tuple-element.40.kept.old, f32[16,128]{1,0:T(8,128)S(1)} %get-tuple-element.43.kept.old, bf16[2048,144]{1,0:T(8,128)(2,1)S(1)} %get-tuple-element.35.wide, ...), custom_call_target="tpu_custom_call" | custom-call | tf_op jit(solution)/shard_map/col_pass_2/pallas_call | solution.py:213
  80.0 12.6 %all_to_all.48.got = f32[16,16,128]{2,1,0:T(8,128)S(1)} all-to-all(f32[16,16,128]{2,1,0:T(8,128)S(1)} %get-tuple-element.44), channel_id=1, replica_groups=mesh['x'=4,'zh'=4,'zl'=2,'y'=4,'c'=2] {'zh','zl','c'}, dimensions={0} | all-to-all | bytes 262144 | tf_op jit(solution)/shard_map/all_to_all | solution.py:225
  92.6 2.8 %row_pass_3.1 = (f32[16,128]{1,0:T(8,128)S(1)}, f32[16,16,128]{2,1,0:T(8,128)S(1)}) custom-call(f32[16,16,128]{2,1,0:T(8,128)S(1)} %all_to_all.48.got, f32[16,128]{1,0:T(8,128)S(1)} %get-tuple-element.43.kept.old, f32[16,128]{1,0:T(8,128)S(1)} %get-tuple-element.45.kept.old, bf16[2048,144]{1,0:T(8,128)(2,1)S(1)} %get-tuple-element.41.wide, ...), custom_call_target="tpu_custom_call" | custom-call | tf_op jit(solution)/shard_map/row_pass_3/pallas_call | solution.py:213
  95.4 10.2 %all_to_all.49.got = f32[16,16,128]{2,1,0:T(8,128)S(1)} all-to-all(f32[16,16,128]{2,1,0:T(8,128)S(1)} %get-tuple-element.46), channel_id=1, replica_groups=mesh['x'=4,'zh'=4,'zl'=2,'y'=4,'c'=2] {'x','y'}, dimensions={0} | all-to-all | bytes 262144 | tf_op jit(solution)/shard_map/all_to_all | solution.py:225
  105.6 2.8 %col_pass_3.1 = (f32[16,128]{1,0:T(8,128)S(1)}, f32[16,16,128]{2,1,0:T(8,128)S(1)}) custom-call(f32[16,16,128]{2,1,0:T(8,128)S(1)} %all_to_all.49.got, f32[16,128]{1,0:T(8,128)S(1)} %get-tuple-element.45.kept.old, f32[16,128]{1,0:T(8,128)S(1)} %get-tuple-element.47.kept.old, bf16[2048,144]{1,0:T(8,128)(2,1)S(1)} %get-tuple-element.35.wide, ...), custom_call_target="tpu_custom_call" | custom-call | tf_op jit(solution)/shard_map/col_pass_3/pallas_call | solution.py:213
  108.3 12.6 %all_to_all.50.got = f32[16,16,128]{2,1,0:T(8,128)S(1)} all-to-all(f32[16,16,128]{2,1,0:T(8,128)S(1)} %get-tuple-element.48), channel_id=1, replica_groups=mesh['x'=4,'zh'=4,'zl'=2,'y'=4,'c'=2] {'zh','zl','c'}, dimensions={0} | all-to-all | bytes 262144 | tf_op jit(solution)/shard_map/all_to_all | solution.py:225
  121.0 2.8 %row_pass_4.1 = (f32[16,128]{1,0:T(8,128)S(1)}, f32[16,16,128]{2,1,0:T(8,128)S(1)}) custom-call(f32[16,16,128]{2,1,0:T(8,128)S(1)} %all_to_all.50.got, f32[16,128]{1,0:T(8,128)S(1)} %get-tuple-element.47.kept.old, f32[16,128]{1,0:T(8,128)S(1)} %get-tuple-element.49.kept.f, bf16[2048,144]{1,0:T(8,128)(2,1)S(1)} %get-tuple-element.41.wide, ...), custom_call_target="tpu_custom_call" | custom-call | tf_op jit(solution)/shard_map/row_pass_4/pallas_call | solution.py:213
  123.7 10.2 %all_to_all.51.got = f32[16,16,128]{2,1,0:T(8,128)S(1)} all-to-all(f32[16,16,128]{2,1,0:T(8,128)S(1)} %get-tuple-element.50), channel_id=1, replica_groups=mesh['x'=4,'zh'=4,'zl'=2,'y'=4,'c'=2] {'x','y'}, dimensions={0} | all-to-all | bytes 262144 | tf_op jit(solution)/shard_map/all_to_all | solution.py:225
  133.9 0.5 mismatch.1
  134.5 11.2 %all_to_all.52 = f32[16,8,128]{2,1,0:T(8,128)S(1)} all-to-all(f32[16,8,128]{2,1,0:T(8,128)S(1)} %get-tuple-element.54), channel_id=1, replica_groups=mesh['x'=4,'zh'=4,'zl'=2,'y'=4,'c'=2] {'zh','zl','c'}, dimensions={0} | all-to-all | bytes 131072 | tf_op jit(solution)/shard_map/all_to_all | solution.py:225
  145.7 0.6 slice_reduce_fusion
  (18 shorter events, 1.9 us)
Async XLA Ops:
  2.1 12.6 %collective-permute-start.3 = (bf16[1,80,128]{2,1,0:T(8,128)(2,1)}, bf16[1,80,128]{2,1,0:T(8,128)(2,1)S(1)}, u32[]{:S(2)}, u32[]{:S(2)}) collective-permute-start(bf16[1,80,128]{2,1,0:T(8,128)(2,1)} %get-tuple-element.30), channel_id=1, source_target_pairs={{0,192},{64,128},{128,64},{192,0},{1,193},{65,129},{129,65},{193,1... | collective-permute-start | bytes 61448 | tf_op jit(solution)/shard_map/ppermute | solution.py:256
  5.5 9.1 %collective-permute-start.2 = (bf16[1,80,128]{2,1,0:T(8,128)(2,1)}, bf16[1,80,128]{2,1,0:T(8,128)(2,1)S(1)}, u32[]{:S(2)}, u32[]{:S(2)}) collective-permute-start(bf16[1,80,128]{2,1,0:T(8,128)(2,1)} %get-tuple-element.30), channel_id=1, source_target_pairs={{0,128},{64,192},{128,0},{192,64},{1,129},{65,193},{129,1},{193,65... | collective-permute-start | bytes 61448 | tf_op jit(solution)/shard_map/ppermute | solution.py:256
  6.0 8.6 %collective-permute-start.1 = (bf16[1,80,128]{2,1,0:T(8,128)(2,1)}, bf16[1,80,128]{2,1,0:T(8,128)(2,1)S(1)}, u32[]{:S(2)}, u32[]{:S(2)}) collective-permute-start(bf16[1,80,128]{2,1,0:T(8,128)(2,1)} %get-tuple-element.30), channel_id=1, source_target_pairs={{0,64},{64,0},{128,192},{192,128},{1,65},{65,1},{129,193},{193,129... | collective-permute-start | bytes 61448 | tf_op jit(solution)/shard_map/ppermute | solution.py:256
  6.2 8.4 %copy-start = (bf16[1,80,128]{2,1,0:T(8,128)(2,1)S(1)}, bf16[1,80,128]{2,1,0:T(8,128)(2,1)}, u32[]{:S(2)}) copy-start(bf16[1,80,128]{2,1,0:T(8,128)(2,1)} %get-tuple-element.30) | copy-start | bytes 61444
  6.2 16.7 %all-to-all-start = ((bf16[8,80,128]{2,1,0:T(8,128)(2,1)}), bf16[8,80,128]{2,1,0:T(8,128)(2,1)S(1)}, u32[]{:S(2)}, u32[]{:S(2)}) async-start(bf16[8,80,128]{2,1,0:T(8,128)(2,1)} %get-tuple-element.29), calls=%async_computation | async-start | bytes 327680 | tf_op jit(solution)/shard_map/all_to_all | solution.py:225
  14.7 11.1 %collective-permute-start.6 = (bf16[4,80,128]{2,1,0:T(8,128)(2,1)S(1)}, bf16[4,80,128]{2,1,0:T(8,128)(2,1)S(1)}, u32[]{:S(2)}, u32[]{:S(2)}) collective-permute-start(bf16[4,80,128]{2,1,0:T(8,128)(2,1)S(1)} %constant_dynamic-update-slice_fusion.own), channel_id=1, source_target_pairs={{0,6},{2,4},{4,2},{6,0},{1,7},{3,5},{5,3},{7,1},{8,14},{10,12},{12... | collective-permute-start | bytes 245768 | tf_op jit(solution)/shard_map/ppermute | solution.py:256
  17.5 8.3 %collective-permute-start.5 = (bf16[4,80,128]{2,1,0:T(8,128)(2,1)S(1)}, bf16[4,80,128]{2,1,0:T(8,128)(2,1)S(1)}, u32[]{:S(2)}, u32[]{:S(2)}) collective-permute-start(bf16[4,80,128]{2,1,0:T(8,128)(2,1)S(1)} %constant_dynamic-update-slice_fusion.own), channel_id=1, source_target_pairs={{0,4},{2,6},{4,0},{6,2},{1,5},{3,7},{5,1},{7,3},{8,12},{10,14},{12... | collective-permute-start | bytes 245768 | tf_op jit(solution)/shard_map/ppermute | solution.py:256
  17.9 8.0 %collective-permute-start.4 = (bf16[4,80,128]{2,1,0:T(8,128)(2,1)S(1)}, bf16[4,80,128]{2,1,0:T(8,128)(2,1)S(1)}, u32[]{:S(2)}, u32[]{:S(2)}) collective-permute-start(bf16[4,80,128]{2,1,0:T(8,128)(2,1)S(1)} %constant_dynamic-update-slice_fusion.own), channel_id=1, source_target_pairs={{0,2},{2,0},{4,6},{6,4},{1,3},{3,1},{5,7},{7,5},{8,10},{10,8},{12,... | collective-permute-start | bytes 245768 | tf_op jit(solution)/shard_map/ppermute | solution.py:256
  22.9 3.9 %collective-permute-start = (bf16[8,80,128]{2,1,0:T(8,128)(2,1)S(1)}, bf16[8,80,128]{2,1,0:T(8,128)(2,1)S(1)}, u32[]{:S(2)}, u32[]{:S(2)}) collective-permute-start(bf16[8,80,128]{2,1,0:T(8,128)(2,1)S(1)} %all-to-all-done.own), channel_id=1, source_target_pairs={{0,1},{1,0},{2,3},{3,2},{4,5},{5,4},{6,7},{7,6},{8,9},{9,8},{10,11... | collective-permute-start | bytes 491528 | tf_op jit(solution)/shard_map/ppermute | solution.py:256

commit v3 on v2

--- a/solution.py
+++ b/solution.py
@@ -13,10 +13,13 @@
 LANES = 128
 TAIL = 16
 PACK = 16
-WIDTH = 2 * LANES
+BLOCKS = 2
+WIDTH = BLOCKS * LANES
 HEAD = 512
-MARGIN = 80.0
+MARGIN = 100.0
+REACH = 110.0
 LARGE = 2.0**120
+SMALL = 2.0**-102
 UNIT = 1.0 / (EPS * math.log(2.0))
 AXES = ("x", "zh", "zl", "y", "c")
 SRC_GROUP = ("x", "y")
@@ -77,54 +80,80 @@
         rows_ref[pl.ds(b * LANES, LANES), :] = jnp.broadcast_to(column[:, b : b + 1], (LANES, LANES))
 
 
-def strip_score(s, wide_ref, raw_ref, tail_ref, scale_ref, ratio, rows_ref):
-    at = pl.ds(s * WIDTH, WIDTH) if isinstance(s, int) else pl.ds(pl.multiple_of(s * WIDTH, WIDTH), WIDTH)
-
-    def row(array):
-        return jnp.concatenate([array[pl.ds(2 * s, 1), :], array[pl.ds(2 * s + 1, 1), :]], axis=1)
-
+def strip_of(s):
+    return pl.ds(s * WIDTH, WIDTH) if isinstance(s, int) else pl.ds(pl.multiple_of(s * WIDTH, WIDTH), WIDTH)
+
+
+def get(ref, s):
+    return jnp.concatenate([ref[pl.ds(BLOCKS * s + k, 1), :] for k in range(BLOCKS)], axis=1)
+
+
+def put(ref, s, value):
+    for k in range(BLOCKS):
+        ref[pl.ds(BLOCKS * s + k, 1), :] = value[:, k * LANES : (k + 1) * LANES]
+
+
+def strip_score(s, count, operands, rows_ref, ratio_ref):
+    wide_ref, raw_ref, tail_ref, scale_ref = operands
+    at = strip_of(s)
     tail = tail_ref[:, at]
-    if ratio is not None:
-        parts = [jnp.concatenate([p[2 * s : 2 * s + 1], p[2 * s + 1 : 2 * s + 2]], axis=1) for p in ratio]
-        tail = tail + stack([(6, parts[0]), (7, parts[1]), (8, parts[2])], WIDTH)
+    if ratio_ref is not None:
+        tail = tail + stack([(6 + k, get(ratio_ref.at[k], s)) for k in range(3)], WIDTH)
     raw = raw_ref[:, at]
     operand = jnp.concatenate([raw, raw, tail.astype(bf16)], axis=0)
-    score = jnp.dot(wide_ref[...], operand, preferred_element_type=f32) * row(scale_ref)
+    score = jnp.dot(wide_ref[:count, :], operand, preferred_element_type=f32) * get(scale_ref, s)
     if rows_ref is not None:
-        score = score + jnp.concatenate([rows_ref[...], rows_ref[...]], axis=1)
+        rows = rows_ref[:count, :]
+        score = score + jnp.concatenate([rows] * BLOCKS, axis=1)
     return score
 
 
-def put(ref, s, value):
-    ref[pl.ds(2 * s, 1), :] = value[:, :LANES]
-    ref[pl.ds(2 * s + 1, 1), :] = value[:, LANES:]
-
-
-def sum_pass(operands, rows_ref, kept, part_ref):
-    ratio = pieces(kept / operands[3][...])
-    for s in range(part_ref.shape[0] // 2):
-        score = strip_score(s, *operands, ratio, rows_ref)
+def strips(count, body, unroll):
+    if unroll:
+        for s in range(count):
+            body(s)
+    else:
+
+        def step(s, carry):
+            body(s)
+            return carry
+
+        lax.fori_loop(0, count, step, 0)
+
+
+def find_tops(count, operands, rows_ref, top_ref, unroll=True):
+    def body(s):
+        put(top_ref, s, jnp.max(strip_score(s, count, operands, rows_ref, None), axis=0, keepdims=True))
+
+    strips(top_ref.shape[0] // BLOCKS, body, unroll)
+
+
+def sum_pass(operands, rows_ref, kept, ratio_ref, part_ref, unroll=True):
+    for k, piece in enumerate(pieces(kept / operands[3][...])):
+        ratio_ref[k] = piece
+
+    def body(s):
+        score = strip_score(s, operands[0].shape[0], operands, rows_ref, ratio_ref)
         put(part_ref, s, jnp.sum(jnp.exp2(score), axis=0, keepdims=True))
 
-
-def log_pass(operands, rows_ref, part_ref, top_ref):
-    count = part_ref.shape[0] // 2
-    for s in range(count):
-        score = strip_score(s, *operands, None, rows_ref)
-        top = jnp.max(score[: min(HEAD, score.shape[0])], axis=0, keepdims=True) + MARGIN
-        put(top_ref, s, top)
-        put(part_ref, s, jnp.sum(jnp.exp2(score - top), axis=0, keepdims=True))
-
-    @pl.when(jnp.logical_not(jnp.max(part_ref[...]) < LARGE))
+    strips(part_ref.shape[0] // BLOCKS, body, unroll)
+
+
+def log_pass(operands, rows_ref, ratio_ref, part_ref, top_ref, bound=None):
+    size = operands[0].shape[0]
+    if bound is None:
+        find_tops(min(HEAD, size), operands, rows_ref, top_ref)
+        top_ref[...] = top_ref[...] + MARGIN
+    else:
+        top_ref[...] = jnp.full(top_ref.shape, bound - REACH, f32)
+    sum_pass(operands, rows_ref, -top_ref[...], ratio_ref, part_ref)
+    mass = part_ref[...]
+    sound = (mass < LARGE) & (mass > SMALL)
+
+    @pl.when(jnp.min(sound.astype(f32)) < 0.5)
     def _():
-        def again(s, carry):
-            score = strip_score(s, *operands, None, rows_ref)
-            top = jnp.max(score, axis=0, keepdims=True)
-            put(top_ref, s, top)
-            put(part_ref, s, jnp.sum(jnp.exp2(score - top), axis=0, keepdims=True))
-            return carry
-
-        lax.fori_loop(0, count, again, 0)
+        find_tops(size, operands, rows_ref, top_ref, unroll=False)
+        sum_pass(operands, rows_ref, -top_ref[...], ratio_ref, part_ref, unroll=False)
 
 
 def combine_logs(got_ref, shift):
@@ -172,33 +201,33 @@
     prepare(blocks, wide, tail, raw, scale)
 
 
-def first_kernel(own, other, s_tail, s_raw, s_scale, t_wide, t_tail, t_raw, t_scale, out, part, top):
+def first_kernel(own, other, s_tail, s_raw, s_scale, t_wide, t_tail, t_raw, t_scale, out, ratio, part, top):
     core = lax.axis_index("c")
     blocks = [(own.at[z], 2 * z + core) for z in range(own.shape[0])]
     blocks += [(other.at[z], 2 * z + 1 - core) for z in range(own.shape[0])]
     prepare(blocks, t_wide, t_tail, t_raw, t_scale)
-    log_pass((t_wide, s_raw, s_tail, s_scale), None, part, top)
+    log_pass((t_wide, s_raw, s_tail, s_scale), None, ratio, part, top)
     send(top[...] + log2(part[...]), out)
 
 
-def second_kernel(shift, got, wide, raw, tail, scale, new, out, rows, part, top):
+def second_kernel(shift, got, wide, raw, tail, scale, new, out, rows, ratio, part, top):
     new[...] = combine_logs(got, shift)
     spread(new[...], rows)
-    log_pass((wide, raw, tail, scale), rows, part, top)
+    log_pass((wide, raw, tail, scale), rows, ratio, part, top, -shift)
     send(top[...] + log2(part[...]), out)
 
 
-def third_kernel(shift, got, kept, wide, raw, tail, scale, new, out, rows, part):
+def third_kernel(shift, got, kept, wide, raw, tail, scale, new, out, rows, ratio, part):
     new[...] = combine_logs(got, shift)
     spread(new[...], rows)
-    sum_pass((wide, raw, tail, scale), rows, kept[...], part)
+    sum_pass((wide, raw, tail, scale), rows, kept[...], ratio, part)
     send(part[...], out)
 
 
-def later_kernel(shift, got, old, kept, wide, raw, tail, scale, new, out, rows, part):
+def later_kernel(shift, got, old, kept, wide, raw, tail, scale, new, out, rows, ratio, part):
     new[...] = combine(got, old[...], shift)
     spread(new[...], rows)
-    sum_pass((wide, raw, tail, scale), rows, kept[...], part)
+    sum_pass((wide, raw, tail, scale), rows, kept[...], ratio, part)
     send(part[...], out)
 
 
@@ -269,6 +298,8 @@
     col_out = ((tgt_count,) + tgt_rows, f32)
     row_part = pltpu.VMEM(src_rows, f32)
     col_part = pltpu.VMEM(tgt_rows, f32)
+    row_ratio = pltpu.VMEM((3,) + src_rows, f32)
+    col_ratio = pltpu.VMEM((3,) + tgt_rows, f32)
 
     s_wide, s_tail, s_raw, s_scale = call(
         sources_kernel, [src, src_far], operands(src_size, src_rows), [], "sources"
@@ -277,7 +308,7 @@
         first_kernel,
         [tgt, tgt_other, s_tail, s_raw, s_scale],
         operands(tgt_size, tgt_rows) + [row_out],
-        [row_part, row_part],
+        [row_ratio, row_part, row_part],
         "row_pass_1",
     )
     got = exchange(sent, SRC_GROUP)
@@ -290,7 +321,7 @@
         functools.partial(second_kernel, shift),
         [got, s_wide] + keep_tgt,
         [(src_rows, f32), col_out],
-        [src_spread, col_part, col_part],
+        [src_spread, col_ratio, col_part, col_part],
         "col_pass_1",
     )
     got = exchange(sent, TGT_GROUP)
@@ -298,7 +329,7 @@
         functools.partial(third_kernel, shift),
         [got, f, t_wide] + keep_src,
         [(tgt_rows, f32), row_out],
-        [tgt_spread, row_part],
+        [tgt_spread, row_ratio, row_part],
         "row_pass_2",
     )
     for step in range(2, ITERS + 1):
@@ -307,22 +338,22 @@
             functools.partial(later_kernel, shift),
             [got, f, g, s_wide] + keep_tgt,
             [(src_rows, f32), col_out],
-            [src_spread, col_part],
-            f"col_pass_{step}",
+            [src_spread, col_ratio, col_part],
+            "later_pass",
         )
         got = exchange(sent, TGT_GROUP)
         g, sent = call(
             functools.partial(later_kernel, shift),
             [got, g, f, t_wide] + keep_src,
             [(tgt_rows, f32), row_out],
-            [tgt_spread, row_part],
-            f"row_pass_{step + 1}",
+            [tgt_spread, row_ratio, row_part],
+            "later_pass",
         )
     got = exchange(sent, SRC_GROUP)
     sent, own_src, own_tgt = call(
         functools.partial(last_kernel, shift),
         [got, f, g],
-        [((tgt_count, 8, LANES), f32), ((1, per_dev), f32), ((1, per_dev), f32)],
+        [((tgt_count, 1, LANES), f32), ((1, per_dev), f32), ((1, per_dev), f32)],
         [],
         "mismatch",
     )

time: 149 us -> 146 us (0.980)
  Pallas kernels: 24.8 us -> 23.2 us
    pallas_call x9, Pallas kernels: 23.3 us -> 21.7 us  [call(): pl.pallas_call(kernel, out_shape=[jax.ShapeDtypeStruct(shape, dtype) for...]
where the time goes in v3:
time: 146 us
  blocking collectives  95.2 us (65%)
  Pallas kernels  23.2 us (16%)
  starting transfers between devices  18.9 us (13%)
  waiting for transfers between devices  5.23 us (4%)
  between operations  2.57 us (2%)
    all_to_all x8, blocking collectives, exchange(): return lax.all_to_all(sent, group, 0, 0)  95.2 us
    pallas_call x9, Pallas kernels, call(): pl.pallas_call(kernel, out_shape=[jax.ShapeDtypeStruct(shape, dtype) for...  21.7 us
    ppermute x7, starting transfers between devices, neighbours(): lax.ppermute(array, axis, [(i, i ^ k) for i in range(size)])  10.5 us
    all_to_all x1, starting transfers between devices, exchange(): return lax.all_to_all(sent, group, 0, 0)  8.42 us
    all_to_all x1, waiting for transfers between devices, exchange(): return lax.all_to_all(sent, group, 0, 0)  4.73 us
  transfers between devices with their start and end apart: 8, of which 2 were waited for; matrix products, arithmetic and copies ran while one was open for 0% of the time, Pallas kernels for 0%

profile of v3, /device:TPU:1, one launch (start us, length us, event | category | flops | bytes accessed | tf_op | source)
XLA Modules:
  0.0 145.8 jit_solution(5432360472282813909)
XLA Ops:
  0.6 1.5 %pack.1 = (bf16[1,80,128]{2,1,0:T(8,128)(2,1)}, bf16[8,80,128]{2,1,0:T(8,128)(2,1)}) custom-call(bf16[64,128]{1,0:T(8,128)(2,1)} %src_embed.1, bf16[64,128]{1,0:T(8,128)(2,1)} %tgt_embed.1, bf16[1,128]{1,0:T(2,128)(2,1)} %bitcast.10, bf16[1,128]{1,0:T(2,128)(2,1)} %bitcast.11), custom_call_target="tpu_custom_call" | custom-call | tf_op jit(solution)/shard_map/pack/pallas_call | solution.py:267
  2.1 3.4 %collective-permute-start.3 = (bf16[1,80,128]{2,1,0:T(8,128)(2,1)}, bf16[1,80,128]{2,1,0:T(8,128)(2,1)S(1)}, u32[]{:S(2)}, u32[]{:S(2)}) collective-permute-start(bf16[1,80,128]{2,1,0:T(8,128)(2,1)} %get-tuple-element.30), channel_id=1, source_target_pairs={{0,192},{64,128},{128,64},{192,0},{1,193},{65,129},{129,65},{193,1... | collective-permute-start | bytes 61448 | tf_op jit(solution)/shard_map/ppermute | solution.py:285
  5.5 0.5 collective-permute-start.2
  6.2 8.4 %all-to-all-start = ((bf16[8,80,128]{2,1,0:T(8,128)(2,1)}), bf16[8,80,128]{2,1,0:T(8,128)(2,1)S(1)}, u32[]{:S(2)}, u32[]{:S(2)}) async-start(bf16[8,80,128]{2,1,0:T(8,128)(2,1)} %get-tuple-element.29), calls=%async_computation | async-start | bytes 327680 | tf_op jit(solution)/shard_map/all_to_all | solution.py:254
  14.7 2.8 %collective-permute-start.6 = (bf16[4,80,128]{2,1,0:T(8,128)(2,1)S(1)}, bf16[4,80,128]{2,1,0:T(8,128)(2,1)S(1)}, u32[]{:S(2)}, u32[]{:S(2)}) collective-permute-start(bf16[4,80,128]{2,1,0:T(8,128)(2,1)S(1)} %constant_dynamic-update-slice_fusion.own), channel_id=1, source_target_pairs={{0,6},{2,4},{4,2},{6,0},{1,7},{3,5},{5,3},{7,1},{8,14},{10,12},{12... | collective-permute-start | bytes 245768 | tf_op jit(solution)/shard_map/ppermute | solution.py:285
  18.2 4.7 %all-to-all-done.own = bf16[8,80,128]{2,1,0:T(8,128)(2,1)S(1)} async-done(((bf16[8,80,128]{2,1,0:T(8,128)(2,1)}), bf16[8,80,128]{2,1,0:T(8,128)(2,1)S(1)}, u32[]{:S(2)}, u32[]{:S(2)}) %all-to-all-start) | async-done | bytes 163872 | tf_op jit(solution)/shard_map/all_to_all | solution.py:254
  22.9 2.9 %collective-permute-start = (bf16[8,80,128]{2,1,0:T(8,128)(2,1)S(1)}, bf16[8,80,128]{2,1,0:T(8,128)(2,1)S(1)}, u32[]{:S(2)}, u32[]{:S(2)}) collective-permute-start(bf16[8,80,128]{2,1,0:T(8,128)(2,1)S(1)} %all-to-all-done.own), channel_id=1, source_target_pairs={{0,1},{1,0},{2,3},{3,2},{4,5},{5,4},{6,7},{7,6},{8,9},{9,8},{10,11... | collective-permute-start | bytes 491528 | tf_op jit(solution)/shard_map/ppermute | solution.py:285
  26.9 3.7 %row_pass_1.1 = (bf16[2048,144]{1,0:T(8,128)(2,1)S(1)}, f32[16,2048]{1,0:T(8,128)S(1)}, bf16[64,2048]{1,0:T(8,128)(2,1)S(1)}, f32[16,128]{1,0:T(8,128)S(1)}, f32[16,16,128]{2,1,0:T(8,128)S(1)}) custom-call(bf16[8,80,128]{2,1,0:T(8,128)(2,1)S(1)} %all-to-all-done.own, bf16[8,80,128]{2,1,0:T(8,128)(2,1)S(1)} %collective-permute-done.other, ...), custom_call_target="tpu_custom_call" | custom-call | tf_op jit(solution)/shard_map/row_pass_1/pallas_call | solution.py:242
  30.5 13.3 %all_to_all.45.got = f32[16,16,128]{2,1,0:T(8,128)S(1)} all-to-all(f32[16,16,128]{2,1,0:T(8,128)S(1)} %get-tuple-element.34), channel_id=1, replica_groups=mesh['x'=4,'zh'=4,'zl'=2,'y'=4,'c'=2] {'x','y'}, dimensions={0} | all-to-all | bytes 262144 | tf_op jit(solution)/shard_map/all_to_all | solution.py:254
  43.8 3.1 %col_pass_1.1 = (f32[16,128]{1,0:T(8,128)S(1)}, f32[16,16,128]{2,1,0:T(8,128)S(1)}) custom-call(f32[16,16,128]{2,1,0:T(8,128)S(1)} %all_to_all.45.got, bf16[2048,144]{1,0:T(8,128)(2,1)S(1)} %get-tuple-element.35.wide, bf16[64,2048]{1,0:T(8,128)(2,1)S(1)} %get-tuple-element.36.raw, f32[16,2048]{1,0:T(8,128)S(1)} %get-tuple-element.37.tail, ...), custom_call_target="tpu_custom_call" | custom-call | tf_op jit(solution)/shard_map/col_pass_1/pallas_call | solution.py:242
  46.9 15.6 %all_to_all.46.got = f32[16,16,128]{2,1,0:T(8,128)S(1)} all-to-all(f32[16,16,128]{2,1,0:T(8,128)S(1)} %get-tuple-element.39), channel_id=1, replica_groups=mesh['x'=4,'zh'=4,'zl'=2,'y'=4,'c'=2] {'zh','zl','c'}, dimensions={0} | all-to-all | bytes 262144 | tf_op jit(solution)/shard_map/all_to_all | solution.py:254
  62.5 2.8 %row_pass_2.1 = (f32[16,128]{1,0:T(8,128)S(1)}, f32[16,16,128]{2,1,0:T(8,128)S(1)}) custom-call(f32[16,16,128]{2,1,0:T(8,128)S(1)} %all_to_all.46.got, f32[16,128]{1,0:T(8,128)S(1)} %get-tuple-element.40.kept.old, bf16[2048,144]{1,0:T(8,128)(2,1)S(1)} %get-tuple-element.41.wide, bf16[64,2048]{1,0:T(8,128)(2,1)S(1)} %get-tuple-element.32.s_raw.raw, ...), custom_call_target="tpu_custom_call" | custom-call | tf_op jit(solution)/shard_map/row_pass_2/pallas_call | solution.py:242
  65.4 10.3 %all_to_all.47.got = f32[16,16,128]{2,1,0:T(8,128)S(1)} all-to-all(f32[16,16,128]{2,1,0:T(8,128)S(1)} %get-tuple-element.42), channel_id=1, replica_groups=mesh['x'=4,'zh'=4,'zl'=2,'y'=4,'c'=2] {'x','y'}, dimensions={0} | all-to-all | bytes 262144 | tf_op jit(solution)/shard_map/all_to_all | solution.py:254
  75.6 2.8 %later_pass.4 = (f32[16,128]{1,0:T(8,128)S(1)}, f32[16,16,128]{2,1,0:T(8,128)S(1)}) custom-call(f32[16,16,128]{2,1,0:T(8,128)S(1)} %all_to_all.47.got, f32[16,128]{1,0:T(8,128)S(1)} %get-tuple-element.40.kept.old, f32[16,128]{1,0:T(8,128)S(1)} %get-tuple-element.43.kept.old, bf16[2048,144]{1,0:T(8,128)(2,1)S(1)} %get-tuple-element.35.wide, ...), custom_call_target="tpu_custom_call" | custom-call | tf_op jit(solution)/shard_map/later_pass/pallas_call | solution.py:242
  78.4 12.6 %all_to_all.48.got = f32[16,16,128]{2,1,0:T(8,128)S(1)} all-to-all(f32[16,16,128]{2,1,0:T(8,128)S(1)} %get-tuple-element.44), channel_id=1, replica_groups=mesh['x'=4,'zh'=4,'zl'=2,'y'=4,'c'=2] {'zh','zl','c'}, dimensions={0} | all-to-all | bytes 262144 | tf_op jit(solution)/shard_map/all_to_all | solution.py:254
  91.0 2.8 %later_pass.5 = (f32[16,128]{1,0:T(8,128)S(1)}, f32[16,16,128]{2,1,0:T(8,128)S(1)}) custom-call(f32[16,16,128]{2,1,0:T(8,128)S(1)} %all_to_all.48.got, f32[16,128]{1,0:T(8,128)S(1)} %get-tuple-element.43.kept.old, f32[16,128]{1,0:T(8,128)S(1)} %get-tuple-element.45.kept.old, bf16[2048,144]{1,0:T(8,128)(2,1)S(1)} %get-tuple-element.41.wide, ...), custom_call_target="tpu_custom_call" | custom-call | tf_op jit(solution)/shard_map/later_pass/pallas_call | solution.py:242
  93.8 10.2 %all_to_all.49.got = f32[16,16,128]{2,1,0:T(8,128)S(1)} all-to-all(f32[16,16,128]{2,1,0:T(8,128)S(1)} %get-tuple-element.46), channel_id=1, replica_groups=mesh['x'=4,'zh'=4,'zl'=2,'y'=4,'c'=2] {'x','y'}, dimensions={0} | all-to-all | bytes 262144 | tf_op jit(solution)/shard_map/all_to_all | solution.py:254
  104.0 2.8 %later_pass.6 = (f32[16,128]{1,0:T(8,128)S(1)}, f32[16,16,128]{2,1,0:T(8,128)S(1)}) custom-call(f32[16,16,128]{2,1,0:T(8,128)S(1)} %all_to_all.49.got, f32[16,128]{1,0:T(8,128)S(1)} %get-tuple-element.45.kept.old, f32[16,128]{1,0:T(8,128)S(1)} %get-tuple-element.47.kept.old, bf16[2048,144]{1,0:T(8,128)(2,1)S(1)} %get-tuple-element.35.wide, ...), custom_call_target="tpu_custom_call" | custom-call | tf_op jit(solution)/shard_map/later_pass/pallas_call | solution.py:242
  106.8 12.6 %all_to_all.50.got = f32[16,16,128]{2,1,0:T(8,128)S(1)} all-to-all(f32[16,16,128]{2,1,0:T(8,128)S(1)} %get-tuple-element.48), channel_id=1, replica_groups=mesh['x'=4,'zh'=4,'zl'=2,'y'=4,'c'=2] {'zh','zl','c'}, dimensions={0} | all-to-all | bytes 262144 | tf_op jit(solution)/shard_map/all_to_all | solution.py:254
  119.4 2.8 %later_pass.7 = (f32[16,128]{1,0:T(8,128)S(1)}, f32[16,16,128]{2,1,0:T(8,128)S(1)}) custom-call(f32[16,16,128]{2,1,0:T(8,128)S(1)} %all_to_all.50.got, f32[16,128]{1,0:T(8,128)S(1)} %get-tuple-element.47.kept.old, f32[16,128]{1,0:T(8,128)S(1)} %get-tuple-element.49.kept.f, bf16[2048,144]{1,0:T(8,128)(2,1)S(1)} %get-tuple-element.41.wide, ...), custom_call_target="tpu_custom_call" | custom-call | tf_op jit(solution)/shard_map/later_pass/pallas_call | solution.py:242
  122.1 10.2 %all_to_all.51.got = f32[16,16,128]{2,1,0:T(8,128)S(1)} all-to-all(f32[16,16,128]{2,1,0:T(8,128)S(1)} %get-tuple-element.50), channel_id=1, replica_groups=mesh['x'=4,'zh'=4,'zl'=2,'y'=4,'c'=2] {'x','y'}, dimensions={0} | all-to-all | bytes 262144 | tf_op jit(solution)/shard_map/all_to_all | solution.py:254
  132.3 0.5 mismatch.1
  132.9 10.4 %all_to_all.52 = f32[16,1,128]{2,1,0:T(1,128)S(1)} all-to-all(f32[16,1,128]{2,1,0:T(1,128)S(1)} %get-tuple-element.54), channel_id=1, replica_groups=mesh['x'=4,'zh'=4,'zl'=2,'y'=4,'c'=2] {'zh','zl','c'}, dimensions={0} | all-to-all | bytes 16384 | tf_op jit(solution)/shard_map/all_to_all | solution.py:254
  143.3 0.6 slice_reduce_fusion
  (18 shorter events, 1.9 us)
Async XLA Ops:
  2.1 12.6 %collective-permute-start.3 = (bf16[1,80,128]{2,1,0:T(8,128)(2,1)}, bf16[1,80,128]{2,1,0:T(8,128)(2,1)S(1)}, u32[]{:S(2)}, u32[]{:S(2)}) collective-permute-start(bf16[1,80,128]{2,1,0:T(8,128)(2,1)} %get-tuple-element.30), channel_id=1, source_target_pairs={{0,192},{64,128},{128,64},{192,0},{1,193},{65,129},{129,65},{193,1... | collective-permute-start | bytes 61448 | tf_op jit(solution)/shard_map/ppermute | solution.py:285
  5.5 9.1 %collective-permute-start.2 = (bf16[1,80,128]{2,1,0:T(8,128)(2,1)}, bf16[1,80,128]{2,1,0:T(8,128)(2,1)S(1)}, u32[]{:S(2)}, u32[]{:S(2)}) collective-permute-start(bf16[1,80,128]{2,1,0:T(8,128)(2,1)} %get-tuple-element.30), channel_id=1, source_target_pairs={{0,128},{64,192},{128,0},{192,64},{1,129},{65,193},{129,1},{193,65... | collective-permute-start | bytes 61448 | tf_op jit(solution)/shard_map/ppermute | solution.py:285
  6.0 8.6 %collective-permute-start.1 = (bf16[1,80,128]{2,1,0:T(8,128)(2,1)}, bf16[1,80,128]{2,1,0:T(8,128)(2,1)S(1)}, u32[]{:S(2)}, u32[]{:S(2)}) collective-permute-start(bf16[1,80,128]{2,1,0:T(8,128)(2,1)} %get-tuple-element.30), channel_id=1, source_target_pairs={{0,64},{64,0},{128,192},{192,128},{1,65},{65,1},{129,193},{193,129... | collective-permute-start | bytes 61448 | tf_op jit(solution)/shard_map/ppermute | solution.py:285
  6.2 8.4 %copy-start = (bf16[1,80,128]{2,1,0:T(8,128)(2,1)S(1)}, bf16[1,80,128]{2,1,0:T(8,128)(2,1)}, u32[]{:S(2)}) copy-start(bf16[1,80,128]{2,1,0:T(8,128)(2,1)} %get-tuple-element.30) | copy-start | bytes 61444
  6.2 16.7 %all-to-all-start = ((bf16[8,80,128]{2,1,0:T(8,128)(2,1)}), bf16[8,80,128]{2,1,0:T(8,128)(2,1)S(1)}, u32[]{:S(2)}, u32[]{:S(2)}) async-start(bf16[8,80,128]{2,1,0:T(8,128)(2,1)} %get-tuple-element.29), calls=%async_computation | async-start | bytes 327680 | tf_op jit(solution)/shard_map/all_to_all | solution.py:254
  14.7 11.1 %collective-permute-start.6 = (bf16[4,80,128]{2,1,0:T(8,128)(2,1)S(1)}, bf16[4,80,128]{2,1,0:T(8,128)(2,1)S(1)}, u32[]{:S(2)}, u32[]{:S(2)}) collective-permute-start(bf16[4,80,128]{2,1,0:T(8,128)(2,1)S(1)} %constant_dynamic-update-slice_fusion.own), channel_id=1, source_target_pairs={{0,6},{2,4},{4,2},{6,0},{1,7},{3,5},{5,3},{7,1},{8,14},{10,12},{12... | collective-permute-start | bytes 245768 | tf_op jit(solution)/shard_map/ppermute | solution.py:285
  17.5 8.3 %collective-permute-start.5 = (bf16[4,80,128]{2,1,0:T(8,128)(2,1)S(1)}, bf16[4,80,128]{2,1,0:T(8,128)(2,1)S(1)}, u32[]{:S(2)}, u32[]{:S(2)}) collective-permute-start(bf16[4,80,128]{2,1,0:T(8,128)(2,1)S(1)} %constant_dynamic-update-slice_fusion.own), channel_id=1, source_target_pairs={{0,4},{2,6},{4,0},{6,2},{1,5},{3,7},{5,1},{7,3},{8,12},{10,14},{12... | collective-permute-start | bytes 245768 | tf_op jit(solution)/shard_map/ppermute | solution.py:285
  17.9 8.0 %collective-permute-start.4 = (bf16[4,80,128]{2,1,0:T(8,128)(2,1)S(1)}, bf16[4,80,128]{2,1,0:T(8,128)(2,1)S(1)}, u32[]{:S(2)}, u32[]{:S(2)}) collective-permute-start(bf16[4,80,128]{2,1,0:T(8,128)(2,1)S(1)} %constant_dynamic-update-slice_fusion.own), channel_id=1, source_target_pairs={{0,2},{2,0},{4,6},{6,4},{1,3},{3,1},{5,7},{7,5},{8,10},{10,8},{12,... | collective-permute-start | bytes 245768 | tf_op jit(solution)/shard_map/ppermute | solution.py:285
  22.9 3.9 %collective-permute-start = (bf16[8,80,128]{2,1,0:T(8,128)(2,1)S(1)}, bf16[8,80,128]{2,1,0:T(8,128)(2,1)S(1)}, u32[]{:S(2)}, u32[]{:S(2)}) collective-permute-start(bf16[8,80,128]{2,1,0:T(8,128)(2,1)S(1)} %all-to-all-done.own), channel_id=1, source_target_pairs={{0,1},{1,0},{2,3},{3,2},{4,5},{5,4},{6,7},{7,6},{8,9},{9,8},{10,11... | collective-permute-start | bytes 491528 | tf_op jit(solution)/shard_map/ppermute | solution.py:285

commit v4 on v3

--- a/solution.py
+++ b/solution.py
@@ -15,11 +15,8 @@
 PACK = 16
 BLOCKS = 2
 WIDTH = BLOCKS * LANES
-HEAD = 512
-MARGIN = 100.0
-REACH = 110.0
-LARGE = 2.0**120
-SMALL = 2.0**-102
+GROUPS = 64
+VMEM = 8 * 1024 * 1024
 UNIT = 1.0 / (EPS * math.log(2.0))
 AXES = ("x", "zh", "zl", "y", "c")
 SRC_GROUP = ("x", "y")
@@ -128,32 +125,45 @@
     strips(top_ref.shape[0] // BLOCKS, body, unroll)
 
 
-def sum_pass(operands, rows_ref, kept, ratio_ref, part_ref, unroll=True):
+def sum_pass(operands, rows_ref, kept, ratio_ref, part_ref, terms_ref=None, unroll=True):
     for k, piece in enumerate(pieces(kept / operands[3][...])):
         ratio_ref[k] = piece
 
     def body(s):
-        score = strip_score(s, operands[0].shape[0], operands, rows_ref, ratio_ref)
-        put(part_ref, s, jnp.sum(jnp.exp2(score), axis=0, keepdims=True))
+        terms = jnp.exp2(strip_score(s, operands[0].shape[0], operands, rows_ref, ratio_ref))
+        if terms_ref is not None:
+            terms_ref[:, strip_of(s)] = terms
+        put(part_ref, s, jnp.sum(terms, axis=0, keepdims=True))
 
     strips(part_ref.shape[0] // BLOCKS, body, unroll)
 
 
-def log_pass(operands, rows_ref, ratio_ref, part_ref, top_ref, bound=None):
+def log_pass(operands, rows_ref, ratio_ref, part_ref, top_ref, head, margin, large, terms_ref=None):
     size = operands[0].shape[0]
-    if bound is None:
-        find_tops(min(HEAD, size), operands, rows_ref, top_ref)
-        top_ref[...] = top_ref[...] + MARGIN
-    else:
-        top_ref[...] = jnp.full(top_ref.shape, bound - REACH, f32)
-    sum_pass(operands, rows_ref, -top_ref[...], ratio_ref, part_ref)
-    mass = part_ref[...]
-    sound = (mass < LARGE) & (mass > SMALL)
-
-    @pl.when(jnp.min(sound.astype(f32)) < 0.5)
+    find_tops(min(head, size), operands, rows_ref, top_ref)
+    top_ref[...] = top_ref[...] + margin
+    sum_pass(operands, rows_ref, -top_ref[...], ratio_ref, part_ref, terms_ref)
+
+    @pl.when(jnp.logical_not(jnp.max(part_ref[...]) < large))
     def _():
         find_tops(size, operands, rows_ref, top_ref, unroll=False)
-        sum_pass(operands, rows_ref, -top_ref[...], ratio_ref, part_ref, unroll=False)
+        sum_pass(operands, rows_ref, -top_ref[...], ratio_ref, part_ref, terms_ref, unroll=False)
+
+
+def product_pass(terms_ref, factor, rows_ref, part_ref):
+    spread(factor, rows_ref)
+    size = terms_ref.shape[1]
+
+    def step(g, total):
+        for q in range(GROUPS):
+            at = pl.ds(pl.multiple_of((g * GROUPS + q) * 8, 8), 8)
+            total = total + terms_ref[at, :] * jnp.concatenate([rows_ref[at, :]] * (size // LANES), axis=1)
+        return total
+
+    total = lax.fori_loop(0, terms_ref.shape[0] // (8 * GROUPS), step, jnp.zeros((8, size), f32))
+    total = jnp.sum(total, axis=0, keepdims=True)
+    for b in range(size // LANES):
+        part_ref[b : b + 1, :] = total[:, b * LANES : (b + 1) * LANES]
 
 
 def combine_logs(got_ref, shift):
@@ -162,8 +172,8 @@
     return -(top + log2(jnp.sum(jnp.exp2(got - top[None]), axis=0))) - shift
 
 
-def combine(got_ref, old, shift):
-    return old - log2(jnp.sum(got_ref[...], axis=0)) - shift
+def combine_sums(got_ref, total):
+    return 1.0 / (total * jnp.sum(got_ref[...], axis=0))
 
 
 def send(part, out_ref):
@@ -191,7 +201,7 @@
         send(jnp.concatenate([embeds[k], row], axis=0), out)
 
 
-def sources_kernel(own, far, wide, tail, raw, scale):
+def sources_kernel(own, far, _, wide, tail, raw, scale):
     x, y = lax.axis_index("x"), lax.axis_index("y")
     blocks = []
     for m in range(4):
@@ -201,41 +211,53 @@
     prepare(blocks, wide, tail, raw, scale)
 
 
-def first_kernel(own, other, s_tail, s_raw, s_scale, t_wide, t_tail, t_raw, t_scale, out, ratio, part, top):
+def targets_kernel(own, other, wide, tail, raw, scale):
     core = lax.axis_index("c")
     blocks = [(own.at[z], 2 * z + core) for z in range(own.shape[0])]
     blocks += [(other.at[z], 2 * z + 1 - core) for z in range(own.shape[0])]
-    prepare(blocks, t_wide, t_tail, t_raw, t_scale)
-    log_pass((t_wide, s_raw, s_tail, s_scale), None, ratio, part, top)
+    prepare(blocks, wide, tail, raw, scale)
+
+
+def first_kernel(wide, raw, tail, scale, out, ratio, part, top):
+    log_pass((wide, raw, tail, scale), None, ratio, part, top, 512, 100.0, 2.0**120)
     send(top[...] + log2(part[...]), out)
 
 
-def second_kernel(shift, got, wide, raw, tail, scale, new, out, rows, ratio, part, top):
+def second_kernel(shift, got, wide, raw, tail, scale, new, part, lse, terms, out, rows, ratio, top):
     new[...] = combine_logs(got, shift)
     spread(new[...], rows)
-    log_pass((wide, raw, tail, scale), rows, ratio, part, top, -shift)
-    send(top[...] + log2(part[...]), out)
-
-
-def third_kernel(shift, got, kept, wide, raw, tail, scale, new, out, rows, ratio, part):
+    log_pass((wide, raw, tail, scale), rows, ratio, part, top, 128, 30.0, 2.0**80, terms)
+    lse[...] = top[...] + log2(part[...])
+    send(lse[...], out)
+
+
+def third_kernel(shift, got, kept, lse, mass, wide, raw, tail, scale, new, terms, weight, one, out, rows, ratio, part):
     new[...] = combine_logs(got, shift)
+    weight[...] = jnp.exp2(lse[...] + new[...]) / mass[...]
+    one[...] = jnp.ones_like(one)
     spread(new[...], rows)
-    sum_pass((wide, raw, tail, scale), rows, kept[...], ratio, part)
+    sum_pass((wide, raw, tail, scale), rows, kept[...], ratio, part, terms)
     send(part[...], out)
 
 
-def later_kernel(shift, got, old, kept, wide, raw, tail, scale, new, out, rows, ratio, part):
-    new[...] = combine(got, old[...], shift)
-    spread(new[...], rows)
-    sum_pass((wide, raw, tail, scale), rows, kept[...], ratio, part)
-    send(part[...], out)
-
-
-def last_kernel(shift, got, f, g, out, own_src, own_tgt):
-    diff = (log2(jnp.sum(got[...], axis=0)) + shift) * math.log(2.0)
+def product_kernel(total, got, terms, weight, out, rows, part, factor):
+    factor[...] = combine_sums(got, total)
+    product_pass(terms, factor[...], rows, part)
+    send(part[...] * weight[...], out)
+
+
+def last_product_kernel(total, got, terms, weight, factor, out, rows, part):
+    product_kernel(total, got, terms, weight, out, rows, part, factor)
+
+
+def last_kernel(shift, got, f, g, f_factor, g_factor, out, own_src, own_tgt):
+    f_change = log2(f_factor[...])
+    diff = (f_change + log2(jnp.sum(got[...], axis=0)) + shift) * math.log(2.0)
     out[...] = jnp.full(out.shape, jnp.sum(diff * diff), f32)
-    own_src[...] = f[pl.ds(lax.axis_index(SRC_GROUP), 1), :] * (1.0 / UNIT)
-    own_tgt[...] = g[pl.ds(lax.axis_index(TGT_GROUP), 1), :] * (1.0 / UNIT)
+    at = pl.ds(lax.axis_index(SRC_GROUP), 1)
+    own_src[...] = (f[at, :] + log2(f_factor[at, :])) * (1.0 / UNIT)
+    at = pl.ds(lax.axis_index(TGT_GROUP), 1)
+    own_tgt[...] = (g[at, :] + log2(g_factor[at, :])) * (1.0 / UNIT)
 
 
 def call(kernel, args, outs, scratch, name):
@@ -245,7 +267,7 @@
         in_specs=[pl.BlockSpec(memory_space=pltpu.VMEM)] * len(args),
         out_specs=[pl.BlockSpec(memory_space=pltpu.VMEM)] * len(outs),
         scratch_shapes=scratch,
-        compiler_params=pltpu.CompilerParams(vmem_limit_bytes=48 * 1024 * 1024),
+        compiler_params=pltpu.CompilerParams(vmem_limit_bytes=VMEM),
         name=name,
     )(*args)
 
@@ -267,8 +289,8 @@
     src_sent, tgt_sent = pl.pallas_call(
         pack_kernel,
         out_shape=[
-            jax.ShapeDtypeStruct((1,) + cells, bf16),
-            jax.ShapeDtypeStruct((z_count,) + cells, bf16),
+            pltpu.VMEM((1,) + cells, bf16),
+            pltpu.VMEM((z_count,) + cells, bf16),
         ],
         in_specs=[pl.BlockSpec(memory_space=pl.ANY)] * 4,
         out_specs=[pl.BlockSpec(memory_space=pltpu.VMEM)] * 2,
@@ -301,13 +323,16 @@
     row_ratio = pltpu.VMEM((3,) + src_rows, f32)
     col_ratio = pltpu.VMEM((3,) + tgt_rows, f32)
 
+    t_wide, t_tail, t_raw, t_scale = call(
+        targets_kernel, [tgt, tgt_other], operands(tgt_size, tgt_rows), [], "targets"
+    )
     s_wide, s_tail, s_raw, s_scale = call(
-        sources_kernel, [src, src_far], operands(src_size, src_rows), [], "sources"
-    )
-    t_wide, t_tail, t_raw, t_scale, sent = call(
+        sources_kernel, [src, src_far, t_scale], operands(src_size, src_rows), [], "sources"
+    )
+    (sent,) = call(
         first_kernel,
-        [tgt, tgt_other, s_tail, s_raw, s_scale],
-        operands(tgt_size, tgt_rows) + [row_out],
+        [t_wide, s_raw, s_tail, s_scale],
+        [row_out],
         [row_ratio, row_part, row_part],
         "row_pass_1",
     )
@@ -317,42 +342,39 @@
     keep_tgt = [t_raw, t_tail, t_scale]
     keep_src = [s_raw, s_tail, s_scale]
 
-    f, sent = call(
+    f, part, lse, terms, sent = call(
         functools.partial(second_kernel, shift),
         [got, s_wide] + keep_tgt,
-        [(src_rows, f32), col_out],
-        [src_spread, col_ratio, col_part, col_part],
+        [(src_rows, f32), (tgt_rows, f32), (tgt_rows, f32), ((src_size, tgt_size), f32), col_out],
+        [src_spread, col_ratio, col_part],
         "col_pass_1",
     )
     got = exchange(sent, TGT_GROUP)
-    g, sent = call(
+    g, mate, weight, one, sent = call(
         functools.partial(third_kernel, shift),
-        [got, f, t_wide] + keep_src,
-        [(tgt_rows, f32), row_out],
+        [got, f, lse, part, t_wide] + keep_src,
+        [(tgt_rows, f32), ((tgt_size, src_size), f32), (tgt_rows, f32), (src_rows, f32), row_out],
         [tgt_spread, row_ratio, row_part],
         "row_pass_2",
     )
+    def product(got, terms, weight, rows, out, spread_rows, part, last):
+        args, kept = [got, terms, weight], (rows, f32)
+        if not last:
+            kernel = functools.partial(product_kernel, float(total))
+            return None, call(kernel, args, [out], [spread_rows, part, pltpu.VMEM(*kept)], "product")[0]
+        kernel = functools.partial(last_product_kernel, float(total))
+        return call(kernel, args, [kept, out], [spread_rows, part], "last_product")
+
     for step in range(2, ITERS + 1):
+        last = step == ITERS
         got = exchange(sent, SRC_GROUP)
-        f, sent = call(
-            functools.partial(later_kernel, shift),
-            [got, f, g, s_wide] + keep_tgt,
-            [(src_rows, f32), col_out],
-            [src_spread, col_ratio, col_part],
-            "later_pass",
-        )
+        f_factor, sent = product(got, terms, weight, src_rows, col_out, src_spread, col_part, last)
         got = exchange(sent, TGT_GROUP)
-        g, sent = call(
-            functools.partial(later_kernel, shift),
-            [got, g, f, t_wide] + keep_src,
-            [(tgt_rows, f32), row_out],
-            [tgt_spread, row_ratio, row_part],
-            "later_pass",
-        )
+        g_factor, sent = product(got, mate, one, tgt_rows, row_out, tgt_spread, row_part, last)
     got = exchange(sent, SRC_GROUP)
     sent, own_src, own_tgt = call(
         functools.partial(last_kernel, shift),
-        [got, f, g],
+        [got, f, g, f_factor, g_factor],
         [((tgt_count, 1, LANES), f32), ((1, per_dev), f32), ((1, per_dev), f32)],
         [],
         "mismatch",

time: 146 us -> 147 us (level)
  blocking collectives: 95.2 us -> 100 us
  Pallas kernels: 23.2 us -> 18.7 us
    all_to_all x8, blocking collectives: 95.2 us -> 100 us  [exchange(): return lax.all_to_all(sent, group, 0, 0)]
    pallas_call x9 -> x10, Pallas kernels: 21.7 us -> 17.2 us  [call(): pl.pallas_call(kernel, out_shape=[jax.ShapeDtypeStruct(shape, dtype) for...]
where the time goes in v4:
time: 147 us
  blocking collectives  100 us (68%)
  starting transfers between devices  18.8 us (13%)
  Pallas kernels  18.7 us (13%)
  waiting for transfers between devices  5.73 us (4%)
  between operations  2.57 us (2%)
    all_to_all x8, blocking collectives, exchange(): return lax.all_to_all(sent, group, 0, 0)  100 us
    pallas_call x10, Pallas kernels, call(): pl.pallas_call(kernel, out_shape=[jax.ShapeDtypeStruct(shape, dtype) for...  17.2 us
    ppermute x7, starting transfers between devices, neighbours(): lax.ppermute(array, axis, [(i, i ^ k) for i in range(size)])  10.5 us
    all_to_all x1, starting transfers between devices, exchange(): return lax.all_to_all(sent, group, 0, 0)  8.28 us
    all_to_all x1, waiting for transfers between devices, exchange(): return lax.all_to_all(sent, group, 0, 0)  4.74 us
  transfers between devices with their start and end apart: 8, of which 2 were waited for; matrix products, arithmetic and copies ran while one was open for 0% of the time, Pallas kernels for 0%

profile of v4, /device:TPU:1, one launch (start us, length us, event | category | flops | bytes accessed | tf_op | source)
XLA Modules:
  0.0 146.7 jit_solution(12979498186441897205)
XLA Ops:
  0.6 1.5 pack.1
  2.1 3.4 %collective-permute-start.3 = (bf16[1,80,128]{2,1,0:T(8,128)(2,1)S(1)}, bf16[1,80,128]{2,1,0:T(8,128)(2,1)S(1)}, u32[]{:S(2)}, u32[]{:S(2)}) collective-permute-start(bf16[1,80,128]{2,1,0:T(8,128)(2,1)S(1)} %get-tuple-element.32), channel_id=1, source_target_pairs={{0,192},{64,128},{128,64},{192,0},{1,193},{65,129},{129,65},{193,1... | collective-permute-start | bytes 61448 | tf_op jit(solution)/shard_map/ppermute | solution.py:307
  6.2 8.3 %all-to-all-start = ((bf16[8,80,128]{2,1,0:T(8,128)(2,1)}), bf16[8,80,128]{2,1,0:T(8,128)(2,1)S(1)}, u32[]{:S(2)}, u32[]{:S(2)}) async-start(bf16[8,80,128]{2,1,0:T(8,128)(2,1)} %get-tuple-element.30), calls=%async_computation | async-start | bytes 327680 | tf_op jit(solution)/shard_map/all_to_all | solution.py:276
  14.5 2.8 %collective-permute-start.6 = (bf16[4,80,128]{2,1,0:T(8,128)(2,1)S(1)}, bf16[4,80,128]{2,1,0:T(8,128)(2,1)S(1)}, u32[]{:S(2)}, u32[]{:S(2)}) collective-permute-start(bf16[4,80,128]{2,1,0:T(8,128)(2,1)S(1)} %constant_dynamic-update-slice_fusion.own), channel_id=1, source_target_pairs={{0,6},{2,4},{4,2},{6,0},{1,7},{3,5},{5,3},{7,1},{8,14},{10,12},{12... | collective-permute-start | bytes 245768 | tf_op jit(solution)/shard_map/ppermute | solution.py:307
  18.0 4.7 %all-to-all-done.own = bf16[8,80,128]{2,1,0:T(8,128)(2,1)S(1)} async-done(((bf16[8,80,128]{2,1,0:T(8,128)(2,1)}), bf16[8,80,128]{2,1,0:T(8,128)(2,1)S(1)}, u32[]{:S(2)}, u32[]{:S(2)}) %all-to-all-start) | async-done | bytes 163872 | tf_op jit(solution)/shard_map/all_to_all | solution.py:276
  22.8 2.9 %collective-permute-start = (bf16[8,80,128]{2,1,0:T(8,128)(2,1)S(1)}, bf16[8,80,128]{2,1,0:T(8,128)(2,1)S(1)}, u32[]{:S(2)}, u32[]{:S(2)}) collective-permute-start(bf16[8,80,128]{2,1,0:T(8,128)(2,1)S(1)} %all-to-all-done.own), channel_id=1, source_target_pairs={{0,1},{1,0},{2,3},{3,2},{4,5},{5,4},{6,7},{7,6},{8,9},{9,8},{10,11... | collective-permute-start | bytes 491528 | tf_op jit(solution)/shard_map/ppermute | solution.py:307
  25.7 1.0 collective-permute-done.other
  27.7 3.2 %row_pass_1.1 = f32[16,16,128]{2,1,0:T(8,128)S(1)} custom-call(bf16[2048,144]{1,0:T(8,128)(2,1)S(1)} %get-tuple-element.31.wide, bf16[64,2048]{1,0:T(8,128)(2,1)S(1)} %get-tuple-element.34.raw, f32[16,2048]{1,0:T(8,128)S(1)} %get-tuple-element.35.tail, f32[16,128]{1,0:T(8,128)S(1)} %get-tuple-element.36.scale), custom_call_target="tpu_custom_call" | custom-call | tf_op jit(solution)/shard_map/row_pass_1/pallas_call | solution.py:264
  30.9 13.2 %all_to_all.45.got = f32[16,16,128]{2,1,0:T(8,128)S(1)} all-to-all(f32[16,16,128]{2,1,0:T(8,128)S(1)} %row_pass_1.1), channel_id=1, replica_groups=mesh['x'=4,'zh'=4,'zl'=2,'y'=4,'c'=2] {'x','y'}, dimensions={0} | all-to-all | bytes 262144 | tf_op jit(solution)/shard_map/all_to_all | solution.py:276
  44.1 2.9 %col_pass_1.1 = (f32[16,128]{1,0:T(8,128)S(1)}, f32[16,128]{1,0:T(8,128)S(1)}, f32[16,128]{1,0:T(8,128)S(1)}, f32[2048,2048]{1,0:T(8,128)S(1)}, f32[16,16,128]{2,1,0:T(8,128)S(1)}) custom-call(f32[16,16,128]{2,1,0:T(8,128)S(1)} %all_to_all.45.got, bf16[2048,144]{1,0:T(8,128)(2,1)S(1)} %get-tuple-element.37.wide, bf16[64,2048]{1,0:T(8,128)(2,1)S(1)} %get-tuple-element.38.raw, ...), custom_call_target="tpu_custom_call" | custom-call | tf_op jit(solution)/shard_map/col_pass_1/pallas_call | solution.py:264
  47.0 15.2 %all_to_all.46.got = f32[16,16,128]{2,1,0:T(8,128)S(1)} all-to-all(f32[16,16,128]{2,1,0:T(8,128)S(1)} %get-tuple-element.40), channel_id=1, replica_groups=mesh['x'=4,'zh'=4,'zl'=2,'y'=4,'c'=2] {'zh','zl','c'}, dimensions={0} | all-to-all | bytes 262144 | tf_op jit(solution)/shard_map/all_to_all | solution.py:276
  62.2 2.9 %row_pass_2.1 = (f32[16,128]{1,0:T(8,128)S(1)}, f32[2048,2048]{1,0:T(8,128)S(1)}, f32[16,128]{1,0:T(8,128)S(1)}, f32[16,128]{1,0:T(8,128)S(1)}, f32[16,16,128]{2,1,0:T(8,128)S(1)}) custom-call(f32[16,16,128]{2,1,0:T(8,128)S(1)} %all_to_all.46.got, f32[16,128]{1,0:T(8,128)S(1)} %get-tuple-element.41.kept.f, f32[16,128]{1,0:T(8,128)S(1)} %get-tuple-element.42.lse, ...), custom_call_target="tpu_custom_call" | custom-call | tf_op jit(solution)/shard_map/row_pass_2/pallas_call | solution.py:264
  65.0 15.7 %all_to_all.47.got = f32[16,16,128]{2,1,0:T(8,128)S(1)} all-to-all(f32[16,16,128]{2,1,0:T(8,128)S(1)} %get-tuple-element.44), channel_id=1, replica_groups=mesh['x'=4,'zh'=4,'zl'=2,'y'=4,'c'=2] {'x','y'}, dimensions={0} | all-to-all | bytes 262144 | tf_op jit(solution)/shard_map/all_to_all | solution.py:276
  80.8 1.7 %product.2 = f32[16,16,128]{2,1,0:T(8,128)S(1)} custom-call(f32[16,16,128]{2,1,0:T(8,128)S(1)} %all_to_all.47.got, f32[2048,2048]{1,0:T(8,128)S(1)} %get-tuple-element.45.terms, f32[16,128]{1,0:T(8,128)S(1)} %get-tuple-element.46.weight), custom_call_target="tpu_custom_call" | custom-call | tf_op jit(solution)/shard_map/product/pallas_call | solution.py:264
  82.5 12.6 %all_to_all.48.got = f32[16,16,128]{2,1,0:T(8,128)S(1)} all-to-all(f32[16,16,128]{2,1,0:T(8,128)S(1)} %product.2), channel_id=1, replica_groups=mesh['x'=4,'zh'=4,'zl'=2,'y'=4,'c'=2] {'zh','zl','c'}, dimensions={0} | all-to-all | bytes 262144 | tf_op jit(solution)/shard_map/all_to_all | solution.py:276
  95.1 1.7 %product.3 = f32[16,16,128]{2,1,0:T(8,128)S(1)} custom-call(f32[16,16,128]{2,1,0:T(8,128)S(1)} %all_to_all.48.got, f32[2048,2048]{1,0:T(8,128)S(1)} %get-tuple-element.47.terms, f32[16,128]{1,0:T(8,128)S(1)} %get-tuple-element.48.weight), custom_call_target="tpu_custom_call" | custom-call | tf_op jit(solution)/shard_map/product/pallas_call | solution.py:264
  96.8 10.2 %all_to_all.49.got = f32[16,16,128]{2,1,0:T(8,128)S(1)} all-to-all(f32[16,16,128]{2,1,0:T(8,128)S(1)} %product.3), channel_id=1, replica_groups=mesh['x'=4,'zh'=4,'zl'=2,'y'=4,'c'=2] {'x','y'}, dimensions={0} | all-to-all | bytes 262144 | tf_op jit(solution)/shard_map/all_to_all | solution.py:276
  107.0 1.7 %last_product.2 = (f32[16,128]{1,0:T(8,128)S(1)}, f32[16,16,128]{2,1,0:T(8,128)S(1)}) custom-call(f32[16,16,128]{2,1,0:T(8,128)S(1)} %all_to_all.49.got, f32[2048,2048]{1,0:T(8,128)S(1)} %get-tuple-element.45.terms, f32[16,128]{1,0:T(8,128)S(1)} %get-tuple-element.46.weight), custom_call_target="tpu_custom_call" | custom-call | tf_op jit(solution)/shard_map/last_product/pallas_call | solution.py:264
  108.7 12.6 %all_to_all.50.got = f32[16,16,128]{2,1,0:T(8,128)S(1)} all-to-all(f32[16,16,128]{2,1,0:T(8,128)S(1)} %get-tuple-element.49), channel_id=1, replica_groups=mesh['x'=4,'zh'=4,'zl'=2,'y'=4,'c'=2] {'zh','zl','c'}, dimensions={0} | all-to-all | bytes 262144 | tf_op jit(solution)/shard_map/all_to_all | solution.py:276
  121.3 1.7 %last_product.3 = (f32[16,128]{1,0:T(8,128)S(1)}, f32[16,16,128]{2,1,0:T(8,128)S(1)}) custom-call(f32[16,16,128]{2,1,0:T(8,128)S(1)} %all_to_all.50.got, f32[2048,2048]{1,0:T(8,128)S(1)} %get-tuple-element.47.terms, f32[16,128]{1,0:T(8,128)S(1)} %get-tuple-element.48.weight), custom_call_target="tpu_custom_call" | custom-call | tf_op jit(solution)/shard_map/last_product/pallas_call | solution.py:264
  123.0 10.2 %all_to_all.51.got = f32[16,16,128]{2,1,0:T(8,128)S(1)} all-to-all(f32[16,16,128]{2,1,0:T(8,128)S(1)} %get-tuple-element.50), channel_id=1, replica_groups=mesh['x'=4,'zh'=4,'zl'=2,'y'=4,'c'=2] {'x','y'}, dimensions={0} | all-to-all | bytes 262144 | tf_op jit(solution)/shard_map/all_to_all | solution.py:276
  133.2 0.6 mismatch.1
  133.8 10.5 %all_to_all.52 = f32[16,1,128]{2,1,0:T(1,128)S(1)} all-to-all(f32[16,1,128]{2,1,0:T(1,128)S(1)} %get-tuple-element.56), channel_id=1, replica_groups=mesh['x'=4,'zh'=4,'zl'=2,'y'=4,'c'=2] {'zh','zl','c'}, dimensions={0} | all-to-all | bytes 16384 | tf_op jit(solution)/shard_map/all_to_all | solution.py:276
  144.2 0.6 slice_reduce_fusion
  (17 shorter events, 2.4 us)
Async XLA Ops:
  2.1 12.4 %collective-permute-start.3 = (bf16[1,80,128]{2,1,0:T(8,128)(2,1)S(1)}, bf16[1,80,128]{2,1,0:T(8,128)(2,1)S(1)}, u32[]{:S(2)}, u32[]{:S(2)}) collective-permute-start(bf16[1,80,128]{2,1,0:T(8,128)(2,1)S(1)} %get-tuple-element.32), channel_id=1, source_target_pairs={{0,192},{64,128},{128,64},{192,0},{1,193},{65,129},{129,65},{193,1... | collective-permute-start | bytes 61448 | tf_op jit(solution)/shard_map/ppermute | solution.py:307
  5.5 9.0 %collective-permute-start.2 = (bf16[1,80,128]{2,1,0:T(8,128)(2,1)S(1)}, bf16[1,80,128]{2,1,0:T(8,128)(2,1)S(1)}, u32[]{:S(2)}, u32[]{:S(2)}) collective-permute-start(bf16[1,80,128]{2,1,0:T(8,128)(2,1)S(1)} %get-tuple-element.32), channel_id=1, source_target_pairs={{0,128},{64,192},{128,0},{192,64},{1,129},{65,193},{129,1},{193,65... | collective-permute-start | bytes 61448 | tf_op jit(solution)/shard_map/ppermute | solution.py:307
  6.0 8.5 %collective-permute-start.1 = (bf16[1,80,128]{2,1,0:T(8,128)(2,1)S(1)}, bf16[1,80,128]{2,1,0:T(8,128)(2,1)S(1)}, u32[]{:S(2)}, u32[]{:S(2)}) collective-permute-start(bf16[1,80,128]{2,1,0:T(8,128)(2,1)S(1)} %get-tuple-element.32), channel_id=1, source_target_pairs={{0,64},{64,0},{128,192},{192,128},{1,65},{65,1},{129,193},{193,129... | collective-permute-start | bytes 61448 | tf_op jit(solution)/shard_map/ppermute | solution.py:307
  6.2 16.6 %all-to-all-start = ((bf16[8,80,128]{2,1,0:T(8,128)(2,1)}), bf16[8,80,128]{2,1,0:T(8,128)(2,1)S(1)}, u32[]{:S(2)}, u32[]{:S(2)}) async-start(bf16[8,80,128]{2,1,0:T(8,128)(2,1)} %get-tuple-element.30), calls=%async_computation | async-start | bytes 327680 | tf_op jit(solution)/shard_map/all_to_all | solution.py:276
  14.5 11.1 %collective-permute-start.6 = (bf16[4,80,128]{2,1,0:T(8,128)(2,1)S(1)}, bf16[4,80,128]{2,1,0:T(8,128)(2,1)S(1)}, u32[]{:S(2)}, u32[]{:S(2)}) collective-permute-start(bf16[4,80,128]{2,1,0:T(8,128)(2,1)S(1)} %constant_dynamic-update-slice_fusion.own), channel_id=1, source_target_pairs={{0,6},{2,4},{4,2},{6,0},{1,7},{3,5},{5,3},{7,1},{8,14},{10,12},{12... | collective-permute-start | bytes 245768 | tf_op jit(solution)/shard_map/ppermute | solution.py:307
  17.4 8.3 %collective-permute-start.5 = (bf16[4,80,128]{2,1,0:T(8,128)(2,1)S(1)}, bf16[4,80,128]{2,1,0:T(8,128)(2,1)S(1)}, u32[]{:S(2)}, u32[]{:S(2)}) collective-permute-start(bf16[4,80,128]{2,1,0:T(8,128)(2,1)S(1)} %constant_dynamic-update-slice_fusion.own), channel_id=1, source_target_pairs={{0,4},{2,6},{4,0},{6,2},{1,5},{3,7},{5,1},{7,3},{8,12},{10,14},{12... | collective-permute-start | bytes 245768 | tf_op jit(solution)/shard_map/ppermute | solution.py:307
  17.7 8.0 %collective-permute-start.4 = (bf16[4,80,128]{2,1,0:T(8,128)(2,1)S(1)}, bf16[4,80,128]{2,1,0:T(8,128)(2,1)S(1)}, u32[]{:S(2)}, u32[]{:S(2)}) collective-permute-start(bf16[4,80,128]{2,1,0:T(8,128)(2,1)S(1)} %constant_dynamic-update-slice_fusion.own), channel_id=1, source_target_pairs={{0,2},{2,0},{4,6},{6,4},{1,3},{3,1},{5,7},{7,5},{8,10},{10,8},{12,... | collective-permute-start | bytes 245768 | tf_op jit(solution)/shard_map/ppermute | solution.py:307
  22.8 3.9 %collective-permute-start = (bf16[8,80,128]{2,1,0:T(8,128)(2,1)S(1)}, bf16[8,80,128]{2,1,0:T(8,128)(2,1)S(1)}, u32[]{:S(2)}, u32[]{:S(2)}) collective-permute-start(bf16[8,80,128]{2,1,0:T(8,128)(2,1)S(1)} %all-to-all-done.own), channel_id=1, source_target_pairs={{0,1},{1,0},{2,3},{3,2},{4,5},{5,4},{6,7},{7,6},{8,9},{9,8},{10,11... | collective-permute-start | bytes 491528 | tf_op jit(solution)/shard_map/ppermute | solution.py:307

commit v5 on v4

--- a/solution.py
+++ b/solution.py
@@ -250,9 +250,8 @@
     product_kernel(total, got, terms, weight, out, rows, part, factor)
 
 
-def last_kernel(shift, got, f, g, f_factor, g_factor, out, own_src, own_tgt):
-    f_change = log2(f_factor[...])
-    diff = (f_change + log2(jnp.sum(got[...], axis=0)) + shift) * math.log(2.0)
+def last_kernel(total, got, f, g, f_factor, g_factor, out, own_src, own_tgt):
+    diff = jnp.log(f_factor[...] * (total * jnp.sum(got[...], axis=0)))
     out[...] = jnp.full(out.shape, jnp.sum(diff * diff), f32)
     at = pl.ds(lax.axis_index(SRC_GROUP), 1)
     own_src[...] = (f[at, :] + log2(f_factor[at, :])) * (1.0 / UNIT)
@@ -373,7 +372,7 @@
         g_factor, sent = product(got, mate, one, tgt_rows, row_out, tgt_spread, row_part, last)
     got = exchange(sent, SRC_GROUP)
     sent, own_src, own_tgt = call(
-        functools.partial(last_kernel, shift),
+        functools.partial(last_kernel, float(total)),
         [got, f, g, f_factor, g_factor],
         [((tgt_count, 1, LANES), f32), ((1, per_dev), f32), ((1, per_dev), f32)],
         [],

time: 147 us -> 147 us (level)
  no operation moved by 1% of the time
where the time goes in v5:
time: 147 us
  blocking collectives  100 us (68%)
  starting transfers between devices  18.8 us (13%)
  Pallas kernels  18.7 us (13%)
  waiting for transfers between devices  5.73 us (4%)
  between operations  2.57 us (2%)
    all_to_all x8, blocking collectives, exchange(): return lax.all_to_all(sent, group, 0, 0)  100 us
    pallas_call x10, Pallas kernels, call(): pl.pallas_call(kernel, out_shape=[jax.ShapeDtypeStruct(shape, dtype) for...  17.2 us
    ppermute x7, starting transfers between devices, neighbours(): lax.ppermute(array, axis, [(i, i ^ k) for i in range(size)])  10.5 us
    all_to_all x1, starting transfers between devices, exchange(): return lax.all_to_all(sent, group, 0, 0)  8.28 us
    all_to_all x1, waiting for transfers between devices, exchange(): return lax.all_to_all(sent, group, 0, 0)  4.74 us
  transfers between devices with their start and end apart: 8, of which 2 were waited for; matrix products, arithmetic and copies ran while one was open for 0% of the time, Pallas kernels for 0%

profile of v5, /device:TPU:1, one launch (start us, length us, event | category | flops | bytes accessed | tf_op | source)
XLA Modules:
  0.0 146.7 jit_solution(5121955421049268407)
XLA Ops:
  0.6 1.5 pack.1
  2.1 3.4 %collective-permute-start.3 = (bf16[1,80,128]{2,1,0:T(8,128)(2,1)S(1)}, bf16[1,80,128]{2,1,0:T(8,128)(2,1)S(1)}, u32[]{:S(2)}, u32[]{:S(2)}) collective-permute-start(bf16[1,80,128]{2,1,0:T(8,128)(2,1)S(1)} %get-tuple-element.32), channel_id=1, source_target_pairs={{0,192},{64,128},{128,64},{192,0},{1,193},{65,129},{129,65},{193,1... | collective-permute-start | bytes 61448 | tf_op jit(solution)/shard_map/ppermute | solution.py:306
  6.2 8.3 %all-to-all-start = ((bf16[8,80,128]{2,1,0:T(8,128)(2,1)}), bf16[8,80,128]{2,1,0:T(8,128)(2,1)S(1)}, u32[]{:S(2)}, u32[]{:S(2)}) async-start(bf16[8,80,128]{2,1,0:T(8,128)(2,1)} %get-tuple-element.30), calls=%async_computation | async-start | bytes 327680 | tf_op jit(solution)/shard_map/all_to_all | solution.py:275
  14.5 2.8 %collective-permute-start.6 = (bf16[4,80,128]{2,1,0:T(8,128)(2,1)S(1)}, bf16[4,80,128]{2,1,0:T(8,128)(2,1)S(1)}, u32[]{:S(2)}, u32[]{:S(2)}) collective-permute-start(bf16[4,80,128]{2,1,0:T(8,128)(2,1)S(1)} %constant_dynamic-update-slice_fusion.own), channel_id=1, source_target_pairs={{0,6},{2,4},{4,2},{6,0},{1,7},{3,5},{5,3},{7,1},{8,14},{10,12},{12... | collective-permute-start | bytes 245768 | tf_op jit(solution)/shard_map/ppermute | solution.py:306
  18.0 4.7 %all-to-all-done.own = bf16[8,80,128]{2,1,0:T(8,128)(2,1)S(1)} async-done(((bf16[8,80,128]{2,1,0:T(8,128)(2,1)}), bf16[8,80,128]{2,1,0:T(8,128)(2,1)S(1)}, u32[]{:S(2)}, u32[]{:S(2)}) %all-to-all-start) | async-done | bytes 163872 | tf_op jit(solution)/shard_map/all_to_all | solution.py:275
  22.8 2.9 %collective-permute-start = (bf16[8,80,128]{2,1,0:T(8,128)(2,1)S(1)}, bf16[8,80,128]{2,1,0:T(8,128)(2,1)S(1)}, u32[]{:S(2)}, u32[]{:S(2)}) collective-permute-start(bf16[8,80,128]{2,1,0:T(8,128)(2,1)S(1)} %all-to-all-done.own), channel_id=1, source_target_pairs={{0,1},{1,0},{2,3},{3,2},{4,5},{5,4},{6,7},{7,6},{8,9},{9,8},{10,11... | collective-permute-start | bytes 491528 | tf_op jit(solution)/shard_map/ppermute | solution.py:306
  25.7 1.0 collective-permute-done.other
  27.7 3.2 %row_pass_1.1 = f32[16,16,128]{2,1,0:T(8,128)S(1)} custom-call(bf16[2048,144]{1,0:T(8,128)(2,1)S(1)} %get-tuple-element.31.wide, bf16[64,2048]{1,0:T(8,128)(2,1)S(1)} %get-tuple-element.34.raw, f32[16,2048]{1,0:T(8,128)S(1)} %get-tuple-element.35.tail, f32[16,128]{1,0:T(8,128)S(1)} %get-tuple-element.36.scale), custom_call_target="tpu_custom_call" | custom-call | tf_op jit(solution)/shard_map/row_pass_1/pallas_call | solution.py:263
  30.9 13.2 %all_to_all.45.got = f32[16,16,128]{2,1,0:T(8,128)S(1)} all-to-all(f32[16,16,128]{2,1,0:T(8,128)S(1)} %row_pass_1.1), channel_id=1, replica_groups=mesh['x'=4,'zh'=4,'zl'=2,'y'=4,'c'=2] {'x','y'}, dimensions={0} | all-to-all | bytes 262144 | tf_op jit(solution)/shard_map/all_to_all | solution.py:275
  44.1 2.9 %col_pass_1.1 = (f32[16,128]{1,0:T(8,128)S(1)}, f32[16,128]{1,0:T(8,128)S(1)}, f32[16,128]{1,0:T(8,128)S(1)}, f32[2048,2048]{1,0:T(8,128)S(1)}, f32[16,16,128]{2,1,0:T(8,128)S(1)}) custom-call(f32[16,16,128]{2,1,0:T(8,128)S(1)} %all_to_all.45.got, bf16[2048,144]{1,0:T(8,128)(2,1)S(1)} %get-tuple-element.37.wide, bf16[64,2048]{1,0:T(8,128)(2,1)S(1)} %get-tuple-element.38.raw, ...), custom_call_target="tpu_custom_call" | custom-call | tf_op jit(solution)/shard_map/col_pass_1/pallas_call | solution.py:263
  47.0 15.2 %all_to_all.46.got = f32[16,16,128]{2,1,0:T(8,128)S(1)} all-to-all(f32[16,16,128]{2,1,0:T(8,128)S(1)} %get-tuple-element.40), channel_id=1, replica_groups=mesh['x'=4,'zh'=4,'zl'=2,'y'=4,'c'=2] {'zh','zl','c'}, dimensions={0} | all-to-all | bytes 262144 | tf_op jit(solution)/shard_map/all_to_all | solution.py:275
  62.2 2.9 %row_pass_2.1 = (f32[16,128]{1,0:T(8,128)S(1)}, f32[2048,2048]{1,0:T(8,128)S(1)}, f32[16,128]{1,0:T(8,128)S(1)}, f32[16,128]{1,0:T(8,128)S(1)}, f32[16,16,128]{2,1,0:T(8,128)S(1)}) custom-call(f32[16,16,128]{2,1,0:T(8,128)S(1)} %all_to_all.46.got, f32[16,128]{1,0:T(8,128)S(1)} %get-tuple-element.41.kept.f, f32[16,128]{1,0:T(8,128)S(1)} %get-tuple-element.42.lse, ...), custom_call_target="tpu_custom_call" | custom-call | tf_op jit(solution)/shard_map/row_pass_2/pallas_call | solution.py:263
  65.0 15.7 %all_to_all.47.got = f32[16,16,128]{2,1,0:T(8,128)S(1)} all-to-all(f32[16,16,128]{2,1,0:T(8,128)S(1)} %get-tuple-element.44), channel_id=1, replica_groups=mesh['x'=4,'zh'=4,'zl'=2,'y'=4,'c'=2] {'x','y'}, dimensions={0} | all-to-all | bytes 262144 | tf_op jit(solution)/shard_map/all_to_all | solution.py:275
  80.8 1.7 %product.2 = f32[16,16,128]{2,1,0:T(8,128)S(1)} custom-call(f32[16,16,128]{2,1,0:T(8,128)S(1)} %all_to_all.47.got, f32[2048,2048]{1,0:T(8,128)S(1)} %get-tuple-element.45.terms, f32[16,128]{1,0:T(8,128)S(1)} %get-tuple-element.46.weight), custom_call_target="tpu_custom_call" | custom-call | tf_op jit(solution)/shard_map/product/pallas_call | solution.py:263
  82.5 12.6 %all_to_all.48.got = f32[16,16,128]{2,1,0:T(8,128)S(1)} all-to-all(f32[16,16,128]{2,1,0:T(8,128)S(1)} %product.2), channel_id=1, replica_groups=mesh['x'=4,'zh'=4,'zl'=2,'y'=4,'c'=2] {'zh','zl','c'}, dimensions={0} | all-to-all | bytes 262144 | tf_op jit(solution)/shard_map/all_to_all | solution.py:275
  95.1 1.7 %product.3 = f32[16,16,128]{2,1,0:T(8,128)S(1)} custom-call(f32[16,16,128]{2,1,0:T(8,128)S(1)} %all_to_all.48.got, f32[2048,2048]{1,0:T(8,128)S(1)} %get-tuple-element.47.terms, f32[16,128]{1,0:T(8,128)S(1)} %get-tuple-element.48.weight), custom_call_target="tpu_custom_call" | custom-call | tf_op jit(solution)/shard_map/product/pallas_call | solution.py:263
  96.8 10.2 %all_to_all.49.got = f32[16,16,128]{2,1,0:T(8,128)S(1)} all-to-all(f32[16,16,128]{2,1,0:T(8,128)S(1)} %product.3), channel_id=1, replica_groups=mesh['x'=4,'zh'=4,'zl'=2,'y'=4,'c'=2] {'x','y'}, dimensions={0} | all-to-all | bytes 262144 | tf_op jit(solution)/shard_map/all_to_all | solution.py:275
  107.0 1.7 %last_product.2 = (f32[16,128]{1,0:T(8,128)S(1)}, f32[16,16,128]{2,1,0:T(8,128)S(1)}) custom-call(f32[16,16,128]{2,1,0:T(8,128)S(1)} %all_to_all.49.got, f32[2048,2048]{1,0:T(8,128)S(1)} %get-tuple-element.45.terms, f32[16,128]{1,0:T(8,128)S(1)} %get-tuple-element.46.weight), custom_call_target="tpu_custom_call" | custom-call | tf_op jit(solution)/shard_map/last_product/pallas_call | solution.py:263
  108.7 12.6 %all_to_all.50.got = f32[16,16,128]{2,1,0:T(8,128)S(1)} all-to-all(f32[16,16,128]{2,1,0:T(8,128)S(1)} %get-tuple-element.49), channel_id=1, replica_groups=mesh['x'=4,'zh'=4,'zl'=2,'y'=4,'c'=2] {'zh','zl','c'}, dimensions={0} | all-to-all | bytes 262144 | tf_op jit(solution)/shard_map/all_to_all | solution.py:275
  121.3 1.7 %last_product.3 = (f32[16,128]{1,0:T(8,128)S(1)}, f32[16,16,128]{2,1,0:T(8,128)S(1)}) custom-call(f32[16,16,128]{2,1,0:T(8,128)S(1)} %all_to_all.50.got, f32[2048,2048]{1,0:T(8,128)S(1)} %get-tuple-element.47.terms, f32[16,128]{1,0:T(8,128)S(1)} %get-tuple-element.48.weight), custom_call_target="tpu_custom_call" | custom-call | tf_op jit(solution)/shard_map/last_product/pallas_call | solution.py:263
  123.0 10.2 %all_to_all.51.got = f32[16,16,128]{2,1,0:T(8,128)S(1)} all-to-all(f32[16,16,128]{2,1,0:T(8,128)S(1)} %get-tuple-element.50), channel_id=1, replica_groups=mesh['x'=4,'zh'=4,'zl'=2,'y'=4,'c'=2] {'x','y'}, dimensions={0} | all-to-all | bytes 262144 | tf_op jit(solution)/shard_map/all_to_all | solution.py:275
  133.2 0.5 mismatch.1
  133.8 10.5 %all_to_all.52 = f32[16,1,128]{2,1,0:T(1,128)S(1)} all-to-all(f32[16,1,128]{2,1,0:T(1,128)S(1)} %get-tuple-element.56), channel_id=1, replica_groups=mesh['x'=4,'zh'=4,'zl'=2,'y'=4,'c'=2] {'zh','zl','c'}, dimensions={0} | all-to-all | bytes 16384 | tf_op jit(solution)/shard_map/all_to_all | solution.py:275
  144.2 0.6 slice_reduce_fusion
  (17 shorter events, 2.4 us)
Async XLA Ops:
  2.1 12.4 %collective-permute-start.3 = (bf16[1,80,128]{2,1,0:T(8,128)(2,1)S(1)}, bf16[1,80,128]{2,1,0:T(8,128)(2,1)S(1)}, u32[]{:S(2)}, u32[]{:S(2)}) collective-permute-start(bf16[1,80,128]{2,1,0:T(8,128)(2,1)S(1)} %get-tuple-element.32), channel_id=1, source_target_pairs={{0,192},{64,128},{128,64},{192,0},{1,193},{65,129},{129,65},{193,1... | collective-permute-start | bytes 61448 | tf_op jit(solution)/shard_map/ppermute | solution.py:306
  5.5 9.0 %collective-permute-start.2 = (bf16[1,80,128]{2,1,0:T(8,128)(2,1)S(1)}, bf16[1,80,128]{2,1,0:T(8,128)(2,1)S(1)}, u32[]{:S(2)}, u32[]{:S(2)}) collective-permute-start(bf16[1,80,128]{2,1,0:T(8,128)(2,1)S(1)} %get-tuple-element.32), channel_id=1, source_target_pairs={{0,128},{64,192},{128,0},{192,64},{1,129},{65,193},{129,1},{193,65... | collective-permute-start | bytes 61448 | tf_op jit(solution)/shard_map/ppermute | solution.py:306
  6.0 8.5 %collective-permute-start.1 = (bf16[1,80,128]{2,1,0:T(8,128)(2,1)S(1)}, bf16[1,80,128]{2,1,0:T(8,128)(2,1)S(1)}, u32[]{:S(2)}, u32[]{:S(2)}) collective-permute-start(bf16[1,80,128]{2,1,0:T(8,128)(2,1)S(1)} %get-tuple-element.32), channel_id=1, source_target_pairs={{0,64},{64,0},{128,192},{192,128},{1,65},{65,1},{129,193},{193,129... | collective-permute-start | bytes 61448 | tf_op jit(solution)/shard_map/ppermute | solution.py:306
  6.2 16.6 %all-to-all-start = ((bf16[8,80,128]{2,1,0:T(8,128)(2,1)}), bf16[8,80,128]{2,1,0:T(8,128)(2,1)S(1)}, u32[]{:S(2)}, u32[]{:S(2)}) async-start(bf16[8,80,128]{2,1,0:T(8,128)(2,1)} %get-tuple-element.30), calls=%async_computation | async-start | bytes 327680 | tf_op jit(solution)/shard_map/all_to_all | solution.py:275
  14.5 11.1 %collective-permute-start.6 = (bf16[4,80,128]{2,1,0:T(8,128)(2,1)S(1)}, bf16[4,80,128]{2,1,0:T(8,128)(2,1)S(1)}, u32[]{:S(2)}, u32[]{:S(2)}) collective-permute-start(bf16[4,80,128]{2,1,0:T(8,128)(2,1)S(1)} %constant_dynamic-update-slice_fusion.own), channel_id=1, source_target_pairs={{0,6},{2,4},{4,2},{6,0},{1,7},{3,5},{5,3},{7,1},{8,14},{10,12},{12... | collective-permute-start | bytes 245768 | tf_op jit(solution)/shard_map/ppermute | solution.py:306
  17.4 8.3 %collective-permute-start.5 = (bf16[4,80,128]{2,1,0:T(8,128)(2,1)S(1)}, bf16[4,80,128]{2,1,0:T(8,128)(2,1)S(1)}, u32[]{:S(2)}, u32[]{:S(2)}) collective-permute-start(bf16[4,80,128]{2,1,0:T(8,128)(2,1)S(1)} %constant_dynamic-update-slice_fusion.own), channel_id=1, source_target_pairs={{0,4},{2,6},{4,0},{6,2},{1,5},{3,7},{5,1},{7,3},{8,12},{10,14},{12... | collective-permute-start | bytes 245768 | tf_op jit(solution)/shard_map/ppermute | solution.py:306
  17.7 8.0 %collective-permute-start.4 = (bf16[4,80,128]{2,1,0:T(8,128)(2,1)S(1)}, bf16[4,80,128]{2,1,0:T(8,128)(2,1)S(1)}, u32[]{:S(2)}, u32[]{:S(2)}) collective-permute-start(bf16[4,80,128]{2,1,0:T(8,128)(2,1)S(1)} %constant_dynamic-update-slice_fusion.own), channel_id=1, source_target_pairs={{0,2},{2,0},{4,6},{6,4},{1,3},{3,1},{5,7},{7,5},{8,10},{10,8},{12,... | collective-permute-start | bytes 245768 | tf_op jit(solution)/shard_map/ppermute | solution.py:306
  22.8 3.9 %collective-permute-start = (bf16[8,80,128]{2,1,0:T(8,128)(2,1)S(1)}, bf16[8,80,128]{2,1,0:T(8,128)(2,1)S(1)}, u32[]{:S(2)}, u32[]{:S(2)}) collective-permute-start(bf16[8,80,128]{2,1,0:T(8,128)(2,1)S(1)} %all-to-all-done.own), channel_id=1, source_target_pairs={{0,1},{1,0},{2,3},{3,2},{4,5},{5,4},{6,7},{7,6},{8,9},{9,8},{10,11... | collective-permute-start | bytes 491528 | tf_op jit(solution)/shard_map/ppermute | solution.py:306

commit v6 on v5

--- a/solution.py
+++ b/solution.py
@@ -201,25 +201,20 @@
         send(jnp.concatenate([embeds[k], row], axis=0), out)
 
 
-def sources_kernel(own, far, _, wide, tail, raw, scale):
-    x, y = lax.axis_index("x"), lax.axis_index("y")
+def first_kernel(
+    src_own, src_far, tgt_own, tgt_other, s_wide, s_tail, s_raw, s_scale, t_wide, t_tail, t_raw, t_scale, out, ratio, part, top
+):
+    x, y, core = lax.axis_index("x"), lax.axis_index("y"), lax.axis_index("c")
+    blocks = [(tgt_own.at[z], 2 * z + core) for z in range(tgt_own.shape[0])]
+    blocks += [(tgt_other.at[z], 2 * z + 1 - core) for z in range(tgt_own.shape[0])]
+    prepare(blocks, t_wide, t_tail, t_raw, t_scale)
     blocks = []
     for m in range(4):
         for k in range(4):
-            ref = (own.at[k] if m == 0 else far.at[m - 1, k])
+            ref = src_own.at[k] if m == 0 else src_far.at[m - 1, k]
             blocks.append((ref, (x ^ k) * 4 + (y ^ m)))
-    prepare(blocks, wide, tail, raw, scale)
-
-
-def targets_kernel(own, other, wide, tail, raw, scale):
-    core = lax.axis_index("c")
-    blocks = [(own.at[z], 2 * z + core) for z in range(own.shape[0])]
-    blocks += [(other.at[z], 2 * z + 1 - core) for z in range(own.shape[0])]
-    prepare(blocks, wide, tail, raw, scale)
-
-
-def first_kernel(wide, raw, tail, scale, out, ratio, part, top):
-    log_pass((wide, raw, tail, scale), None, ratio, part, top, 512, 100.0, 2.0**120)
+    prepare(blocks, s_wide, s_tail, s_raw, s_scale)
+    log_pass((t_wide, s_raw, s_tail, s_scale), None, ratio, part, top, 512, 100.0, 2.0**120)
     send(top[...] + log2(part[...]), out)
 
 
@@ -322,16 +317,10 @@
     row_ratio = pltpu.VMEM((3,) + src_rows, f32)
     col_ratio = pltpu.VMEM((3,) + tgt_rows, f32)
 
-    t_wide, t_tail, t_raw, t_scale = call(
-        targets_kernel, [tgt, tgt_other], operands(tgt_size, tgt_rows), [], "targets"
-    )
-    s_wide, s_tail, s_raw, s_scale = call(
-        sources_kernel, [src, src_far, t_scale], operands(src_size, src_rows), [], "sources"
-    )
-    (sent,) = call(
+    s_wide, s_tail, s_raw, s_scale, t_wide, t_tail, t_raw, t_scale, sent = call(
         first_kernel,
-        [t_wide, s_raw, s_tail, s_scale],
-        [row_out],
+        [src, src_far, tgt, tgt_other],
+        operands(src_size, src_rows) + operands(tgt_size, tgt_rows) + [row_out],
         [row_ratio, row_part, row_part],
         "row_pass_1",
     )

time: 147 us -> 148 us (level)
    pallas_call x10 -> x8, Pallas kernels: 17.2 us -> 17.4 us  [call(): pl.pallas_call(kernel, out_shape=[jax.ShapeDtypeStruct(shape, dtype) for...]
where the time goes in v6:
time: 148 us; the launch traced here: 147 us
  blocking collectives  100 us (68%)
  Pallas kernels  18.9 us (13%)
  starting transfers between devices  18.8 us (13%)
  waiting for transfers between devices  5.73 us (4%)
  between operations  2.55 us (2%)
    all_to_all x8, blocking collectives, exchange(): return lax.all_to_all(sent, group, 0, 0)  100 us
    pallas_call x8, Pallas kernels, call(): pl.pallas_call(kernel, out_shape=[jax.ShapeDtypeStruct(shape, dtype) for...  17.4 us
    ppermute x7, starting transfers between devices, neighbours(): lax.ppermute(array, axis, [(i, i ^ k) for i in range(size)])  10.5 us
    all_to_all x1, starting transfers between devices, exchange(): return lax.all_to_all(sent, group, 0, 0)  8.28 us
    all_to_all x1, waiting for transfers between devices, exchange(): return lax.all_to_all(sent, group, 0, 0)  4.74 us
  transfers between devices with their start and end apart: 8, of which 2 were waited for; matrix products, arithmetic and copies ran while one was open for 0% of the time, Pallas kernels for 0%

profile of v6, /device:TPU:1, one launch (start us, length us, event | category | flops | bytes accessed | tf_op | source)
XLA Modules:
  0.0 146.8 jit_solution(3718206837924526756)
XLA Ops:
  0.6 1.5 pack.1
  2.1 3.4 %collective-permute-start.2 = (bf16[1,80,128]{2,1,0:T(8,128)(2,1)S(1)}, bf16[1,80,128]{2,1,0:T(8,128)(2,1)S(1)}, u32[]{:S(2)}, u32[]{:S(2)}) collective-permute-start(bf16[1,80,128]{2,1,0:T(8,128)(2,1)S(1)} %get-tuple-element.31), channel_id=1, source_target_pairs={{0,192},{64,128},{128,64},{192,0},{1,193},{65,129},{129,65},{193,1... | collective-permute-start | bytes 61448 | tf_op jit(solution)/shard_map/ppermute | solution.py:301
  6.2 8.3 %all-to-all-start = ((bf16[8,80,128]{2,1,0:T(8,128)(2,1)}), bf16[8,80,128]{2,1,0:T(8,128)(2,1)S(1)}, u32[]{:S(2)}, u32[]{:S(2)}) async-start(bf16[8,80,128]{2,1,0:T(8,128)(2,1)} %get-tuple-element.32), calls=%async_computation | async-start | bytes 327680 | tf_op jit(solution)/shard_map/all_to_all | solution.py:270
  14.5 2.8 %collective-permute-start.5 = (bf16[4,80,128]{2,1,0:T(8,128)(2,1)S(1)}, bf16[4,80,128]{2,1,0:T(8,128)(2,1)S(1)}, u32[]{:S(2)}, u32[]{:S(2)}) collective-permute-start(bf16[4,80,128]{2,1,0:T(8,128)(2,1)S(1)} %constant_dynamic-update-slice_fusion.src_own), channel_id=1, source_target_pairs={{0,6},{2,4},{4,2},{6,0},{1,7},{3,5},{5,3},{7,1},{8,14},{10,12},{12... | collective-permute-start | bytes 245768 | tf_op jit(solution)/shard_map/ppermute | solution.py:301
  18.0 4.7 %all-to-all-done.tgt_own = bf16[8,80,128]{2,1,0:T(8,128)(2,1)S(1)} async-done(((bf16[8,80,128]{2,1,0:T(8,128)(2,1)}), bf16[8,80,128]{2,1,0:T(8,128)(2,1)S(1)}, u32[]{:S(2)}, u32[]{:S(2)}) %all-to-all-start) | async-done | bytes 163872 | tf_op jit(solution)/shard_map/all_to_all | solution.py:270
  22.8 2.9 %collective-permute-start.6 = (bf16[8,80,128]{2,1,0:T(8,128)(2,1)S(1)}, bf16[8,80,128]{2,1,0:T(8,128)(2,1)S(1)}, u32[]{:S(2)}, u32[]{:S(2)}) collective-permute-start(bf16[8,80,128]{2,1,0:T(8,128)(2,1)S(1)} %all-to-all-done.tgt_own), channel_id=1, source_target_pairs={{0,1},{1,0},{2,3},{3,2},{4,5},{5,4},{6,7},{7,6},{8,9},{9,8},{10,11... | collective-permute-start | bytes 491528 | tf_op jit(solution)/shard_map/ppermute | solution.py:301
  25.7 1.0 collective-permute-done.6.tgt_other
  26.7 4.0 %row_pass_1.1 = (bf16[2048,144]{1,0:T(8,128)(2,1)S(1)}, f32[16,2048]{1,0:T(8,128)S(1)}, bf16[64,2048]{1,0:T(8,128)(2,1)S(1)}, f32[16,128]{1,0:T(8,128)S(1)}, bf1...) custom-call(bf16[4,80,128]{2,1,0:T(8,128)(2,1)S(1)} %constant_dynami, ...), custom_call_target="tpu_custom_call" | custom-call | tf_op jit(solution)/shard_map/row_pass_1/pallas_call | solution.py:258
  30.7 13.2 %all_to_all.45.got = f32[16,16,128]{2,1,0:T(8,128)S(1)} all-to-all(f32[16,16,128]{2,1,0:T(8,128)S(1)} %get-tuple-element.33), channel_id=1, replica_groups=mesh['x'=4,'zh'=4,'zl'=2,'y'=4,'c'=2] {'x','y'}, dimensions={0} | all-to-all | bytes 262144 | tf_op jit(solution)/shard_map/all_to_all | solution.py:270
  43.9 3.1 %col_pass_1.1 = (f32[16,128]{1,0:T(8,128)S(1)}, f32[16,128]{1,0:T(8,128)S(1)}, f32[16,128]{1,0:T(8,128)S(1)}, f32[2048,2048]{1,0:T(8,128)S(1)}, f32[16,16,128]{2,1,0:T(8,128)S(1)}) custom-call(f32[16,16,128]{2,1,0:T(8,128)S(1)} %all_to_all.45.got, bf16[2048,144]{1,0:T(8,128)(2,1)S(1)} %get-tuple-element.34.wide, bf16[64,2048]{1,0:T(8,128)(2,1)S(1)} %get-tuple-element.35.raw, ...), custom_call_target="tpu_custom_call" | custom-call | tf_op jit(solution)/shard_map/col_pass_1/pallas_call | solution.py:258
  47.0 15.1 %all_to_all.46.got = f32[16,16,128]{2,1,0:T(8,128)S(1)} all-to-all(f32[16,16,128]{2,1,0:T(8,128)S(1)} %get-tuple-element.38), channel_id=1, replica_groups=mesh['x'=4,'zh'=4,'zl'=2,'y'=4,'c'=2] {'zh','zl','c'}, dimensions={0} | all-to-all | bytes 262144 | tf_op jit(solution)/shard_map/all_to_all | solution.py:270
  62.2 3.0 %row_pass_2.1 = (f32[16,128]{1,0:T(8,128)S(1)}, f32[2048,2048]{1,0:T(8,128)S(1)}, f32[16,128]{1,0:T(8,128)S(1)}, f32[16,128]{1,0:T(8,128)S(1)}, f32[16,16,128]{2,1,0:T(8,128)S(1)}) custom-call(f32[16,16,128]{2,1,0:T(8,128)S(1)} %all_to_all.46.got, f32[16,128]{1,0:T(8,128)S(1)} %get-tuple-element.39.kept.f, f32[16,128]{1,0:T(8,128)S(1)} %get-tuple-element.40.lse, ...), custom_call_target="tpu_custom_call" | custom-call | tf_op jit(solution)/shard_map/row_pass_2/pallas_call | solution.py:258
  65.2 15.7 %all_to_all.47.got = f32[16,16,128]{2,1,0:T(8,128)S(1)} all-to-all(f32[16,16,128]{2,1,0:T(8,128)S(1)} %get-tuple-element.46), channel_id=1, replica_groups=mesh['x'=4,'zh'=4,'zl'=2,'y'=4,'c'=2] {'x','y'}, dimensions={0} | all-to-all | bytes 262144 | tf_op jit(solution)/shard_map/all_to_all | solution.py:270
  80.9 1.7 %product.2 = f32[16,16,128]{2,1,0:T(8,128)S(1)} custom-call(f32[16,16,128]{2,1,0:T(8,128)S(1)} %all_to_all.47.got, f32[2048,2048]{1,0:T(8,128)S(1)} %get-tuple-element.47.terms, f32[16,128]{1,0:T(8,128)S(1)} %get-tuple-element.48.weight), custom_call_target="tpu_custom_call" | custom-call | tf_op jit(solution)/shard_map/product/pallas_call | solution.py:258
  82.6 12.6 %all_to_all.48.got = f32[16,16,128]{2,1,0:T(8,128)S(1)} all-to-all(f32[16,16,128]{2,1,0:T(8,128)S(1)} %product.2), channel_id=1, replica_groups=mesh['x'=4,'zh'=4,'zl'=2,'y'=4,'c'=2] {'zh','zl','c'}, dimensions={0} | all-to-all | bytes 262144 | tf_op jit(solution)/shard_map/all_to_all | solution.py:270
  95.2 1.7 %product.3 = f32[16,16,128]{2,1,0:T(8,128)S(1)} custom-call(f32[16,16,128]{2,1,0:T(8,128)S(1)} %all_to_all.48.got, f32[2048,2048]{1,0:T(8,128)S(1)} %get-tuple-element.49.terms, f32[16,128]{1,0:T(8,128)S(1)} %get-tuple-element.50.weight), custom_call_target="tpu_custom_call" | custom-call | tf_op jit(solution)/shard_map/product/pallas_call | solution.py:258
  96.9 10.2 %all_to_all.49.got = f32[16,16,128]{2,1,0:T(8,128)S(1)} all-to-all(f32[16,16,128]{2,1,0:T(8,128)S(1)} %product.3), channel_id=1, replica_groups=mesh['x'=4,'zh'=4,'zl'=2,'y'=4,'c'=2] {'x','y'}, dimensions={0} | all-to-all | bytes 262144 | tf_op jit(solution)/shard_map/all_to_all | solution.py:270
  107.1 1.7 %last_product.2 = (f32[16,128]{1,0:T(8,128)S(1)}, f32[16,16,128]{2,1,0:T(8,128)S(1)}) custom-call(f32[16,16,128]{2,1,0:T(8,128)S(1)} %all_to_all.49.got, f32[2048,2048]{1,0:T(8,128)S(1)} %get-tuple-element.47.terms, f32[16,128]{1,0:T(8,128)S(1)} %get-tuple-element.48.weight), custom_call_target="tpu_custom_call" | custom-call | tf_op jit(solution)/shard_map/last_product/pallas_call | solution.py:258
  108.8 12.6 %all_to_all.50.got = f32[16,16,128]{2,1,0:T(8,128)S(1)} all-to-all(f32[16,16,128]{2,1,0:T(8,128)S(1)} %get-tuple-element.51), channel_id=1, replica_groups=mesh['x'=4,'zh'=4,'zl'=2,'y'=4,'c'=2] {'zh','zl','c'}, dimensions={0} | all-to-all | bytes 262144 | tf_op jit(solution)/shard_map/all_to_all | solution.py:270
  121.5 1.7 %last_product.3 = (f32[16,128]{1,0:T(8,128)S(1)}, f32[16,16,128]{2,1,0:T(8,128)S(1)}) custom-call(f32[16,16,128]{2,1,0:T(8,128)S(1)} %all_to_all.50.got, f32[2048,2048]{1,0:T(8,128)S(1)} %get-tuple-element.49.terms, f32[16,128]{1,0:T(8,128)S(1)} %get-tuple-element.50.weight), custom_call_target="tpu_custom_call" | custom-call | tf_op jit(solution)/shard_map/last_product/pallas_call | solution.py:258
  123.2 10.2 %all_to_all.51.got = f32[16,16,128]{2,1,0:T(8,128)S(1)} all-to-all(f32[16,16,128]{2,1,0:T(8,128)S(1)} %get-tuple-element.52), channel_id=1, replica_groups=mesh['x'=4,'zh'=4,'zl'=2,'y'=4,'c'=2] {'x','y'}, dimensions={0} | all-to-all | bytes 262144 | tf_op jit(solution)/shard_map/all_to_all | solution.py:270
  133.4 0.5 mismatch.1
  133.9 10.5 %all_to_all.52 = f32[16,1,128]{2,1,0:T(1,128)S(1)} all-to-all(f32[16,1,128]{2,1,0:T(1,128)S(1)} %get-tuple-element.58), channel_id=1, replica_groups=mesh['x'=4,'zh'=4,'zl'=2,'y'=4,'c'=2] {'zh','zl','c'}, dimensions={0} | all-to-all | bytes 16384 | tf_op jit(solution)/shard_map/all_to_all | solution.py:270
  144.4 0.6 slice_reduce_fusion
  (15 shorter events, 1.4 us)
Async XLA Ops:
  2.1 12.4 %collective-permute-start.2 = (bf16[1,80,128]{2,1,0:T(8,128)(2,1)S(1)}, bf16[1,80,128]{2,1,0:T(8,128)(2,1)S(1)}, u32[]{:S(2)}, u32[]{:S(2)}) collective-permute-start(bf16[1,80,128]{2,1,0:T(8,128)(2,1)S(1)} %get-tuple-element.31), channel_id=1, source_target_pairs={{0,192},{64,128},{128,64},{192,0},{1,193},{65,129},{129,65},{193,1... | collective-permute-start | bytes 61448 | tf_op jit(solution)/shard_map/ppermute | solution.py:301
  5.5 9.0 %collective-permute-start.1 = (bf16[1,80,128]{2,1,0:T(8,128)(2,1)S(1)}, bf16[1,80,128]{2,1,0:T(8,128)(2,1)S(1)}, u32[]{:S(2)}, u32[]{:S(2)}) collective-permute-start(bf16[1,80,128]{2,1,0:T(8,128)(2,1)S(1)} %get-tuple-element.31), channel_id=1, source_target_pairs={{0,128},{64,192},{128,0},{192,64},{1,129},{65,193},{129,1},{193,65... | collective-permute-start | bytes 61448 | tf_op jit(solution)/shard_map/ppermute | solution.py:301
  6.0 8.5 %collective-permute-start = (bf16[1,80,128]{2,1,0:T(8,128)(2,1)S(1)}, bf16[1,80,128]{2,1,0:T(8,128)(2,1)S(1)}, u32[]{:S(2)}, u32[]{:S(2)}) collective-permute-start(bf16[1,80,128]{2,1,0:T(8,128)(2,1)S(1)} %get-tuple-element.31), channel_id=1, source_target_pairs={{0,64},{64,0},{128,192},{192,128},{1,65},{65,1},{129,193},{193,129... | collective-permute-start | bytes 61448 | tf_op jit(solution)/shard_map/ppermute | solution.py:301
  6.2 16.6 %all-to-all-start = ((bf16[8,80,128]{2,1,0:T(8,128)(2,1)}), bf16[8,80,128]{2,1,0:T(8,128)(2,1)S(1)}, u32[]{:S(2)}, u32[]{:S(2)}) async-start(bf16[8,80,128]{2,1,0:T(8,128)(2,1)} %get-tuple-element.32), calls=%async_computation | async-start | bytes 327680 | tf_op jit(solution)/shard_map/all_to_all | solution.py:270
  14.5 11.1 %collective-permute-start.5 = (bf16[4,80,128]{2,1,0:T(8,128)(2,1)S(1)}, bf16[4,80,128]{2,1,0:T(8,128)(2,1)S(1)}, u32[]{:S(2)}, u32[]{:S(2)}) collective-permute-start(bf16[4,80,128]{2,1,0:T(8,128)(2,1)S(1)} %constant_dynamic-update-slice_fusion.src_own), channel_id=1, source_target_pairs={{0,6},{2,4},{4,2},{6,0},{1,7},{3,5},{5,3},{7,1},{8,14},{10,12},{12... | collective-permute-start | bytes 245768 | tf_op jit(solution)/shard_map/ppermute | solution.py:301
  17.4 8.3 %collective-permute-start.4 = (bf16[4,80,128]{2,1,0:T(8,128)(2,1)S(1)}, bf16[4,80,128]{2,1,0:T(8,128)(2,1)S(1)}, u32[]{:S(2)}, u32[]{:S(2)}) collective-permute-start(bf16[4,80,128]{2,1,0:T(8,128)(2,1)S(1)} %constant_dynamic-update-slice_fusion.src_own), channel_id=1, source_target_pairs={{0,4},{2,6},{4,0},{6,2},{1,5},{3,7},{5,1},{7,3},{8,12},{10,14},{12... | collective-permute-start | bytes 245768 | tf_op jit(solution)/shard_map/ppermute | solution.py:301
  17.7 8.0 %collective-permute-start.3 = (bf16[4,80,128]{2,1,0:T(8,128)(2,1)S(1)}, bf16[4,80,128]{2,1,0:T(8,128)(2,1)S(1)}, u32[]{:S(2)}, u32[]{:S(2)}) collective-permute-start(bf16[4,80,128]{2,1,0:T(8,128)(2,1)S(1)} %constant_dynamic-update-slice_fusion.src_own), channel_id=1, source_target_pairs={{0,2},{2,0},{4,6},{6,4},{1,3},{3,1},{5,7},{7,5},{8,10},{10,8},{12,... | collective-permute-start | bytes 245768 | tf_op jit(solution)/shard_map/ppermute | solution.py:301
  22.8 3.9 %collective-permute-start.6 = (bf16[8,80,128]{2,1,0:T(8,128)(2,1)S(1)}, bf16[8,80,128]{2,1,0:T(8,128)(2,1)S(1)}, u32[]{:S(2)}, u32[]{:S(2)}) collective-permute-start(bf16[8,80,128]{2,1,0:T(8,128)(2,1)S(1)} %all-to-all-done.tgt_own), channel_id=1, source_target_pairs={{0,1},{1,0},{2,3},{3,2},{4,5},{5,4},{6,7},{7,6},{8,9},{9,8},{10,11... | collective-permute-start | bytes 491528 | tf_op jit(solution)/shard_map/ppermute | solution.py:301

commit v7 on v5

--- a/solution.py
+++ b/solution.py
@@ -202,12 +202,13 @@
 
 
 def sources_kernel(own, far, _, wide, tail, raw, scale):
-    x, y = lax.axis_index("x"), lax.axis_index("y")
+    x, y, core = lax.axis_index("x"), lax.axis_index("y"), lax.axis_index("c")
     blocks = []
     for m in range(4):
         for k in range(4):
-            ref = (own.at[k] if m == 0 else far.at[m - 1, k])
-            blocks.append((ref, (x ^ k) * 4 + (y ^ m)))
+            ref = own.at[k] if m == 0 else far.at[m - 1, k]
+            dx, dy = jnp.where(core == 0, k, m), jnp.where(core == 0, m, k)
+            blocks.append((ref, (x ^ dx) * 4 + (y ^ dy)))
     prepare(blocks, wide, tail, raw, scale)
 
 
@@ -273,6 +274,19 @@
 
 def exchange(sent, group):
     return lax.all_to_all(sent, group, 0, 0)
+
+
+def crossed(array, turn):
+    out = []
+    for k in range(1, 4):
+        pairs = []
+        for x in range(4):
+            for y in range(4):
+                for core in range(2):
+                    other = (x ^ k, y) if core == turn else (x, y ^ k)
+                    pairs.append(((x * 4 + y) * 2 + core, (other[0] * 4 + other[1]) * 2 + core))
+        out.append(lax.ppermute(array, ("x", "y", "c"), pairs))
+    return out
 
 
 def on_device(src_embed, tgt_embed, src_weight, tgt_weight):
@@ -306,8 +320,8 @@
         return [lax.ppermute(array, axis, [(i, i ^ k) for i in range(size)]) for k in range(1, size)]
 
     tgt = exchange(tgt_sent, ("zh", "zl"))
-    src = jnp.concatenate([src_sent] + neighbours(src_sent, "x"), axis=0)
-    src_far = jnp.stack(neighbours(src, "y"))
+    src = jnp.concatenate([src_sent] + crossed(src_sent, 0), axis=0)
+    src_far = jnp.stack(crossed(src, 1))
     (tgt_other,) = neighbours(tgt, "c")
 
     wide = 2 * depth + TAIL

time: 147 us -> 148 us (level)
    ppermute x7 -> x1, starting transfers between devices: 10.5 us -> 2.69 us  [neighbours(): lax.ppermute(array, axis, [(i, i ^ k) for i in range(size)])]
    ppermute x0 -> x6, starting transfers between devices: none -> 7.67 us  [crossed(): out.append(lax.ppermute(array, ('x', 'y', 'c'), pairs))]
where the time goes in v7:
time: 148 us
  blocking collectives  101 us (68%)
  Pallas kernels  18.9 us (13%)
  starting transfers between devices  18.5 us (12%)
  waiting for transfers between devices  5.95 us (4%)
  between operations  2.57 us (2%)
    all_to_all x8, blocking collectives, exchange(): return lax.all_to_all(sent, group, 0, 0)  101 us
    pallas_call x10, Pallas kernels, call(): pl.pallas_call(kernel, out_shape=[jax.ShapeDtypeStruct(shape, dtype) for...  17.4 us
    all_to_all x1, starting transfers between devices, exchange(): return lax.all_to_all(sent, group, 0, 0)  8.19 us
    ppermute x6, starting transfers between devices, crossed(): out.append(lax.ppermute(array, ('x', 'y', 'c'), pairs))  7.67 us
    all_to_all x1, waiting for transfers between devices, exchange(): return lax.all_to_all(sent, group, 0, 0)  4.96 us
  transfers between devices with their start and end apart: 8, of which 2 were waited for; matrix products, arithmetic and copies ran while one was open for 0% of the time, Pallas kernels for 0%

profile of v7, /device:TPU:1, one launch (start us, length us, event | category | flops | bytes accessed | tf_op | source)
XLA Modules:
  0.0 147.9 jit_solution(10599071883907698261)
XLA Ops:
  0.6 1.5 pack.1
  2.1 3.7 %collective-permute-start.3 = (bf16[1,80,128]{2,1,0:T(8,128)(2,1)S(1)}, bf16[1,80,128]{2,1,0:T(8,128)(2,1)S(1)}, u32[]{:S(2)}, u32[]{:S(2)}) collective-permute-start(bf16[1,80,128]{2,1,0:T(8,128)(2,1)S(1)} %get-tuple-element.32), channel_id=1, source_target_pairs={{0,192},{1,7},{2,194},{3,5},{4,196},{5,3},{6,198},{7,1},{64,128},{... | collective-permute-start | bytes 61448 | tf_op jit(solution)/shard_map/ppermute | solution.py:288
  6.4 8.2 %all-to-all-start = ((bf16[8,80,128]{2,1,0:T(8,128)(2,1)}), bf16[8,80,128]{2,1,0:T(8,128)(2,1)S(1)}, u32[]{:S(2)}, u32[]{:S(2)}) async-start(bf16[8,80,128]{2,1,0:T(8,128)(2,1)} %get-tuple-element.30), calls=%async_computation | async-start | bytes 327680 | tf_op jit(solution)/shard_map/all_to_all | solution.py:276
  14.7 2.6 %collective-permute-start.6 = (bf16[4,80,128]{2,1,0:T(8,128)(2,1)S(1)}, bf16[4,80,128]{2,1,0:T(8,128)(2,1)S(1)}, u32[]{:S(2)}, u32[]{:S(2)}) collective-permute-start(bf16[4,80,128]{2,1,0:T(8,128)(2,1)S(1)} %constant_dynamic-update-slice_fusion.own), channel_id=1, source_target_pairs={{0,6},{1,193},{2,4},{3,195},{4,2},{5,197},{6,0},{7,199},{64,70},{6... | collective-permute-start | bytes 245768 | tf_op jit(solution)/shard_map/ppermute | solution.py:288
  18.0 5.0 %all-to-all-done.own = bf16[8,80,128]{2,1,0:T(8,128)(2,1)S(1)} async-done(((bf16[8,80,128]{2,1,0:T(8,128)(2,1)}), bf16[8,80,128]{2,1,0:T(8,128)(2,1)S(1)}, u32[]{:S(2)}, u32[]{:S(2)}) %all-to-all-start) | async-done | bytes 163872 | tf_op jit(solution)/shard_map/all_to_all | solution.py:276
  23.0 2.7 %collective-permute-start = (bf16[8,80,128]{2,1,0:T(8,128)(2,1)S(1)}, bf16[8,80,128]{2,1,0:T(8,128)(2,1)S(1)}, u32[]{:S(2)}, u32[]{:S(2)}) collective-permute-start(bf16[8,80,128]{2,1,0:T(8,128)(2,1)S(1)} %all-to-all-done.own), channel_id=1, source_target_pairs={{0,1},{1,0},{2,3},{3,2},{4,5},{5,4},{6,7},{7,6},{8,9},{9,8},{10,11... | collective-permute-start | bytes 491528 | tf_op jit(solution)/shard_map/ppermute | solution.py:320
  25.7 1.0 collective-permute-done.other
  27.7 3.2 %row_pass_1.1 = f32[16,16,128]{2,1,0:T(8,128)S(1)} custom-call(bf16[2048,144]{1,0:T(8,128)(2,1)S(1)} %get-tuple-element.31.wide, bf16[64,2048]{1,0:T(8,128)(2,1)S(1)} %get-tuple-element.34.raw, f32[16,2048]{1,0:T(8,128)S(1)} %get-tuple-element.35.tail, f32[16,128]{1,0:T(8,128)S(1)} %get-tuple-element.36.scale), custom_call_target="tpu_custom_call" | custom-call | tf_op jit(solution)/shard_map/row_pass_1/pallas_call | solution.py:264
  30.9 13.2 %all_to_all.45.got = f32[16,16,128]{2,1,0:T(8,128)S(1)} all-to-all(f32[16,16,128]{2,1,0:T(8,128)S(1)} %row_pass_1.1), channel_id=1, replica_groups=mesh['x'=4,'zh'=4,'zl'=2,'y'=4,'c'=2] {'x','y'}, dimensions={0} | all-to-all | bytes 262144 | tf_op jit(solution)/shard_map/all_to_all | solution.py:276
  44.1 3.1 %col_pass_1.1 = (f32[16,128]{1,0:T(8,128)S(1)}, f32[16,128]{1,0:T(8,128)S(1)}, f32[16,128]{1,0:T(8,128)S(1)}, f32[2048,2048]{1,0:T(8,128)S(1)}, f32[16,16,128]{2,1,0:T(8,128)S(1)}) custom-call(f32[16,16,128]{2,1,0:T(8,128)S(1)} %all_to_all.45.got, bf16[2048,144]{1,0:T(8,128)(2,1)S(1)} %get-tuple-element.37.wide, bf16[64,2048]{1,0:T(8,128)(2,1)S(1)} %get-tuple-element.38.raw, ...), custom_call_target="tpu_custom_call" | custom-call | tf_op jit(solution)/shard_map/col_pass_1/pallas_call | solution.py:264
  47.2 15.2 %all_to_all.46.got = f32[16,16,128]{2,1,0:T(8,128)S(1)} all-to-all(f32[16,16,128]{2,1,0:T(8,128)S(1)} %get-tuple-element.40), channel_id=1, replica_groups=mesh['x'=4,'zh'=4,'zl'=2,'y'=4,'c'=2] {'zh','zl','c'}, dimensions={0} | all-to-all | bytes 262144 | tf_op jit(solution)/shard_map/all_to_all | solution.py:276
  62.4 2.9 %row_pass_2.1 = (f32[16,128]{1,0:T(8,128)S(1)}, f32[2048,2048]{1,0:T(8,128)S(1)}, f32[16,128]{1,0:T(8,128)S(1)}, f32[16,128]{1,0:T(8,128)S(1)}, f32[16,16,128]{2,1,0:T(8,128)S(1)}) custom-call(f32[16,16,128]{2,1,0:T(8,128)S(1)} %all_to_all.46.got, f32[16,128]{1,0:T(8,128)S(1)} %get-tuple-element.41.kept.f, f32[16,128]{1,0:T(8,128)S(1)} %get-tuple-element.42.lse, ...), custom_call_target="tpu_custom_call" | custom-call | tf_op jit(solution)/shard_map/row_pass_2/pallas_call | solution.py:264
  65.2 16.8 %all_to_all.47.got = f32[16,16,128]{2,1,0:T(8,128)S(1)} all-to-all(f32[16,16,128]{2,1,0:T(8,128)S(1)} %get-tuple-element.44), channel_id=1, replica_groups=mesh['x'=4,'zh'=4,'zl'=2,'y'=4,'c'=2] {'x','y'}, dimensions={0} | all-to-all | bytes 262144 | tf_op jit(solution)/shard_map/all_to_all | solution.py:276
  82.0 1.7 %product.2 = f32[16,16,128]{2,1,0:T(8,128)S(1)} custom-call(f32[16,16,128]{2,1,0:T(8,128)S(1)} %all_to_all.47.got, f32[2048,2048]{1,0:T(8,128)S(1)} %get-tuple-element.45.terms, f32[16,128]{1,0:T(8,128)S(1)} %get-tuple-element.46.weight), custom_call_target="tpu_custom_call" | custom-call | tf_op jit(solution)/shard_map/product/pallas_call | solution.py:264
  83.7 12.6 %all_to_all.48.got = f32[16,16,128]{2,1,0:T(8,128)S(1)} all-to-all(f32[16,16,128]{2,1,0:T(8,128)S(1)} %product.2), channel_id=1, replica_groups=mesh['x'=4,'zh'=4,'zl'=2,'y'=4,'c'=2] {'zh','zl','c'}, dimensions={0} | all-to-all | bytes 262144 | tf_op jit(solution)/shard_map/all_to_all | solution.py:276
  96.3 1.7 %product.3 = f32[16,16,128]{2,1,0:T(8,128)S(1)} custom-call(f32[16,16,128]{2,1,0:T(8,128)S(1)} %all_to_all.48.got, f32[2048,2048]{1,0:T(8,128)S(1)} %get-tuple-element.47.terms, f32[16,128]{1,0:T(8,128)S(1)} %get-tuple-element.48.weight), custom_call_target="tpu_custom_call" | custom-call | tf_op jit(solution)/shard_map/product/pallas_call | solution.py:264
  98.0 10.2 %all_to_all.49.got = f32[16,16,128]{2,1,0:T(8,128)S(1)} all-to-all(f32[16,16,128]{2,1,0:T(8,128)S(1)} %product.3), channel_id=1, replica_groups=mesh['x'=4,'zh'=4,'zl'=2,'y'=4,'c'=2] {'x','y'}, dimensions={0} | all-to-all | bytes 262144 | tf_op jit(solution)/shard_map/all_to_all | solution.py:276
  108.2 1.7 %last_product.2 = (f32[16,128]{1,0:T(8,128)S(1)}, f32[16,16,128]{2,1,0:T(8,128)S(1)}) custom-call(f32[16,16,128]{2,1,0:T(8,128)S(1)} %all_to_all.49.got, f32[2048,2048]{1,0:T(8,128)S(1)} %get-tuple-element.45.terms, f32[16,128]{1,0:T(8,128)S(1)} %get-tuple-element.46.weight), custom_call_target="tpu_custom_call" | custom-call | tf_op jit(solution)/shard_map/last_product/pallas_call | solution.py:264
  109.9 12.6 %all_to_all.50.got = f32[16,16,128]{2,1,0:T(8,128)S(1)} all-to-all(f32[16,16,128]{2,1,0:T(8,128)S(1)} %get-tuple-element.49), channel_id=1, replica_groups=mesh['x'=4,'zh'=4,'zl'=2,'y'=4,'c'=2] {'zh','zl','c'}, dimensions={0} | all-to-all | bytes 262144 | tf_op jit(solution)/shard_map/all_to_all | solution.py:276
  122.5 1.7 %last_product.3 = (f32[16,128]{1,0:T(8,128)S(1)}, f32[16,16,128]{2,1,0:T(8,128)S(1)}) custom-call(f32[16,16,128]{2,1,0:T(8,128)S(1)} %all_to_all.50.got, f32[2048,2048]{1,0:T(8,128)S(1)} %get-tuple-element.47.terms, f32[16,128]{1,0:T(8,128)S(1)} %get-tuple-element.48.weight), custom_call_target="tpu_custom_call" | custom-call | tf_op jit(solution)/shard_map/last_product/pallas_call | solution.py:264
  124.2 10.2 %all_to_all.51.got = f32[16,16,128]{2,1,0:T(8,128)S(1)} all-to-all(f32[16,16,128]{2,1,0:T(8,128)S(1)} %get-tuple-element.50), channel_id=1, replica_groups=mesh['x'=4,'zh'=4,'zl'=2,'y'=4,'c'=2] {'x','y'}, dimensions={0} | all-to-all | bytes 262144 | tf_op jit(solution)/shard_map/all_to_all | solution.py:276
  134.4 0.5 mismatch.1
  135.0 10.5 %all_to_all.52 = f32[16,1,128]{2,1,0:T(1,128)S(1)} all-to-all(f32[16,1,128]{2,1,0:T(1,128)S(1)} %get-tuple-element.56), channel_id=1, replica_groups=mesh['x'=4,'zh'=4,'zl'=2,'y'=4,'c'=2] {'zh','zl','c'}, dimensions={0} | all-to-all | bytes 16384 | tf_op jit(solution)/shard_map/all_to_all | solution.py:276
  145.4 0.6 slice_reduce_fusion
  (17 shorter events, 2.5 us)
Async XLA Ops:
  2.1 12.6 %collective-permute-start.3 = (bf16[1,80,128]{2,1,0:T(8,128)(2,1)S(1)}, bf16[1,80,128]{2,1,0:T(8,128)(2,1)S(1)}, u32[]{:S(2)}, u32[]{:S(2)}) collective-permute-start(bf16[1,80,128]{2,1,0:T(8,128)(2,1)S(1)} %get-tuple-element.32), channel_id=1, source_target_pairs={{0,192},{1,7},{2,194},{3,5},{4,196},{5,3},{6,198},{7,1},{64,128},{... | collective-permute-start | bytes 61448 | tf_op jit(solution)/shard_map/ppermute | solution.py:288
  5.7 8.9 %collective-permute-start.2 = (bf16[1,80,128]{2,1,0:T(8,128)(2,1)S(1)}, bf16[1,80,128]{2,1,0:T(8,128)(2,1)S(1)}, u32[]{:S(2)}, u32[]{:S(2)}) collective-permute-start(bf16[1,80,128]{2,1,0:T(8,128)(2,1)S(1)} %get-tuple-element.32), channel_id=1, source_target_pairs={{0,128},{1,5},{2,130},{3,7},{4,132},{5,1},{6,134},{7,3},{64,192},{... | collective-permute-start | bytes 61448 | tf_op jit(solution)/shard_map/ppermute | solution.py:288
  6.1 8.5 %collective-permute-start.1 = (bf16[1,80,128]{2,1,0:T(8,128)(2,1)S(1)}, bf16[1,80,128]{2,1,0:T(8,128)(2,1)S(1)}, u32[]{:S(2)}, u32[]{:S(2)}) collective-permute-start(bf16[1,80,128]{2,1,0:T(8,128)(2,1)S(1)} %get-tuple-element.32), channel_id=1, source_target_pairs={{0,64},{1,3},{2,66},{3,1},{4,68},{5,7},{6,70},{7,5},{64,0},{65,67}... | collective-permute-start | bytes 61448 | tf_op jit(solution)/shard_map/ppermute | solution.py:288
  6.4 16.6 %all-to-all-start = ((bf16[8,80,128]{2,1,0:T(8,128)(2,1)}), bf16[8,80,128]{2,1,0:T(8,128)(2,1)S(1)}, u32[]{:S(2)}, u32[]{:S(2)}) async-start(bf16[8,80,128]{2,1,0:T(8,128)(2,1)} %get-tuple-element.30), calls=%async_computation | async-start | bytes 327680 | tf_op jit(solution)/shard_map/all_to_all | solution.py:276
  14.7 11.0 %collective-permute-start.6 = (bf16[4,80,128]{2,1,0:T(8,128)(2,1)S(1)}, bf16[4,80,128]{2,1,0:T(8,128)(2,1)S(1)}, u32[]{:S(2)}, u32[]{:S(2)}) collective-permute-start(bf16[4,80,128]{2,1,0:T(8,128)(2,1)S(1)} %constant_dynamic-update-slice_fusion.own), channel_id=1, source_target_pairs={{0,6},{1,193},{2,4},{3,195},{4,2},{5,197},{6,0},{7,199},{64,70},{6... | collective-permute-start | bytes 245768 | tf_op jit(solution)/shard_map/ppermute | solution.py:288
  17.3 8.4 %collective-permute-start.5 = (bf16[4,80,128]{2,1,0:T(8,128)(2,1)S(1)}, bf16[4,80,128]{2,1,0:T(8,128)(2,1)S(1)}, u32[]{:S(2)}, u32[]{:S(2)}) collective-permute-start(bf16[4,80,128]{2,1,0:T(8,128)(2,1)S(1)} %constant_dynamic-update-slice_fusion.own), channel_id=1, source_target_pairs={{0,4},{1,129},{2,6},{3,131},{4,0},{5,133},{6,2},{7,135},{64,68},{6... | collective-permute-start | bytes 245768 | tf_op jit(solution)/shard_map/ppermute | solution.py:288
  17.8 7.9 %collective-permute-start.4 = (bf16[4,80,128]{2,1,0:T(8,128)(2,1)S(1)}, bf16[4,80,128]{2,1,0:T(8,128)(2,1)S(1)}, u32[]{:S(2)}, u32[]{:S(2)}) collective-permute-start(bf16[4,80,128]{2,1,0:T(8,128)(2,1)S(1)} %constant_dynamic-update-slice_fusion.own), channel_id=1, source_target_pairs={{0,2},{1,65},{2,0},{3,67},{4,6},{5,69},{6,4},{7,71},{64,66},{65,1}... | collective-permute-start | bytes 245768 | tf_op jit(solution)/shard_map/ppermute | solution.py:288
  23.0 3.7 %collective-permute-start = (bf16[8,80,128]{2,1,0:T(8,128)(2,1)S(1)}, bf16[8,80,128]{2,1,0:T(8,128)(2,1)S(1)}, u32[]{:S(2)}, u32[]{:S(2)}) collective-permute-start(bf16[8,80,128]{2,1,0:T(8,128)(2,1)S(1)} %all-to-all-done.own), channel_id=1, source_target_pairs={{0,1},{1,0},{2,3},{3,2},{4,5},{5,4},{6,7},{7,6},{8,9},{9,8},{10,11... | collective-permute-start | bytes 491528 | tf_op jit(solution)/shard_map/ppermute | solution.py:320

commit v8 on v5

--- a/solution.py
+++ b/solution.py
@@ -15,7 +15,7 @@
 PACK = 16
 BLOCKS = 2
 WIDTH = BLOCKS * LANES
-GROUPS = 64
+GROUPS = 128
 VMEM = 8 * 1024 * 1024
 UNIT = 1.0 / (EPS * math.log(2.0))
 AXES = ("x", "zh", "zl", "y", "c")

time: 147 us -> 148 us (level)
  no operation moved by 1% of the time
where the time goes in v8:
time: 148 us; the launch traced here: 147 us
  blocking collectives  101 us (68%)
  starting transfers between devices  18.8 us (13%)
  Pallas kernels  18.6 us (13%)
  waiting for transfers between devices  5.73 us (4%)
  between operations  2.57 us (2%)
    all_to_all x8, blocking collectives, exchange(): return lax.all_to_all(sent, group, 0, 0)  101 us
    pallas_call x10, Pallas kernels, call(): pl.pallas_call(kernel, out_shape=[jax.ShapeDtypeStruct(shape, dtype) for...  17.2 us
    ppermute x7, starting transfers between devices, neighbours(): lax.ppermute(array, axis, [(i, i ^ k) for i in range(size)])  10.5 us
    all_to_all x1, starting transfers between devices, exchange(): return lax.all_to_all(sent, group, 0, 0)  8.28 us
    all_to_all x1, waiting for transfers between devices, exchange(): return lax.all_to_all(sent, group, 0, 0)  4.74 us
  transfers between devices with their start and end apart: 8, of which 2 were waited for; matrix products, arithmetic and copies ran while one was open for 0% of the time, Pallas kernels for 0%

profile of v8, /device:TPU:1, one launch (start us, length us, event | category | flops | bytes accessed | tf_op | source)
XLA Modules:
  0.0 147.0 jit_solution(2683614069870632641)
XLA Ops:
  0.6 1.5 pack.1
  2.1 3.4 %collective-permute-start.3 = (bf16[1,80,128]{2,1,0:T(8,128)(2,1)S(1)}, bf16[1,80,128]{2,1,0:T(8,128)(2,1)S(1)}, u32[]{:S(2)}, u32[]{:S(2)}) collective-permute-start(bf16[1,80,128]{2,1,0:T(8,128)(2,1)S(1)} %get-tuple-element.32), channel_id=1, source_target_pairs={{0,192},{64,128},{128,64},{192,0},{1,193},{65,129},{129,65},{193,1... | collective-permute-start | bytes 61448 | tf_op jit(solution)/shard_map/ppermute | solution.py:306
  6.2 8.3 %all-to-all-start = ((bf16[8,80,128]{2,1,0:T(8,128)(2,1)}), bf16[8,80,128]{2,1,0:T(8,128)(2,1)S(1)}, u32[]{:S(2)}, u32[]{:S(2)}) async-start(bf16[8,80,128]{2,1,0:T(8,128)(2,1)} %get-tuple-element.30), calls=%async_computation | async-start | bytes 327680 | tf_op jit(solution)/shard_map/all_to_all | solution.py:275
  14.5 2.8 %collective-permute-start.6 = (bf16[4,80,128]{2,1,0:T(8,128)(2,1)S(1)}, bf16[4,80,128]{2,1,0:T(8,128)(2,1)S(1)}, u32[]{:S(2)}, u32[]{:S(2)}) collective-permute-start(bf16[4,80,128]{2,1,0:T(8,128)(2,1)S(1)} %constant_dynamic-update-slice_fusion.own), channel_id=1, source_target_pairs={{0,6},{2,4},{4,2},{6,0},{1,7},{3,5},{5,3},{7,1},{8,14},{10,12},{12... | collective-permute-start | bytes 245768 | tf_op jit(solution)/shard_map/ppermute | solution.py:306
  18.0 4.7 %all-to-all-done.own = bf16[8,80,128]{2,1,0:T(8,128)(2,1)S(1)} async-done(((bf16[8,80,128]{2,1,0:T(8,128)(2,1)}), bf16[8,80,128]{2,1,0:T(8,128)(2,1)S(1)}, u32[]{:S(2)}, u32[]{:S(2)}) %all-to-all-start) | async-done | bytes 163872 | tf_op jit(solution)/shard_map/all_to_all | solution.py:275
  22.8 2.9 %collective-permute-start = (bf16[8,80,128]{2,1,0:T(8,128)(2,1)S(1)}, bf16[8,80,128]{2,1,0:T(8,128)(2,1)S(1)}, u32[]{:S(2)}, u32[]{:S(2)}) collective-permute-start(bf16[8,80,128]{2,1,0:T(8,128)(2,1)S(1)} %all-to-all-done.own), channel_id=1, source_target_pairs={{0,1},{1,0},{2,3},{3,2},{4,5},{5,4},{6,7},{7,6},{8,9},{9,8},{10,11... | collective-permute-start | bytes 491528 | tf_op jit(solution)/shard_map/ppermute | solution.py:306
  25.7 1.0 collective-permute-done.other
  27.7 3.2 %row_pass_1.1 = f32[16,16,128]{2,1,0:T(8,128)S(1)} custom-call(bf16[2048,144]{1,0:T(8,128)(2,1)S(1)} %get-tuple-element.31.wide, bf16[64,2048]{1,0:T(8,128)(2,1)S(1)} %get-tuple-element.34.raw, f32[16,2048]{1,0:T(8,128)S(1)} %get-tuple-element.35.tail, f32[16,128]{1,0:T(8,128)S(1)} %get-tuple-element.36.scale), custom_call_target="tpu_custom_call" | custom-call | tf_op jit(solution)/shard_map/row_pass_1/pallas_call | solution.py:263
  30.9 13.2 %all_to_all.45.got = f32[16,16,128]{2,1,0:T(8,128)S(1)} all-to-all(f32[16,16,128]{2,1,0:T(8,128)S(1)} %row_pass_1.1), channel_id=1, replica_groups=mesh['x'=4,'zh'=4,'zl'=2,'y'=4,'c'=2] {'x','y'}, dimensions={0} | all-to-all | bytes 262144 | tf_op jit(solution)/shard_map/all_to_all | solution.py:275
  44.1 2.9 %col_pass_1.1 = (f32[16,128]{1,0:T(8,128)S(1)}, f32[16,128]{1,0:T(8,128)S(1)}, f32[16,128]{1,0:T(8,128)S(1)}, f32[2048,2048]{1,0:T(8,128)S(1)}, f32[16,16,128]{2,1,0:T(8,128)S(1)}) custom-call(f32[16,16,128]{2,1,0:T(8,128)S(1)} %all_to_all.45.got, bf16[2048,144]{1,0:T(8,128)(2,1)S(1)} %get-tuple-element.37.wide, bf16[64,2048]{1,0:T(8,128)(2,1)S(1)} %get-tuple-element.38.raw, ...), custom_call_target="tpu_custom_call" | custom-call | tf_op jit(solution)/shard_map/col_pass_1/pallas_call | solution.py:263
  47.0 15.2 %all_to_all.46.got = f32[16,16,128]{2,1,0:T(8,128)S(1)} all-to-all(f32[16,16,128]{2,1,0:T(8,128)S(1)} %get-tuple-element.40), channel_id=1, replica_groups=mesh['x'=4,'zh'=4,'zl'=2,'y'=4,'c'=2] {'zh','zl','c'}, dimensions={0} | all-to-all | bytes 262144 | tf_op jit(solution)/shard_map/all_to_all | solution.py:275
  62.2 2.9 %row_pass_2.1 = (f32[16,128]{1,0:T(8,128)S(1)}, f32[2048,2048]{1,0:T(8,128)S(1)}, f32[16,128]{1,0:T(8,128)S(1)}, f32[16,128]{1,0:T(8,128)S(1)}, f32[16,16,128]{2,1,0:T(8,128)S(1)}) custom-call(f32[16,16,128]{2,1,0:T(8,128)S(1)} %all_to_all.46.got, f32[16,128]{1,0:T(8,128)S(1)} %get-tuple-element.41.kept.f, f32[16,128]{1,0:T(8,128)S(1)} %get-tuple-element.42.lse, ...), custom_call_target="tpu_custom_call" | custom-call | tf_op jit(solution)/shard_map/row_pass_2/pallas_call | solution.py:263
  65.0 16.1 %all_to_all.47.got = f32[16,16,128]{2,1,0:T(8,128)S(1)} all-to-all(f32[16,16,128]{2,1,0:T(8,128)S(1)} %get-tuple-element.44), channel_id=1, replica_groups=mesh['x'=4,'zh'=4,'zl'=2,'y'=4,'c'=2] {'x','y'}, dimensions={0} | all-to-all | bytes 262144 | tf_op jit(solution)/shard_map/all_to_all | solution.py:275
  81.1 1.7 %product.2 = f32[16,16,128]{2,1,0:T(8,128)S(1)} custom-call(f32[16,16,128]{2,1,0:T(8,128)S(1)} %all_to_all.47.got, f32[2048,2048]{1,0:T(8,128)S(1)} %get-tuple-element.45.terms, f32[16,128]{1,0:T(8,128)S(1)} %get-tuple-element.46.weight), custom_call_target="tpu_custom_call" | custom-call | tf_op jit(solution)/shard_map/product/pallas_call | solution.py:263
  82.8 12.6 %all_to_all.48.got = f32[16,16,128]{2,1,0:T(8,128)S(1)} all-to-all(f32[16,16,128]{2,1,0:T(8,128)S(1)} %product.2), channel_id=1, replica_groups=mesh['x'=4,'zh'=4,'zl'=2,'y'=4,'c'=2] {'zh','zl','c'}, dimensions={0} | all-to-all | bytes 262144 | tf_op jit(solution)/shard_map/all_to_all | solution.py:275
  95.4 1.7 %product.3 = f32[16,16,128]{2,1,0:T(8,128)S(1)} custom-call(f32[16,16,128]{2,1,0:T(8,128)S(1)} %all_to_all.48.got, f32[2048,2048]{1,0:T(8,128)S(1)} %get-tuple-element.47.terms, f32[16,128]{1,0:T(8,128)S(1)} %get-tuple-element.48.weight), custom_call_target="tpu_custom_call" | custom-call | tf_op jit(solution)/shard_map/product/pallas_call | solution.py:263
  97.1 10.2 %all_to_all.49.got = f32[16,16,128]{2,1,0:T(8,128)S(1)} all-to-all(f32[16,16,128]{2,1,0:T(8,128)S(1)} %product.3), channel_id=1, replica_groups=mesh['x'=4,'zh'=4,'zl'=2,'y'=4,'c'=2] {'x','y'}, dimensions={0} | all-to-all | bytes 262144 | tf_op jit(solution)/shard_map/all_to_all | solution.py:275
  107.3 1.7 %last_product.2 = (f32[16,128]{1,0:T(8,128)S(1)}, f32[16,16,128]{2,1,0:T(8,128)S(1)}) custom-call(f32[16,16,128]{2,1,0:T(8,128)S(1)} %all_to_all.49.got, f32[2048,2048]{1,0:T(8,128)S(1)} %get-tuple-element.45.terms, f32[16,128]{1,0:T(8,128)S(1)} %get-tuple-element.46.weight), custom_call_target="tpu_custom_call" | custom-call | tf_op jit(solution)/shard_map/last_product/pallas_call | solution.py:263
  109.0 12.6 %all_to_all.50.got = f32[16,16,128]{2,1,0:T(8,128)S(1)} all-to-all(f32[16,16,128]{2,1,0:T(8,128)S(1)} %get-tuple-element.49), channel_id=1, replica_groups=mesh['x'=4,'zh'=4,'zl'=2,'y'=4,'c'=2] {'zh','zl','c'}, dimensions={0} | all-to-all | bytes 262144 | tf_op jit(solution)/shard_map/all_to_all | solution.py:275
  121.6 1.7 %last_product.3 = (f32[16,128]{1,0:T(8,128)S(1)}, f32[16,16,128]{2,1,0:T(8,128)S(1)}) custom-call(f32[16,16,128]{2,1,0:T(8,128)S(1)} %all_to_all.50.got, f32[2048,2048]{1,0:T(8,128)S(1)} %get-tuple-element.47.terms, f32[16,128]{1,0:T(8,128)S(1)} %get-tuple-element.48.weight), custom_call_target="tpu_custom_call" | custom-call | tf_op jit(solution)/shard_map/last_product/pallas_call | solution.py:263
  123.3 10.2 %all_to_all.51.got = f32[16,16,128]{2,1,0:T(8,128)S(1)} all-to-all(f32[16,16,128]{2,1,0:T(8,128)S(1)} %get-tuple-element.50), channel_id=1, replica_groups=mesh['x'=4,'zh'=4,'zl'=2,'y'=4,'c'=2] {'x','y'}, dimensions={0} | all-to-all | bytes 262144 | tf_op jit(solution)/shard_map/all_to_all | solution.py:275
  133.5 0.5 mismatch.1
  134.1 10.5 %all_to_all.52 = f32[16,1,128]{2,1,0:T(1,128)S(1)} all-to-all(f32[16,1,128]{2,1,0:T(1,128)S(1)} %get-tuple-element.56), channel_id=1, replica_groups=mesh['x'=4,'zh'=4,'zl'=2,'y'=4,'c'=2] {'zh','zl','c'}, dimensions={0} | all-to-all | bytes 16384 | tf_op jit(solution)/shard_map/all_to_all | solution.py:275
  144.5 0.6 slice_reduce_fusion
  (17 shorter events, 2.4 us)
Async XLA Ops:
  2.1 12.4 %collective-permute-start.3 = (bf16[1,80,128]{2,1,0:T(8,128)(2,1)S(1)}, bf16[1,80,128]{2,1,0:T(8,128)(2,1)S(1)}, u32[]{:S(2)}, u32[]{:S(2)}) collective-permute-start(bf16[1,80,128]{2,1,0:T(8,128)(2,1)S(1)} %get-tuple-element.32), channel_id=1, source_target_pairs={{0,192},{64,128},{128,64},{192,0},{1,193},{65,129},{129,65},{193,1... | collective-permute-start | bytes 61448 | tf_op jit(solution)/shard_map/ppermute | solution.py:306
  5.5 9.0 %collective-permute-start.2 = (bf16[1,80,128]{2,1,0:T(8,128)(2,1)S(1)}, bf16[1,80,128]{2,1,0:T(8,128)(2,1)S(1)}, u32[]{:S(2)}, u32[]{:S(2)}) collective-permute-start(bf16[1,80,128]{2,1,0:T(8,128)(2,1)S(1)} %get-tuple-element.32), channel_id=1, source_target_pairs={{0,128},{64,192},{128,0},{192,64},{1,129},{65,193},{129,1},{193,65... | collective-permute-start | bytes 61448 | tf_op jit(solution)/shard_map/ppermute | solution.py:306
  6.0 8.5 %collective-permute-start.1 = (bf16[1,80,128]{2,1,0:T(8,128)(2,1)S(1)}, bf16[1,80,128]{2,1,0:T(8,128)(2,1)S(1)}, u32[]{:S(2)}, u32[]{:S(2)}) collective-permute-start(bf16[1,80,128]{2,1,0:T(8,128)(2,1)S(1)} %get-tuple-element.32), channel_id=1, source_target_pairs={{0,64},{64,0},{128,192},{192,128},{1,65},{65,1},{129,193},{193,129... | collective-permute-start | bytes 61448 | tf_op jit(solution)/shard_map/ppermute | solution.py:306
  6.2 16.6 %all-to-all-start = ((bf16[8,80,128]{2,1,0:T(8,128)(2,1)}), bf16[8,80,128]{2,1,0:T(8,128)(2,1)S(1)}, u32[]{:S(2)}, u32[]{:S(2)}) async-start(bf16[8,80,128]{2,1,0:T(8,128)(2,1)} %get-tuple-element.30), calls=%async_computation | async-start | bytes 327680 | tf_op jit(solution)/shard_map/all_to_all | solution.py:275
  14.5 11.1 %collective-permute-start.6 = (bf16[4,80,128]{2,1,0:T(8,128)(2,1)S(1)}, bf16[4,80,128]{2,1,0:T(8,128)(2,1)S(1)}, u32[]{:S(2)}, u32[]{:S(2)}) collective-permute-start(bf16[4,80,128]{2,1,0:T(8,128)(2,1)S(1)} %constant_dynamic-update-slice_fusion.own), channel_id=1, source_target_pairs={{0,6},{2,4},{4,2},{6,0},{1,7},{3,5},{5,3},{7,1},{8,14},{10,12},{12... | collective-permute-start | bytes 245768 | tf_op jit(solution)/shard_map/ppermute | solution.py:306
  17.4 8.3 %collective-permute-start.5 = (bf16[4,80,128]{2,1,0:T(8,128)(2,1)S(1)}, bf16[4,80,128]{2,1,0:T(8,128)(2,1)S(1)}, u32[]{:S(2)}, u32[]{:S(2)}) collective-permute-start(bf16[4,80,128]{2,1,0:T(8,128)(2,1)S(1)} %constant_dynamic-update-slice_fusion.own), channel_id=1, source_target_pairs={{0,4},{2,6},{4,0},{6,2},{1,5},{3,7},{5,1},{7,3},{8,12},{10,14},{12... | collective-permute-start | bytes 245768 | tf_op jit(solution)/shard_map/ppermute | solution.py:306
  17.7 8.0 %collective-permute-start.4 = (bf16[4,80,128]{2,1,0:T(8,128)(2,1)S(1)}, bf16[4,80,128]{2,1,0:T(8,128)(2,1)S(1)}, u32[]{:S(2)}, u32[]{:S(2)}) collective-permute-start(bf16[4,80,128]{2,1,0:T(8,128)(2,1)S(1)} %constant_dynamic-update-slice_fusion.own), channel_id=1, source_target_pairs={{0,2},{2,0},{4,6},{6,4},{1,3},{3,1},{5,7},{7,5},{8,10},{10,8},{12,... | collective-permute-start | bytes 245768 | tf_op jit(solution)/shard_map/ppermute | solution.py:306
  22.8 3.9 %collective-permute-start = (bf16[8,80,128]{2,1,0:T(8,128)(2,1)S(1)}, bf16[8,80,128]{2,1,0:T(8,128)(2,1)S(1)}, u32[]{:S(2)}, u32[]{:S(2)}) collective-permute-start(bf16[8,80,128]{2,1,0:T(8,128)(2,1)S(1)} %all-to-all-done.own), channel_id=1, source_target_pairs={{0,1},{1,0},{2,3},{3,2},{4,5},{5,4},{6,7},{7,6},{8,9},{9,8},{10,11... | collective-permute-start | bytes 491528 | tf_op jit(solution)/shard_map/ppermute | solution.py:306
